TPU v7x, 512 devices: a whole 4x4x16 slice. The times are simulated.
512 devices in a mesh: lat: 16 (over z_lo, x), lon: 32 (over y, z_hi, core).
Axes of the slice: x: 4, y: 4, z: 16 (z_hi: 4, z_lo: 4; z = z_hi * 4 + z_lo), core: 2. Of those that a mesh axis runs over, the one named last changes fastest.
Arguments:
- tokens: bfloat16 [2, 384, 768, 512], P(None, 'lat', 'lon'), may hold values from -6 to 6
- attn_gain: float32 [512], replicated, may hold values from 0.1 to 1.9
- w_qkv: bfloat16 [512, 1536], P('lon'), may hold values from -1.5 to 1.5
- w_proj: bfloat16 [512, 512], P('lon'), may hold values from -0.25 to 0.25
- merge_gain: float32 [2048], replicated, may hold values from 0.1 to 1.9
- w_merge: bfloat16 [2048, 1024], P('lon'), may hold values from -0.125 to 0.125
Outputs:
- fine: bfloat16 [2, 384, 768, 512], P(None, 'lat', 'lon')
- coarse: bfloat16 [2, 192, 384, 1024], P(None, 'lat', 'lon')
All inputs are finite; a program needn't handle non-finite values.
Results may differ from a plain program's by a relative error of at most 0.011.
Values may be sent and summed in bfloat16 or wider, within the bound.
No kernel may reach another device: no remote copies, remote signals or barrier semaphores. Data moves between devices by JAX's collectives and lax.ppermute only.
A program may use at most 64 MiB of HBM per device.

v0:
```python
import jax
import jax.numpy as jnp
from jax import lax
from jax.sharding import PartitionSpec as P

HEADS = 8
WL = 6
WW = 12


eps = 1e-05


def from_behind(block, axis, distance):
    devices = range(lax.axis_size(axis))
    route = [((i - distance) % len(devices), i) for i in devices]
    return lax.ppermute(block, axis, route)


def layer_norm(values, gain):
    data = values.astype(jnp.float32)
    centred = data - jnp.mean(data, axis=-1, keepdims=True)
    spread = jnp.mean(centred * centred, axis=-1, keepdims=True)
    return centred * lax.rsqrt(spread + eps) * gain


def add_rows(flat, piece):
    return jnp.dot(flat, piece, preferred_element_type=jnp.float32)


def qkv_product(flat, w_qkv):
    return add_rows(flat, lax.all_gather(w_qkv, "lon", axis=0, tiled=True))


def proj_product(flat, w_proj):
    return add_rows(flat, lax.all_gather(w_proj, "lon", axis=0, tiled=True))


def merge_product(flat, w_merge):
    return add_rows(flat, lax.all_gather(w_merge, "lon", axis=0, tiled=True))


def shift_forward(normed):
    half_lat = WL // 2
    half_lon = WW // 2
    upper = from_behind(normed[:, :half_lat], "lat", -1)
    banded = jnp.concatenate([normed[:, half_lat:], upper], axis=1)
    right = from_behind(banded[:, :, :half_lon], "lon", -1)
    return jnp.concatenate([banded[:, :, half_lon:], right], axis=2)


def back_sums(values):
    half_lat = WL // 2
    half_lon = WW // 2
    lower = from_behind(values[:, -half_lat:].astype(jnp.bfloat16), "lat", 1).astype(jnp.float32)
    banded = jnp.concatenate([lower, values[:, :-half_lat]], axis=1)
    left = from_behind(banded[:, :, -half_lon:].astype(jnp.bfloat16), "lon", 1).astype(jnp.float32)
    return jnp.concatenate([left, banded[:, :, :-half_lon]], axis=2)


def window_attention(qkv, first_row, total_rows):
    levels, lat_rows, lon_cols, triple = qkv.shape
    width = triple // 3
    head = width // HEADS
    band_count = lat_rows // WL
    col_count = lon_cols // WW
    window = levels * WL * WW
    blocks = qkv.reshape(levels, band_count, WL, col_count, WW, 3, HEADS, head)
    blocks = blocks.transpose(5, 1, 3, 6, 0, 2, 4, 7).reshape(
        3, band_count, col_count, HEADS, window, head
    )
    scores = jnp.einsum(
        "abhqd,abhkd->abhqk", blocks[0], blocks[1], preferred_element_type=jnp.float32
    ) * head ** (-0.5)
    rows = first_row + jnp.arange(lat_rows, dtype=jnp.int32)
    region = (rows >= total_rows - WL // 2).astype(jnp.int32).reshape(band_count, 1, WL, 1)
    region = jnp.broadcast_to(region, (band_count, levels, WL, WW)).reshape(band_count, window)
    same = region[:, :, None] == region[:, None, :]
    scores = jnp.where(same[:, None, None], scores, -1e30)
    top = jnp.max(scores, axis=-1, keepdims=True)
    expo = jnp.exp(scores - top)
    probs = (expo / jnp.sum(expo, axis=-1, keepdims=True)).astype(jnp.bfloat16)
    attended = jnp.einsum(
        "abhqk,abhkd->abhqd", probs, blocks[2], preferred_element_type=jnp.float32
    ).astype(jnp.bfloat16)
    attended = attended.reshape(band_count, col_count, HEADS, levels, WL, WW, head)
    return attended.transpose(3, 0, 4, 1, 5, 2, 6).reshape(levels, lat_rows, lon_cols, width)


def merge_rows(fine):
    levels, rows, cols, width = fine.shape
    grouped = fine.reshape(levels, rows // 2, 2, cols // 2, 2, width).transpose(0, 1, 3, 4, 2, 5)
    return grouped.reshape(levels, rows // 2, cols // 2, 4 * width)


def on_device(tokens, attn_gain, w_qkv, w_proj, merge_gain, w_merge):
    levels, lat_rows, lon_cols, width = tokens.shape
    normed = layer_norm(tokens, attn_gain).astype(jnp.bfloat16)
    shifted = shift_forward(normed)
    qkv = qkv_product(shifted.reshape(-1, width), w_qkv).astype(jnp.bfloat16)
    qkv = qkv.reshape(levels, lat_rows, lon_cols, 3 * width)
    first_row = lax.axis_index("lat") * lat_rows
    total_rows = lat_rows * lax.axis_size("lat")
    attended = window_attention(qkv, first_row, total_rows)
    projected = proj_product(attended.reshape(-1, width), w_proj).reshape(tokens.shape)
    moved = back_sums(projected)
    fine = (tokens.astype(jnp.float32) + moved).astype(jnp.bfloat16)
    merged = layer_norm(merge_rows(fine), merge_gain).astype(jnp.bfloat16)
    coarse = merge_product(merged.reshape(-1, 4 * width), w_merge).astype(jnp.bfloat16)
    coarse = coarse.reshape(levels, lat_rows // 2, lon_cols // 2, 2 * width)
    return (fine, coarse)


def solution(mesh):
    in_specs = (
        P(None, "lat", "lon", None),
        P(),
        P("lon", None),
        P("lon", None),
        P(),
        P("lon", None),
    )
    out_specs = (P(None, "lat", "lon", None), P(None, "lat", "lon", None))
    return jax.shard_map(
        on_device, mesh=mesh, in_specs=in_specs, out_specs=out_specs, check_vma=False
    )
```

profile of v0, /device:TPU:32, one launch (start us, length us, event | category | flops | bytes accessed | tf_op | source)
XLA Modules:
  0.0 239.1 jit_solution(3577648043177261991)
XLA Ops:
  10.2 1.8 fusion.8
  12.5 4.2 %collective-permute-start = (bf16[2,3,24,512]{3,2,1,0:T(8,128)(2,1)S(1)}, bf16[2,3,24,512]{3,2,1,0:T(8,128)(2,1)S(1)}, u32[]{:S(2)}, u32[]{:S(2)}) collective-permute-start(bf16[2,3,24,512]{3,2,1,0:T(8,128)(2,1)S(1)} %slice.50), channel_id=1, source_target_pairs={{32,0},{64,32},{96,64},{128,96},{160,128},{192,160},{224,192},{256... | collective-permute-start | bytes 442376 | tf_op jit(solution)/shard_map/ppermute | solution.py:17
  17.0 66.6 %all_gather.10 = bf16[512,512]{1,0:T(8,128)(2,1)} all-gather(bf16[16,512]{1,0:T(8,128)(2,1)S(1)} %copy-done.2), channel_id=1, replica_groups=mesh['lat'=16,'lon'=32] {'lon'}, dimensions={0}, use_global_device_ids=true | all-gather | bytes 540672 | tf_op jit(solution)/shard_map/all_gather | solution.py:36
  83.6 4.2 %collective-permute-start.1 = (bf16[2,24,6,512]{3,2,1,0:T(8,128)(2,1)S(1)}, bf16[2,24,6,512]{3,2,1,0:T(8,128)(2,1)S(1)}, u32[]{:S(2)}, u32[]{:S(2)}) collective-permute-start(bf16[2,24,6,512]{3,2,1,0:T(8,128)(2,1)S(1)} %pad_maximum_fusion.2), channel_id=1, source_target_pairs={{1,0},{2,1},{3,2},{4,3},{5,4},{6,5},{7,6},{8,7},{9,8},{10,9},{11,1... | collective-permute-start | bytes 884744 | tf_op jit(solution)/shard_map/ppermute | solution.py:17
  88.3 13.1 %collective-permute-done.1 = bf16[2,24,6,512]{3,2,1,0:T(8,128)(2,1)S(1)} collective-permute-done((bf16[2,24,6,512]{3,2,1,0:T(8,128)(2,1)S(1)}, bf16[2,24,6,512]{3,2,1,0:T(8,128)(2,1)S(1)}, u32[]{:S(2)}, u32[]{:S(2)}) %collective-permute-start.1) | collective-permute-done | bytes 294944 | tf_op jit(solution)/shard_map/ppermute | solution.py:17
  101.7 5.2 %convolution_convert_fusion = bf16[1152,1536]{1,0:T(8,128)(2,1)} fusion(bf16[1152,512]{1,0:T(8,128)(2,1)S(1)} %bitcast.36, bf16[512,1536]{1,0:T(8,128)(2,1)} %all-gather.3.cloned.1.call-done), kind=kOutput, calls=%fused_computation.4 | convolution fusion | flops 1813708800 | bytes 6291456 | tf_op jit(solution)/shard_map/dot_general | solution.py:28
  106.9 9.6 %reshape_reshape.4 = bf16[2,4,6,2,12,3,8,64]{7,6,5,4,3,2,1,0:T(8,128)(2,1)} reshape(bf16[1152,1536]{1,0:T(8,128)(2,1)} %convolution_convert_fusion) | data formatting | bytes 7077888 | tf_op jit(solution)/shard_map/reshape;reshape | solution.py:68
  116.6 5.0 %copy.47 = bf16[2,4,6,2,12,3,8,64]{7,6,4,2,0,3,1,5:T(8,128)(2,1)S(1)} copy(bf16[2,4,6,2,12,3,8,64]{7,6,5,4,3,2,1,0:T(8,128)(2,1)} %reshape_reshape.4) | data formatting | bytes 7077888 | tf_op jit(solution)/shard_map/reshape;reshape | solution.py:68
  124.2 5.0 %fusion.32 = (f32[4,2,8,144]{3,2,1,0:T(8,128)S(1)}, f32[4,2,8,144,144]{3,4,2,1,0:T(8,128)}) fusion(f32[4,2,8,144,144]{3,4,2,1,0:T(8,128)S(1)} %fusion.14, pred[4,144,144]{1,2,0:T(8,128)(4,1)S(1)} %broadcast_compare_fusion), kind=kOutput, calls=%fused_computation.55 | output fusion | flops 7962767 | bytes 10736640 | tf_op jit(solution)/shard_map/sub | solution.py:81
  129.2 6.3 %fusion.17 = bf16[4,2,8,144,64]{3,4,2,1,0:T(8,128)(2,1)} fusion(f32[4,2,8,144,144]{3,4,2,1,0:T(8,128)} %get-tuple-element.12, f32[4,2,8,144]{3,2,1,0:T(8,128)S(1)} %get-tuple-element.11, bf16[4,2,8,144,64]{4,2,3,1,0:T(8,128)(2,1)S(1)} %bitcast.35), kind=kOutput, calls=%fused_computation.31 | convolution fusion | flops 173113344 | bytes 7704576 | tf_op jit(solution)/shard_map/abhqk,abhkd->abhqd/dot_general | solution.py:83
  135.6 3.2 %copy.27 = bf16[4,2,8,144,64]{4,2,3,1,0:T(8,128)(2,1)S(1)} copy(bf16[4,2,8,144,64]{3,4,2,1,0:T(8,128)(2,1)} %fusion.17) | data formatting | bytes 2359296 | tf_op jit(solution)/shard_map/convert_element_type | solution.py:85
  138.8 1.8 copy.28
  140.6 3.5 %dot_general.20 = bf16[2,24,24,512]{3,2,1,0:T(8,128)(2,1)S(1)} reshape(bf16[2,4,6,2,12,8,64]{6,5,4,3,2,1,0:T(8,128)(2,1)} %copy.28) | data formatting | bytes 2359296 | tf_op jit(solution)/shard_map/dot_general | solution.py:28
  144.9 1.9 collective-permute-start.2
  147.1 12.0 %collective-permute-done.2 = bf16[2,3,24,512]{3,2,1,0:T(8,128)(2,1)S(1)} collective-permute-done((bf16[2,3,24,512]{3,2,1,0:T(8,128)(2,1)S(1)}, bf16[2,3,24,512]{3,2,1,0:T(8,128)(2,1)S(1)}, u32[]{:S(2)}, u32[]{:S(2)}) %collective-permute-start.2) | collective-permute-done | bytes 147488 | tf_op jit(solution)/shard_map/ppermute | solution.py:17
  159.1 33.0 %collective-permute-start.3 = (bf16[2,24,6,512]{3,2,1,0:T(8,128)(2,1)S(1)}, bf16[2,24,6,512]{3,2,1,0:T(8,128)(2,1)S(1)}, u32[]{:S(2)}, u32[]{:S(2)}) collective-permute-start(bf16[2,24,6,512]{3,2,1,0:T(8,128)(2,1)S(1)} %fusion.24), channel_id=1, source_target_pairs={{31,0},{0,1},{1,2},{2,3},{3,4},{4,5},{5,6},{6,7},{7,8},{8,9},{9,10... | collective-permute-start | bytes 884744 | tf_op jit(solution)/shard_map/ppermute | solution.py:17
  192.2 16.9 %collective-permute-done.3 = bf16[2,24,6,512]{3,2,1,0:T(8,128)(2,1)S(1)} collective-permute-done((bf16[2,24,6,512]{3,2,1,0:T(8,128)(2,1)S(1)}, bf16[2,24,6,512]{3,2,1,0:T(8,128)(2,1)S(1)}, u32[]{:S(2)}, u32[]{:S(2)}) %collective-permute-start.3) | collective-permute-done | bytes 294944 | tf_op jit(solution)/shard_map/ppermute | solution.py:17
  209.2 1.6 fusion.11
  210.8 2.9 %reshape.93 = f32[2,12,2,12,2,512]{5,4,3,2,1,0:T(2,128)S(1)} reshape(bf16[2,24,24,512]{3,2,1,0:T(8,128)(2,1)} %fusion.11) | data formatting | bytes 3538944 | tf_op jit(solution)/shard_map/convert_element_type | solution.py:21
  213.7 3.2 %copy.48 = f32[2,12,2,12,2,512]{5,2,4,3,1,0:T(2,128)} copy(f32[2,12,2,12,2,512]{5,4,3,2,1,0:T(2,128)S(1)} %reshape.93) | data formatting | bytes 4718592 | tf_op jit(solution)/shard_map/convert_element_type | solution.py:21
  216.9 2.2 fusion.30
  219.2 2.4 %multiply_reduce_fusion = f32[2,12,12]{2,1,0:T(8,128)S(1)} fusion(f32[2,12,12]{2,1,0:T(8,128)S(1)} %broadcast_multiply_fusion.1, f32[2,12,2,12,2,512]{5,4,3,2,1,0:T(2,128)S(1)} %reshape.93), kind=kLoop, calls=%fused_computation.30 | loop fusion | flops 1769184 | bytes 2361600 | tf_op jit(solution)/shard_map/reduce_sum | solution.py:23
  221.7 3.3 %reshape.91 = f32[288,2048]{1,0:T(8,128)S(1)} reshape(f32[2,12,12,2,2,512]{5,4,3,2,1,0:T(2,128)} %bitcast.33) | data formatting | bytes 4718592 | tf_op jit(solution)/shard_map/convert_element_type | solution.py:21
  225.1 4.4 %convolution_convert_fusion.1 = bf16[288,1024]{1,0:T(8,128)(2,1)} fusion(bf16[2048,1024]{1,0:T(8,128)(2,1)} %all-gather.5.cloned.1.call-done, f32[288,2048]{1,0:T(8,128)S(1)} %reshape.91, f32[2048]{0:T(1024)S(1)} %copy-done.4, f32[288]{0:T(512)S(1)} %rsqrt.21, f32[288]{0:T(512)S(1)} %div.27), kind=kOutput, calls=%fused_computation.32 | convolution fusion | flops 1210613760 | bytes 7153920 | tf_op jit(solution)/shard_map/dot_general | solution.py:28
  (44 shorter events, 11.1 us)
Async XLA Ops:
  7.2 4.8 %copy-start = (bf16[2,24,24,512]{3,2,1,0:T(8,128)(2,1)S(1)}, bf16[2,24,24,512]{3,2,1,0:T(8,128)(2,1)}, u32[]{:S(2)}) copy-start(bf16[2,24,24,512]{3,2,1,0:T(8,128)(2,1)} %param.6) | copy-start | bytes 3538948
  7.2 4.8 %copy-start.3 = (f32[512]{0:T(512)S(1)}, f32[512]{0:T(512)}, u32[]{:S(2)}) copy-start(f32[512]{0:T(512)} %param.7) | copy-start | bytes 6148
  7.2 94.5 %all-gather.3.cloned.1.call-start = ((), (), s32[]{:S(2)}) async-start(), calls=%async_computation | async-start | bytes 1622016 | tf_op jit(solution)/shard_map/all_gather | solution.py:32
  7.9 217.2 %all-gather.5.cloned.1.call-start = ((), (), s32[]{:S(2)}) async-start(), calls=%async_computation.1 | async-start | bytes 4325376 | tf_op jit(solution)/shard_map/all_gather | solution.py:40
  12.0 5.0 %copy-start.2 = (bf16[16,512]{1,0:T(8,128)(2,1)S(1)}, bf16[16,512]{1,0:T(8,128)(2,1)}, u32[]{:S(2)}) copy-start(bf16[16,512]{1,0:T(8,128)(2,1)} %param.9) | copy-start | bytes 49156
  12.5 71.1 %collective-permute-start = (bf16[2,3,24,512]{3,2,1,0:T(8,128)(2,1)S(1)}, bf16[2,3,24,512]{3,2,1,0:T(8,128)(2,1)S(1)}, u32[]{:S(2)}, u32[]{:S(2)}) collective-permute-start(bf16[2,3,24,512]{3,2,1,0:T(8,128)(2,1)S(1)} %slice.50), channel_id=1, source_target_pairs={{32,0},{64,32},{96,64},{128,96},{160,128},{192,160},{224,192},{256... | collective-permute-start | bytes 442376 | tf_op jit(solution)/shard_map/ppermute | solution.py:17
  83.6 17.8 %collective-permute-start.1 = (bf16[2,24,6,512]{3,2,1,0:T(8,128)(2,1)S(1)}, bf16[2,24,6,512]{3,2,1,0:T(8,128)(2,1)S(1)}, u32[]{:S(2)}, u32[]{:S(2)}) collective-permute-start(bf16[2,24,6,512]{3,2,1,0:T(8,128)(2,1)S(1)} %pad_maximum_fusion.2), channel_id=1, source_target_pairs={{1,0},{2,1},{3,2},{4,3},{5,4},{6,5},{7,6},{8,7},{9,8},{10,9},{11,1... | collective-permute-start | bytes 884744 | tf_op jit(solution)/shard_map/ppermute | solution.py:17
  140.6 3.5 %copy-start.1 = (bf16[512,512]{1,0:T(8,128)(2,1)S(1)}, bf16[512,512]{1,0:T(8,128)(2,1)}, u32[]{:S(2)}) copy-start(bf16[512,512]{1,0:T(8,128)(2,1)} %all_gather.10) | copy-start | bytes 1572868
  144.9 14.1 %collective-permute-start.2 = (bf16[2,3,24,512]{3,2,1,0:T(8,128)(2,1)S(1)}, bf16[2,3,24,512]{3,2,1,0:T(8,128)(2,1)S(1)}, u32[]{:S(2)}, u32[]{:S(2)}) collective-permute-start(bf16[2,3,24,512]{3,2,1,0:T(8,128)(2,1)S(1)} %slice.71), channel_id=1, source_target_pairs={{480,0},{0,32},{32,64},{64,96},{96,128},{128,160},{160,192},{192,2... | collective-permute-start | bytes 442376 | tf_op jit(solution)/shard_map/ppermute | solution.py:17
  159.1 49.9 %collective-permute-start.3 = (bf16[2,24,6,512]{3,2,1,0:T(8,128)(2,1)S(1)}, bf16[2,24,6,512]{3,2,1,0:T(8,128)(2,1)S(1)}, u32[]{:S(2)}, u32[]{:S(2)}) collective-permute-start(bf16[2,24,6,512]{3,2,1,0:T(8,128)(2,1)S(1)} %fusion.24), channel_id=1, source_target_pairs={{31,0},{0,1},{1,2},{2,3},{3,4},{4,5},{5,6},{6,7},{7,8},{8,9},{9,10... | collective-permute-start | bytes 884744 | tf_op jit(solution)/shard_map/ppermute | solution.py:17
  221.7 3.4 %copy-start.4 = (f32[2048]{0:T(1024)S(1)}, f32[2048]{0:T(1024)}, u32[]{:S(2)}) copy-start(f32[2048]{0:T(1024)} %param.10) | copy-start | bytes 24580
Sparse Core Ops, SparseCore 0:
  11.1 80.0 all-gather.2
  94.4 110.0 all-gather.4
where the time goes:
time: 240 us; the launch traced here: 239 us
  blocking collectives  66.6 us (28%)
  starting transfers between devices  43.4 us (18%)
  waiting for transfers between devices  43.4 us (18%)
  local copies, waits for them, and re-layouts  37.1 us (15%)
  matrix products  18.2 us (8%)
  other arithmetic  15.9 us (7%)
  between operations  14.4 us (6%)
    all_gather x1, blocking collectives, proj_product(): return add_rows(flat, lax.all_gather(w_proj, 'lon', axis=0, tiled=True))  66.6 us
    ppermute x4, starting transfers between devices, from_behind(): return lax.ppermute(block, axis, route)  43.3 us
    ppermute x4, waiting for transfers between devices, from_behind(): return lax.ppermute(block, axis, route)  42 us
    another operation x2, local copies, waits for them, and re-layouts, window_attention(): blocks = qkv.reshape(levels, band_count, WL, col_count, WW, 3, HEADS, head)  14.7 us
    dot_general x3, matrix products, add_rows(): return jnp.dot(flat, piece, preferred_element_type=jnp.float32)  10.5 us
    convert_element_type x3, local copies, waits for them, and re-layouts, layer_norm(): data = values.astype(jnp.float32)  9.46 us
    dot_general x1, matrix products, window_attention(): jnp.einsum('abhqk,abhkd->abhqd', probs, blocks[2], preferred_element_type...  6.34 us
    sub x1, other arithmetic, window_attention(): expo = jnp.exp(scores - top)  5.01 us
  transfers between devices with their start and end apart: 6, of which 3 were waited for; matrix products, arithmetic and copies ran while one was open for 27% of the time, Pallas kernels for 0%

commit v1 on v0

v1 whole, which is shorter than its diff:
```python
import functools
import numpy as np
import jax
import jax.numpy as jnp
from jax import lax
from jax.sharding import Mesh, PartitionSpec as P
from jax.experimental import pallas as pl
from jax.experimental.pallas import tpu as pltpu

HEADS = 8
WL = 6
WW = 12
eps = 1e-05
f32 = jnp.float32
bf16 = jnp.bfloat16


def centre_order():
    order = []
    for first, last in ((0, 6), (6, 18), (18, 24)):
        for l in range(2):
            for r in range(6):
                order += [(l * 6 + r) * 24 + c for c in range(first, last)]
    return np.array(order)


def one_hot(order, n):
    return (order[:, None] == np.arange(n)[None, :]).astype(jnp.bfloat16)


def row_half():
    side = [r // 3 for l in range(2) for r in range(6) for c in range(6)]
    mid = [r // 3 for l in range(2) for r in range(6) for c in range(12)]
    return np.array(side + side + mid + side + side, np.float32)


def merge_order():
    return np.array([i * 24 + 2 * j + p for p in range(2) for i in range(12) for j in range(12)])


def dot(a, b, ca=1, cb=0):
    return lax.dot_general(a, b, (((ca,), (cb,)), ((), ())), preferred_element_type=f32)


def norm(x, gain):
    centred = x - jnp.mean(x, axis=-1, keepdims=True)
    spread = jnp.mean(centred * centred, axis=-1, keepdims=True)
    return centred * lax.rsqrt(spread + eps) * gain


def attend(q, k, v, bias, low):
    n = q.shape[0]
    out = []
    ones = jnp.ones((k.shape[0], 128), bf16)
    zero = jnp.zeros((), bf16)
    for pair in range(HEADS // 2):
        cols = slice(pair * 128, pair * 128 + 128)
        qp = q[:, cols]
        both = jnp.concatenate([jnp.where(low, qp, zero), jnp.where(low, zero, qp)], axis=0)
        s = dot(both, k[:, cols], 1, 1)
        s = s + jnp.concatenate([bias, bias], axis=0)
        e = jnp.exp(s - jnp.max(s, axis=-1, keepdims=True)).astype(bf16)
        o = dot(e, jnp.concatenate([v[:, cols], ones], axis=1))
        o = o[:, :128] / o[:, 128:]
        out.append(jnp.where(low, o[:n], o[n:]))
    return jnp.concatenate(out, axis=1)


def block_kernel(place_ref, mid_ref, left_ref, right_ref, gain_ref, own_ref, sibling_ref, perm_ref, back_ref, mask_ref,
                 fine_ref, weights, sems):
    band = pl.program_id(0)
    bands = pl.num_programs(0)

    @pl.when(band == 0)
    def _():
        core = place_ref[2]
        copies = [pltpu.make_async_copy(ref, weights.at[:, at], sems.at[n])
                  for n, (ref, at) in enumerate(((own_ref, core), (sibling_ref, 1 - core)))]
        for copy in copies:
            copy.start()
        for copy in copies:
            copy.wait()

    gain = gain_ref[...]
    raw = mid_ref[:, pl.ds(band * WL, WL)].reshape(288, 512)
    centre = norm(raw.astype(f32), gain).astype(bf16)
    centre = dot(perm_ref[...], centre)
    left = norm(left_ref[...].reshape(72, 512).astype(f32), gain)
    right = norm(right_ref[...].reshape(72, 512).astype(f32), gain)
    tokens = jnp.concatenate([left, centre, right], axis=0).astype(bf16)
    columns = [weights[:, :, :, n * 512:n * 512 + 512].reshape(512, 512) for n in range(4)]
    q = dot(centre.astype(bf16), columns[0]).astype(bf16) * jnp.asarray(0.125, bf16)
    k = dot(tokens, columns[1]).astype(bf16)
    v = dot(tokens, columns[2]).astype(bf16)
    low = lax.broadcasted_iota(jnp.int32, (1, 128), 1) < 64
    edge = ((place_ref[0] == 0) & (band == 0)) | ((place_ref[0] == place_ref[1]) & (band == bands - 1))
    scale = jnp.where(edge, 1.0, 0.0).astype(f32)
    mask = mask_ref[...] * scale
    spans = ((0, 72, 0), (72, 216, 144), (216, 288, 288))
    att = [attend(q[a:b], k[c:c + 144], v[c:c + 144], mask[a:b], low) for a, b, c in spans]
    att = jnp.concatenate(att, axis=0).astype(bf16)
    att = dot(back_ref[...], att).astype(bf16)
    out = dot(att, columns[3]) + raw.astype(f32)
    out = out.astype(bf16).reshape(2, WL, 24, 512)

    @pl.when(band > 0)
    def _():
        fine_ref[:, pl.ds(band * WL - 3, 3)] = out[:, :3]

    @pl.when(band < bands - 1)
    def _():
        fine_ref[:, pl.ds(band * WL, 3)] = out[:, 3:]


def norm_kernel(fine_ref, gain_ref, sel_ref, merged_ref):
    for l in range(2):
        parts = {}
        for p in range(2):
            rows = jnp.concatenate([fine_ref[l, 2 * i + p] for i in range(12)], axis=0)
            both = dot(sel_ref[...], rows)
            parts[p, 0] = both[:144]
            parts[p, 1] = both[144:]
        order = [parts[0, 0], parts[1, 0], parts[0, 1], parts[1, 1]]
        mean = sum(jnp.sum(a, axis=-1, keepdims=True) for a in order) * (1 / 2048)
        centred = [a - mean for a in order]
        spread = sum(jnp.sum(a * a, axis=-1, keepdims=True) for a in centred) * (1 / 2048)
        scale = lax.rsqrt(spread + eps)
        for n, a in enumerate(centred):
            cols = slice(n * 512, n * 512 + 512)
            merged_ref[l * 144:l * 144 + 144, cols] = (a * scale * gain_ref[:, cols]).astype(bf16)


def merge_kernel(merged_ref, w_ref, coarse_ref):
    coarse_ref[...] = dot(merged_ref[...], w_ref[...]).astype(bf16)


def whole(shape):
    return pl.BlockSpec(shape, lambda *_: (0,) * len(shape))


def attention_block(mid, left, right, gain, own, sibling, place):
    order = centre_order()
    perm = one_hot(order, 288)
    half = row_half()
    key_half = [half[0:144], half[144:288], half[288:432]]
    query_half = half[72:360]
    spans = ((0, 72), (72, 216), (216, 288))
    mask = np.concatenate([
        np.where(query_half[a:b, None] == key_half[n][None, :], 0.0, -1e30).astype(np.float32)
        for n, (a, b) in enumerate(spans)])
    bands = mid.shape[1] // WL
    return pl.pallas_call(
        block_kernel,
        grid=(bands,),
        in_specs=[
            pl.BlockSpec(memory_space=pltpu.SMEM),
            whole(mid.shape),
            pl.BlockSpec((1, 72, 512), lambda b: (b, 0, 0)),
            pl.BlockSpec((1, 72, 512), lambda b: (b, 0, 0)),
            whole((1, 512)),
            pl.BlockSpec(memory_space=pl.ANY),
            pl.BlockSpec(memory_space=pl.ANY),
            whole((288, 288)),
            whole((288, 288)),
            whole((288, 144)),
        ],
        out_specs=whole((2, 24, 24, 512)),
        out_shape=jax.ShapeDtypeStruct((2, 24, 24, 512), bf16),
        scratch_shapes=[pltpu.VMEM((own.shape[0], 2) + own.shape[1:], bf16), pltpu.SemaphoreType.DMA((2,))],
        compiler_params=pltpu.CompilerParams(vmem_limit_bytes=48 << 20),
        cost_estimate=pl.CostEstimate(flops=5_200_000_000, bytes_accessed=8 << 20, transcendentals=2_500_000),
        name="attention_block",
    )(place, mid, left, right, gain.reshape(1, 512), own, sibling, jnp.asarray(perm), jnp.asarray(perm.T), jnp.asarray(mask))


def merge_norm(fine, gain):
    sel = one_hot(merge_order(), 288)
    return pl.pallas_call(
        norm_kernel,
        out_shape=jax.ShapeDtypeStruct((288, 2048), bf16),
        compiler_params=pltpu.CompilerParams(vmem_limit_bytes=32 << 20),
        cost_estimate=pl.CostEstimate(flops=340_000_000, bytes_accessed=3 << 20, transcendentals=300),
        name="merge_norm",
    )(fine, gain.reshape(1, 2048), jnp.asarray(sel))


def merge_product(merged, w):
    return pl.pallas_call(
        merge_kernel,
        grid=(4,),
        in_specs=[whole((288, 2048)), pl.BlockSpec((2048, 256), lambda n: (0, n))],
        out_specs=pl.BlockSpec((288, 256), lambda n: (0, n)),
        out_shape=jax.ShapeDtypeStruct((288, 1024), bf16),
        compiler_params=pltpu.CompilerParams(vmem_limit_bytes=32 << 20),
        cost_estimate=pl.CostEstimate(flops=1_200_000_000, bytes_accessed=6 << 20, transcendentals=0),
        name="merge_product",
    )(merged, w)


LAT = ("zl", "x")
LON = ("y", "zh", "c")


def shift(block, axes, distance):
    devices = range(lax.axis_size(axes))
    route = [((i - distance) % len(devices), i) for i in devices]
    return lax.ppermute(block, axes, route)


def band_rows(piece):
    bands = piece.shape[1] // WL
    return piece.reshape(2, bands, WL, 6, 512).transpose(1, 0, 2, 3, 4).reshape(bands, 72, 512)


def on_device(tokens, attn_gain, w_qkv, w_proj, merge_gain, w_merge):
    above = shift(tokens[:, -3:], LAT, 1)
    below = shift(tokens[:, :3], LAT, -1)
    mid = jnp.concatenate([above, tokens, below], axis=1)
    left = shift(band_rows(mid[:, :, -6:]), LON, 1)
    right = shift(band_rows(mid[:, :, :6]), LON, -1)
    rows = w_qkv.shape[0]
    packed = jnp.concatenate([w_qkv, w_proj], axis=1)
    packed = lax.all_gather(packed, "zh")
    qkv_part = lax.all_gather(packed[:, :, :1536], "y")
    proj_part = lax.all_gather(packed[:, :, 1536:], "y")
    own = jnp.concatenate([qkv_part, proj_part], axis=-1).reshape(-1, rows, 2048)
    sibling = shift(own, "c", 1)
    place = jnp.stack([lax.axis_index(LAT), lax.axis_size(LAT) - 1, lax.axis_index("c")]).astype(jnp.int32)
    fine = attention_block(mid, left, right, attn_gain, own, sibling, place)
    merged = merge_norm(fine, merge_gain)
    coarse = merge_product(merged, lax.all_gather(w_merge, LON, axis=0, tiled=True))
    return fine, coarse.reshape(2, 12, 12, 1024)


def solution(mesh):
    lat, lon = mesh.shape["lat"], mesh.shape["lon"]
    fine_mesh = Mesh(mesh.devices.reshape(lat // 4, 4, 4, lon // 8, 2), LAT + LON)
    in_specs = (P(None, LAT, LON, None), P(), P(LON, None), P(LON, None), P(), P(LON, None))
    out_specs = (P(None, LAT, LON, None), P(None, LAT, LON, None))
    return jax.shard_map(
        on_device, mesh=fine_mesh, in_specs=in_specs, out_specs=out_specs, check_vma=False
    )
```

time: 240 us -> 167 us (0.70)
  the two profiles are of different devices: /device:TPU:32 before, /device:TPU:1 now
where the time goes in v1:
time: 167 us; the launch traced here: 166 us
  blocking collectives  47.7 us (29%)
  waiting for transfers between devices  42.8 us (26%)
  starting transfers between devices  27.4 us (16%)
  Pallas kernels  19.2 us (11%)
  between operations  14.2 us (9%)
  local copies, waits for them, and re-layouts  13.6 us (8%)
    ppermute x5, waiting for transfers between devices, shift(): return lax.ppermute(block, axes, route)  42.1 us
    ppermute x5, starting transfers between devices, shift(): return lax.ppermute(block, axes, route)  27.4 us
    all_gather x1, blocking collectives, on_device(): packed = lax.all_gather(packed, 'zh')  24.4 us
    pallas_call x1, Pallas kernels, attention_block(): pl.pallas_call(block_kernel, grid=(bands,), in_specs=[pl.BlockSpec(memory...  15.5 us
    all_gather x1, blocking collectives, on_device(): qkv_part = lax.all_gather(packed[:, :, :1536], 'y')  11.8 us
    all_gather x1, blocking collectives, on_device(): proj_part = lax.all_gather(packed[:, :, 1536:], 'y')  11.5 us
    unnamed x21, local copies, waits for them, and re-layouts  6.88 us
    reshape x4, local copies, waits for them, and re-layouts, band_rows(): piece.reshape(2, bands, WL, 6, 512).transpose(1, 0, 2, 3, 4)  4.68 us
  transfers between devices with their start and end apart: 6, of which 3 were waited for; matrix products, arithmetic and copies ran while one was open for 5% of the time, Pallas kernels for 10%

profile of v1, /device:TPU:1, one launch (start us, length us, event | category | flops | bytes accessed | tf_op | source)
XLA Modules:
  0.0 166.0 jit_solution(8046573079956699686)
XLA Ops:
  7.9 1.0 fusion.1
  8.9 3.9 %collective-permute-start = (bf16[2,3,24,512]{3,2,1,0:T(8,128)(2,1)S(1)}, bf16[2,3,24,512]{3,2,1,0:T(8,128)(2,1)S(1)}, u32[]{:S(2)}, u32[]{:S(2)}) collective-permute-start(bf16[2,3,24,512]{3,2,1,0:T(8,128)(2,1)S(1)} %get-tuple-element.11), channel_id=1, source_target_pairs={{480,0},{0,32},{32,64},{64,96},{96,128},{128,160},{160,192},{192,2... | collective-permute-start | bytes 442376 | tf_op jit(solution)/shard_map/ppermute | solution.py:207
  13.7 24.4 %all-gather = bf16[64,2048]{1,0:T(8,128)(2,1)S(1)} all-gather(bf16[16,2048]{1,0:T(8,128)(2,1)S(1)} %pad_maximum_fusion.1), channel_id=2, replica_groups=mesh['zl'=4,'x'=4,'y'=4,'zh'=4,'c'=2] {'zh'}, dimensions={0}, use_global_device_ids=true | all-gather | bytes 327680 | tf_op jit(solution)/shard_map/all_gather | solution.py:223
  38.1 11.5 %all-gather.2 = bf16[16,16,512]{2,1,0:T(8,128)(2,1)S(1)} all-gather(bf16[4,16,512]{2,1,0:T(8,128)(2,1)S(1)} %slice.27), channel_id=4, replica_groups=mesh['zl'=4,'x'=4,'y'=4,'zh'=4,'c'=2] {'y'}, dimensions={0}, use_global_device_ids=true | all-gather | bytes 327680 | tf_op jit(solution)/shard_map/all_gather | solution.py:225
  49.6 11.8 %all-gather.1 = bf16[16,16,1536]{2,1,0:T(8,128)(2,1)S(1)} all-gather(bf16[4,16,1536]{2,1,0:T(8,128)(2,1)S(1)} %slice.26), channel_id=3, replica_groups=mesh['zl'=4,'x'=4,'y'=4,'zh'=4,'c'=2] {'y'}, dimensions={0}, use_global_device_ids=true | all-gather | bytes 983040 | tf_op jit(solution)/shard_map/all_gather | solution.py:224
  61.5 9.1 %collective-permute-start.4 = (bf16[16,16,2048]{2,1,0:T(8,128)(2,1)S(1)}, bf16[16,16,2048]{2,1,0:T(8,128)(2,1)}, u32[]{:S(2)}, u32[]{:S(2)}) collective-permute-start(bf16[16,16,2048]{2,1,0:T(8,128)(2,1)S(1)} %bitcast.16), channel_id=1, source_target_pairs={{1,0},{0,1},{3,2},{2,3},{5,4},{4,5},{7,6},{6,7},{9,8},{8,9},{11,10... | collective-permute-start | bytes 3145736 | tf_op jit(solution)/shard_map/ppermute | solution.py:207
  70.6 7.2 %collective-permute-start.1 = (bf16[2,3,24,512]{3,2,1,0:T(8,128)(2,1)S(1)}, bf16[2,3,24,512]{3,2,1,0:T(8,128)(2,1)S(1)}, u32[]{:S(2)}, u32[]{:S(2)}) collective-permute-start(bf16[2,3,24,512]{3,2,1,0:T(8,128)(2,1)S(1)} %get-tuple-element.10), channel_id=1, source_target_pairs={{32,0},{64,32},{96,64},{128,96},{160,128},{192,160},{224,192},{256... | collective-permute-start | bytes 442376 | tf_op jit(solution)/shard_map/ppermute | solution.py:207
  78.0 31.2 %collective-permute-done.1 = bf16[2,3,24,512]{3,2,1,0:T(8,128)(2,1)S(1)} collective-permute-done((bf16[2,3,24,512]{3,2,1,0:T(8,128)(2,1)S(1)}, bf16[2,3,24,512]{3,2,1,0:T(8,128)(2,1)S(1)}, u32[]{:S(2)}, u32[]{:S(2)}) %collective-permute-start.1) | collective-permute-done | bytes 147488 | tf_op jit(solution)/shard_map/ppermute | solution.py:207
  109.2 0.9 fusion
  110.2 0.9 reshape.29
  111.1 5.2 %collective-permute-start.2 = (bf16[5,72,512]{2,1,0:T(8,128)(2,1)}, bf16[5,72,512]{2,1,0:T(8,128)(2,1)S(1)}, u32[]{:S(2)}, u32[]{:S(2)}) collective-permute-start(bf16[5,72,512]{2,1,0:T(8,128)(2,1)} %reshape.29), channel_id=1, source_target_pairs={{31,0},{0,1},{1,2},{2,3},{3,4},{4,5},{5,6},{6,7},{7,8},{8,9},{9,10... | collective-permute-start | bytes 1105928 | tf_op jit(solution)/shard_map/ppermute | solution.py:207
  116.3 1.9 %copy.23 = bf16[2,5,6,6,512]{4,3,2,0,1:T(8,128)(2,1)} copy(bf16[2,5,6,6,512]{4,3,2,1,0:T(8,128)(2,1)} %bitcast.23) | data formatting | bytes 737280 | tf_op jit(solution)/shard_map/reshape | solution.py:212
  118.1 1.9 %reshape.31 = bf16[5,72,512]{2,1,0:T(8,128)(2,1)} reshape(bf16[5,2,6,6,512]{4,3,2,1,0:T(8,128)(2,1)} %bitcast.22) | data formatting | bytes 737280 | tf_op jit(solution)/shard_map/reshape | solution.py:212
  120.0 1.9 %collective-permute-start.3 = (bf16[5,72,512]{2,1,0:T(8,128)(2,1)}, bf16[5,72,512]{2,1,0:T(8,128)(2,1)S(1)}, u32[]{:S(2)}, u32[]{:S(2)}) collective-permute-start(bf16[5,72,512]{2,1,0:T(8,128)(2,1)} %reshape.31), channel_id=1, source_target_pairs={{1,0},{2,1},{3,2},{4,3},{5,4},{6,5},{7,6},{8,7},{9,8},{10,9},{11,1... | collective-permute-start | bytes 1105928 | tf_op jit(solution)/shard_map/ppermute | solution.py:207
  122.0 3.3 %collective-permute-done.2.left_ref = bf16[5,72,512]{2,1,0:T(8,128)(2,1)S(1)} collective-permute-done((bf16[5,72,512]{2,1,0:T(8,128)(2,1)}, bf16[5,72,512]{2,1,0:T(8,128)(2,1)S(1)}, u32[]{:S(2)}, u32[]{:S(2)}) %collective-permute-start.2) | collective-permute-done | bytes 368672 | tf_op jit(solution)/shard_map/ppermute | solution.py:207
  125.3 7.7 %collective-permute-done.3.right_ref = bf16[5,72,512]{2,1,0:T(8,128)(2,1)S(1)} collective-permute-done((bf16[5,72,512]{2,1,0:T(8,128)(2,1)}, bf16[5,72,512]{2,1,0:T(8,128)(2,1)S(1)}, u32[]{:S(2)}, u32[]{:S(2)}) %collective-permute-start.3) | collective-permute-done | bytes 368672 | tf_op jit(solution)/shard_map/ppermute | solution.py:207
  133.0 1.0 copy-done.5
  133.9 0.9 copy-done.7
  134.9 15.5 %attention_block.1.fine_ref = bf16[2,24,24,512]{3,2,1,0:T(8,128)(2,1)} custom-call(s32[3]{0:T(128)S(1)} %pad_add_fusion.place_ref, bf16[2,30,24,512]{3,2,1,0:T(8,128)(2,1)S(1)} %constant_dynamic-update-slice_fusion.mid_ref, bf16[5,72,512]{2,1,0:T(8,128)(2,1)S(1)} %collective-permute-done.2.left_ref, ...), custom_call_target="tpu_custom_call" | custom-call | flops 5200000000 | bytes 8388608 | tf_op jit(solution)/shard_map/attention_block/pallas_call | solution.py:152
  150.4 1.3 copy-done.1
  151.6 1.2 merge_norm.1.merged_ref
  152.9 2.2 %copy-done = bf16[2048,1024]{1,0:T(8,128)(2,1)S(1)} copy-done((bf16[2048,1024]{1,0:T(8,128)(2,1)S(1)}, bf16[2048,1024]{1,0:T(8,128)(2,1)}, u32[]{:S(2)}) %copy-start) | copy-done | bytes 4194328
  155.0 2.6 %merge_product.1 = bf16[288,1024]{1,0:T(8,128)(2,1)S(1)} custom-call(bf16[288,2048]{1,0:T(8,128)(2,1)S(1)} %merge_norm.1.merged_ref, bf16[2048,1024]{1,0:T(8,128)(2,1)S(1)} %copy-done), custom_call_target="tpu_custom_call" | custom-call | flops 1200000000 | bytes 6291456 | tf_op jit(solution)/shard_map/merge_product/pallas_call | solution.py:188
  157.7 1.4 copy.20
  (29 shorter events, 2.1 us)
Async XLA Ops:
  7.2 145.7 %all-gather.5.cloned.1.call-start = ((), (), s32[]{:S(2)}) async-start(), calls=%async_computation | async-start | bytes 4325376 | tf_op jit(solution)/shard_map/all_gather | solution.py:231
  8.9 69.0 %collective-permute-start = (bf16[2,3,24,512]{3,2,1,0:T(8,128)(2,1)S(1)}, bf16[2,3,24,512]{3,2,1,0:T(8,128)(2,1)S(1)}, u32[]{:S(2)}, u32[]{:S(2)}) collective-permute-start(bf16[2,3,24,512]{3,2,1,0:T(8,128)(2,1)S(1)} %get-tuple-element.11), channel_id=1, source_target_pairs={{480,0},{0,32},{32,64},{64,96},{96,128},{128,160},{160,192},{192,2... | collective-permute-start | bytes 442376 | tf_op jit(solution)/shard_map/ppermute | solution.py:207
  49.6 28.3 %copy-start.8 = (bf16[2,24,24,512]{3,2,1,0:T(8,128)(2,1)S(1)}, bf16[2,24,24,512]{3,2,1,0:T(8,128)(2,1)}, u32[]{:S(2)}) copy-start(bf16[2,24,24,512]{3,2,1,0:T(8,128)(2,1)} %param.10) | copy-start | bytes 3538948
  61.5 71.5 %collective-permute-start.4 = (bf16[16,16,2048]{2,1,0:T(8,128)(2,1)S(1)}, bf16[16,16,2048]{2,1,0:T(8,128)(2,1)}, u32[]{:S(2)}, u32[]{:S(2)}) collective-permute-start(bf16[16,16,2048]{2,1,0:T(8,128)(2,1)S(1)} %bitcast.16), channel_id=1, source_target_pairs={{1,0},{0,1},{3,2},{2,3},{5,4},{4,5},{7,6},{6,7},{9,8},{8,9},{11,10... | collective-permute-start | bytes 3145736 | tf_op jit(solution)/shard_map/ppermute | solution.py:207
  70.6 38.6 %collective-permute-start.1 = (bf16[2,3,24,512]{3,2,1,0:T(8,128)(2,1)S(1)}, bf16[2,3,24,512]{3,2,1,0:T(8,128)(2,1)S(1)}, u32[]{:S(2)}, u32[]{:S(2)}) collective-permute-start(bf16[2,3,24,512]{3,2,1,0:T(8,128)(2,1)S(1)} %get-tuple-element.10), channel_id=1, source_target_pairs={{32,0},{64,32},{96,64},{128,96},{160,128},{192,160},{224,192},{256... | collective-permute-start | bytes 442376 | tf_op jit(solution)/shard_map/ppermute | solution.py:207
  110.2 22.8 %copy-start.4 = (f32[512]{0:T(512)S(1)}, f32[512]{0:T(512)}, u32[]{:S(2)}) copy-start(f32[512]{0:T(512)} %param.11) | copy-start | bytes 6148
  110.2 22.8 %copy-start.6 = (bf16[288,288]{1,0:T(8,128)(2,1)S(1)}, bf16[288,288]{1,0:T(8,128)(2,1)}, u32[]{:S(2)}) copy-start(bf16[288,288]{1,0:T(8,128)(2,1)} %constant.26.clone.perm_ref) | copy-start | bytes 497668
  111.1 14.2 %collective-permute-start.2 = (bf16[5,72,512]{2,1,0:T(8,128)(2,1)}, bf16[5,72,512]{2,1,0:T(8,128)(2,1)S(1)}, u32[]{:S(2)}, u32[]{:S(2)}) collective-permute-start(bf16[5,72,512]{2,1,0:T(8,128)(2,1)} %reshape.29), channel_id=1, source_target_pairs={{31,0},{0,1},{1,2},{2,3},{3,4},{4,5},{5,6},{6,7},{7,8},{8,9},{9,10... | collective-permute-start | bytes 1105928 | tf_op jit(solution)/shard_map/ppermute | solution.py:207
  120.0 12.9 %collective-permute-start.3 = (bf16[5,72,512]{2,1,0:T(8,128)(2,1)}, bf16[5,72,512]{2,1,0:T(8,128)(2,1)S(1)}, u32[]{:S(2)}, u32[]{:S(2)}) collective-permute-start(bf16[5,72,512]{2,1,0:T(8,128)(2,1)} %reshape.31), channel_id=1, source_target_pairs={{1,0},{2,1},{3,2},{4,3},{5,4},{6,5},{7,6},{8,7},{9,8},{10,9},{11,1... | collective-permute-start | bytes 1105928 | tf_op jit(solution)/shard_map/ppermute | solution.py:207
  133.0 1.0 copy-start.5
  133.9 0.9 copy-start.7
  134.9 15.5 %copy-start.2 = (bf16[288,288]{1,0:T(8,128)(2,1)S(1)}, bf16[288,288]{1,0:T(8,128)(2,1)}, u32[]{:S(2)}) copy-start(bf16[288,288]{1,0:T(8,128)(2,1)} %constant.29.clone.sel_ref) | copy-start | bytes 497668
  134.9 15.5 %copy-start.3 = (f32[2048]{0:T(1024)S(1)}, f32[2048]{0:T(1024)}, u32[]{:S(2)}) copy-start(f32[2048]{0:T(1024)} %param.14) | copy-start | bytes 24580
  150.4 1.3 copy-start.1
  152.9 2.2 %copy-start = (bf16[2048,1024]{1,0:T(8,128)(2,1)S(1)}, bf16[2048,1024]{1,0:T(8,128)(2,1)}, u32[]{:S(2)}) copy-start(bf16[2048,1024]{1,0:T(8,128)(2,1)} %all-gather.5.cloned.1.call-done.w_ref) | copy-start | bytes 12582916
Sparse Core Ops, SparseCore 0:
  11.1 117.4 all-gather.4

commit v2 on v1

--- a/solution.py
+++ b/solution.py
@@ -66,16 +66,51 @@
     return jnp.concatenate(out, axis=1)
 
 
-def block_kernel(place_ref, mid_ref, left_ref, right_ref, gain_ref, own_ref, sibling_ref, perm_ref, back_ref, mask_ref,
-                 fine_ref, weights, sems):
+def pack_kernel(place_ref, qkv_ref, proj_ref, merge_ref, out_ref):
+    for n in range(3):
+        out_ref[n] = qkv_ref[:, n * 512:n * 512 + 512]
+    out_ref[3] = proj_ref[...]
+    quarter = merge_ref[pl.ds(pl.multiple_of(place_ref[3] * 16, 16), 16), :]
+    out_ref[4] = quarter[:, :512]
+    out_ref[5] = quarter[:, 512:]
+
+
+def edge_kernel(place_ref, tokens_ref, above_ref, below_ref, sel_ref, outer_ref, inner_ref):
+    first = place_ref[2] == 0
+    for band in range(5):
+        parts = []
+        if band > 0:
+            parts.append(tokens_ref[:, band * WL - 3:band * WL])
+        else:
+            parts.append(above_ref[...])
+        if band < 4:
+            parts.append(tokens_ref[:, band * WL:band * WL + 3])
+        else:
+            parts.append(below_ref[...])
+        rows = jnp.concatenate(parts, axis=1).reshape(288, 512)
+        both = dot(sel_ref[...], rows)
+        left, right = both[:72], both[72:]
+        outer_ref[band] = jnp.where(first, left, right).astype(bf16)
+        inner_ref[band] = jnp.where(first, right, left).astype(bf16)
+
+
+def block_kernel(place_ref, tokens_ref, above_ref, below_ref, outer_ref, inner_ref, gain_ref, own_qkv_ref, own_rest_ref, sibling_qkv_ref,
+                 sibling_rest_ref, perm_ref, back_ref, mask_ref, fine_ref, mid_ref, weights, sems):
     band = pl.program_id(0)
     bands = pl.num_programs(0)
+    core = place_ref[2]
 
     @pl.when(band == 0)
     def _():
-        core = place_ref[2]
-        copies = [pltpu.make_async_copy(ref, weights.at[:, at], sems.at[n])
-                  for n, (ref, at) in enumerate(((own_ref, core), (sibling_ref, 1 - core)))]
+        copies = [
+            pltpu.make_async_copy(above_ref, mid_ref.at[:, 0:3], sems.at[8]),
+            pltpu.make_async_copy(tokens_ref, mid_ref.at[:, 3:27], sems.at[9]),
+            pltpu.make_async_copy(below_ref, mid_ref.at[:, 27:30], sems.at[10]),
+        ]
+        for m, (qkv, rest, at) in enumerate(((own_qkv_ref, own_rest_ref, core), (sibling_qkv_ref, sibling_rest_ref, 1 - core))):
+            for n in range(4):
+                source = qkv.at[:, n] if n < 3 else rest.at[:, 0]
+                copies.append(pltpu.make_async_copy(source, weights.at[n, :, at], sems.at[4 * m + n]))
         for copy in copies:
             copy.start()
         for copy in copies:
@@ -85,10 +120,12 @@
     raw = mid_ref[:, pl.ds(band * WL, WL)].reshape(288, 512)
     centre = norm(raw.astype(f32), gain).astype(bf16)
     centre = dot(perm_ref[...], centre)
-    left = norm(left_ref[...].reshape(72, 512).astype(f32), gain)
-    right = norm(right_ref[...].reshape(72, 512).astype(f32), gain)
+    outer = norm(outer_ref[...].reshape(72, 512).astype(f32), gain)
+    inner = norm(inner_ref[...].reshape(72, 512).astype(f32), gain)
+    left = jnp.where(core == 0, outer, inner)
+    right = jnp.where(core == 0, inner, outer)
     tokens = jnp.concatenate([left, centre, right], axis=0).astype(bf16)
-    columns = [weights[:, :, :, n * 512:n * 512 + 512].reshape(512, 512) for n in range(4)]
+    columns = [weights[n].reshape(512, 512) for n in range(4)]
     q = dot(centre.astype(bf16), columns[0]).astype(bf16) * jnp.asarray(0.125, bf16)
     k = dot(tokens, columns[1]).astype(bf16)
     v = dot(tokens, columns[2]).astype(bf16)
@@ -112,7 +149,20 @@
         fine_ref[:, pl.ds(band * WL, 3)] = out[:, 3:]
 
 
-def norm_kernel(fine_ref, gain_ref, sel_ref, merged_ref):
+def merge_kernel(place_ref, fine_ref, gain_ref, sel_ref, own_ref, sibling_ref, own_far_ref, sibling_far_ref, coarse_ref,
+                 weights, merged, sems):
+    core = place_ref[2]
+    x = place_ref[3]
+    copies = []
+    for col in range(2):
+        for at, near, far in ((core, own_ref, own_far_ref), (1 - core, sibling_ref, sibling_far_ref)):
+            side = 0 if near is own_ref else 1
+            copies.append(pltpu.make_async_copy(near.at[:, 1 + col], weights.at[col, :, at, x], sems.at[col, side, 0]))
+            for n, step in enumerate((3, 1, 2)):
+                there = lax.rem(x + step, 4)
+                copies.append(pltpu.make_async_copy(far.at[n, :, col], weights.at[col, :, at, there], sems.at[col, side, n + 1]))
+    for copy in copies:
+        copy.start()
     for l in range(2):
         parts = {}
         for p in range(2):
@@ -127,18 +177,19 @@
         scale = lax.rsqrt(spread + eps)
         for n, a in enumerate(centred):
             cols = slice(n * 512, n * 512 + 512)
-            merged_ref[l * 144:l * 144 + 144, cols] = (a * scale * gain_ref[:, cols]).astype(bf16)
-
-
-def merge_kernel(merged_ref, w_ref, coarse_ref):
-    coarse_ref[...] = dot(merged_ref[...], w_ref[...]).astype(bf16)
+            merged[l * 144:l * 144 + 144, cols] = (a * scale * gain_ref[:, cols]).astype(bf16)
+    for copy in copies:
+        copy.wait()
+    for col in range(2):
+        part = dot(merged[...], weights[col].reshape(2048, 512))
+        coarse_ref[:, col * 512:col * 512 + 512] = part.astype(bf16)
 
 
 def whole(shape):
     return pl.BlockSpec(shape, lambda *_: (0,) * len(shape))
 
 
-def attention_block(mid, left, right, gain, own, sibling, place):
+def attention_block(tokens, above, below, outer, inner, gain, own_qkv, own_rest, sibling_qkv, sibling_rest, place):
     order = centre_order()
     perm = one_hot(order, 288)
     half = row_half()
@@ -148,53 +199,84 @@
     mask = np.concatenate([
         np.where(query_half[a:b, None] == key_half[n][None, :], 0.0, -1e30).astype(np.float32)
         for n, (a, b) in enumerate(spans)])
-    bands = mid.shape[1] // WL
+    bands = 5
+    anywhere = pl.BlockSpec(memory_space=pl.ANY)
     return pl.pallas_call(
         block_kernel,
         grid=(bands,),
         in_specs=[
             pl.BlockSpec(memory_space=pltpu.SMEM),
-            whole(mid.shape),
+            anywhere,
+            anywhere,
+            anywhere,
             pl.BlockSpec((1, 72, 512), lambda b: (b, 0, 0)),
             pl.BlockSpec((1, 72, 512), lambda b: (b, 0, 0)),
             whole((1, 512)),
-            pl.BlockSpec(memory_space=pl.ANY),
-            pl.BlockSpec(memory_space=pl.ANY),
+            anywhere,
+            anywhere,
+            anywhere,
+            anywhere,
             whole((288, 288)),
             whole((288, 288)),
             whole((288, 144)),
         ],
         out_specs=whole((2, 24, 24, 512)),
         out_shape=jax.ShapeDtypeStruct((2, 24, 24, 512), bf16),
-        scratch_shapes=[pltpu.VMEM((own.shape[0], 2) + own.shape[1:], bf16), pltpu.SemaphoreType.DMA((2,))],
+        scratch_shapes=[
+            pltpu.VMEM((2, 30, 24, 512), bf16),
+            pltpu.VMEM((4, 16, 2, 16, 512), bf16),
+            pltpu.SemaphoreType.DMA((11,)),
+        ],
         compiler_params=pltpu.CompilerParams(vmem_limit_bytes=48 << 20),
         cost_estimate=pl.CostEstimate(flops=5_200_000_000, bytes_accessed=8 << 20, transcendentals=2_500_000),
         name="attention_block",
-    )(place, mid, left, right, gain.reshape(1, 512), own, sibling, jnp.asarray(perm), jnp.asarray(perm.T), jnp.asarray(mask))
-
-
-def merge_norm(fine, gain):
+    )(place, tokens, above, below, outer, inner, gain.reshape(1, 512), own_qkv, own_rest, sibling_qkv, sibling_rest, jnp.asarray(perm), jnp.asarray(perm.T), jnp.asarray(mask))
+
+
+def pack(w_qkv, w_proj, w_merge, place):
+    vmem = pl.BlockSpec(memory_space=pltpu.VMEM)
+    return pl.pallas_call(
+        pack_kernel,
+        in_specs=[pl.BlockSpec(memory_space=pltpu.SMEM), vmem, vmem, vmem],
+        out_specs=vmem,
+        out_shape=jax.ShapeDtypeStruct((6, 16, 512), bf16),
+        name="pack_weights",
+    )(place, w_qkv, w_proj, w_merge)
+
+
+def edges(tokens, above, below, place):
+    cols = list(range(6)), list(range(18, 24))
+    order = np.array([(l * 6 + r) * 24 + c for side in cols for l in range(2) for r in range(6) for c in side])
+    vmem = pl.BlockSpec(memory_space=pltpu.VMEM)
+    shape = jax.ShapeDtypeStruct((5, 72, 512), bf16)
+    return pl.pallas_call(
+        edge_kernel,
+        in_specs=[pl.BlockSpec(memory_space=pltpu.SMEM), vmem, vmem, vmem, vmem],
+        out_specs=(vmem, vmem),
+        out_shape=(shape, shape),
+        compiler_params=pltpu.CompilerParams(vmem_limit_bytes=32 << 20),
+        cost_estimate=pl.CostEstimate(flops=212_000_000, bytes_accessed=3 << 20, transcendentals=0),
+        name="edge_rows",
+    )(place, tokens, above, below, jnp.asarray(one_hot(order, 288)))
+
+
+def merge_block(fine, gain, own, sibling, own_far, sibling_far, place):
     sel = one_hot(merge_order(), 288)
-    return pl.pallas_call(
-        norm_kernel,
-        out_shape=jax.ShapeDtypeStruct((288, 2048), bf16),
-        compiler_params=pltpu.CompilerParams(vmem_limit_bytes=32 << 20),
-        cost_estimate=pl.CostEstimate(flops=340_000_000, bytes_accessed=3 << 20, transcendentals=300),
-        name="merge_norm",
-    )(fine, gain.reshape(1, 2048), jnp.asarray(sel))
-
-
-def merge_product(merged, w):
+    vmem = pl.BlockSpec(memory_space=pltpu.VMEM)
+    anywhere = pl.BlockSpec(memory_space=pl.ANY)
     return pl.pallas_call(
         merge_kernel,
-        grid=(4,),
-        in_specs=[whole((288, 2048)), pl.BlockSpec((2048, 256), lambda n: (0, n))],
-        out_specs=pl.BlockSpec((288, 256), lambda n: (0, n)),
+        in_specs=[pl.BlockSpec(memory_space=pltpu.SMEM), vmem, vmem, vmem] + [anywhere] * 4,
         out_shape=jax.ShapeDtypeStruct((288, 1024), bf16),
-        compiler_params=pltpu.CompilerParams(vmem_limit_bytes=32 << 20),
-        cost_estimate=pl.CostEstimate(flops=1_200_000_000, bytes_accessed=6 << 20, transcendentals=0),
-        name="merge_product",
-    )(merged, w)
+        scratch_shapes=[
+            pltpu.VMEM((2, own.shape[0], 2, 4) + own.shape[2:], bf16),
+            pltpu.VMEM((288, 2048), bf16),
+            pltpu.SemaphoreType.DMA((2, 2, 4)),
+        ],
+        compiler_params=pltpu.CompilerParams(vmem_limit_bytes=40 << 20),
+        cost_estimate=pl.CostEstimate(flops=1_540_000_000, bytes_accessed=8 << 20, transcendentals=300),
+        name="merge_block",
+    )(place, fine, gain.reshape(1, 2048), jnp.asarray(sel), own, sibling, own_far, sibling_far)
 
 
 LAT = ("zl", "x")
@@ -207,28 +289,34 @@
     return lax.ppermute(block, axes, route)
 
 
-def band_rows(piece):
-    bands = piece.shape[1] // WL
-    return piece.reshape(2, bands, WL, 6, 512).transpose(1, 0, 2, 3, 4).reshape(bands, 72, 512)
+def between_chips(block):
+    devices = range(lax.axis_size(LON))
+    return lax.ppermute(block, LON, [(i, (i + (1 if i % 2 else -1)) % len(devices)) for i in devices])
 
 
 def on_device(tokens, attn_gain, w_qkv, w_proj, merge_gain, w_merge):
+    place = jnp.stack([lax.axis_index(LAT), lax.axis_size(LAT) - 1, lax.axis_index("c"), lax.axis_index("x")]).astype(jnp.int32)
     above = shift(tokens[:, -3:], LAT, 1)
     below = shift(tokens[:, :3], LAT, -1)
-    mid = jnp.concatenate([above, tokens, below], axis=1)
-    left = shift(band_rows(mid[:, :, -6:]), LON, 1)
-    right = shift(band_rows(mid[:, :, :6]), LON, -1)
-    rows = w_qkv.shape[0]
-    packed = jnp.concatenate([w_qkv, w_proj], axis=1)
-    packed = lax.all_gather(packed, "zh")
-    qkv_part = lax.all_gather(packed[:, :, :1536], "y")
-    proj_part = lax.all_gather(packed[:, :, 1536:], "y")
-    own = jnp.concatenate([qkv_part, proj_part], axis=-1).reshape(-1, rows, 2048)
-    sibling = shift(own, "c", 1)
-    place = jnp.stack([lax.axis_index(LAT), lax.axis_size(LAT) - 1, lax.axis_index("c")]).astype(jnp.int32)
-    fine = attention_block(mid, left, right, attn_gain, own, sibling, place)
-    merged = merge_norm(fine, merge_gain)
-    coarse = merge_product(merged, lax.all_gather(w_merge, LON, axis=0, tiled=True))
+    packed = lax.all_gather(pack(w_qkv, w_proj, w_merge, place), "zh")
+    packed, above, below = lax.optimization_barrier((packed, above, below))
+    outer, inner = edges(tokens, above, below, place)
+    outer = between_chips(outer)
+    inner = shift(inner, "c", 1)
+    rest = lax.all_gather(packed[:, 3:], "y").reshape(16, 3, 16, 512)
+    rest, outer, inner = lax.optimization_barrier((rest, outer, inner))
+    sibling_rest = shift(rest, "c", 1)
+    merge_own = rest[:, 1:]
+    before = shift(merge_own, "x", 1)
+    after = shift(merge_own, "x", -1)
+    qkv = lax.all_gather(packed[:, :3], "y").reshape(16, 3, 16, 512)
+    before, after, sibling_rest, qkv = lax.optimization_barrier((before, after, sibling_rest, qkv))
+    sibling_qkv = shift(qkv, "c", 1)
+    across = [shift(before[:8], "x", 1), shift(after[8:], "x", -1)]
+    own_far = jnp.stack([before, after, jnp.concatenate(across, axis=0)])
+    sibling_far = shift(own_far, "c", 1)
+    fine = attention_block(tokens, above, below, outer, inner, attn_gain, qkv, rest, sibling_qkv, sibling_rest, place)
+    coarse = merge_block(fine, merge_gain, rest, sibling_rest, own_far, sibling_far, place)
     return fine, coarse.reshape(2, 12, 12, 1024)
 
 

time: 167 us -> 139 us (0.83)
  waiting for transfers between devices: 42.8 us -> 9.85 us
  starting transfers between devices: 27.4 us -> 46.5 us
  between operations: 14.2 us -> 0.94 us
  local copies, waits for them, and re-layouts: 13.6 us -> 5.65 us
  blocking collectives: 47.7 us -> 53.7 us
  Pallas kernels: 19.2 us -> 21.2 us
    ppermute x5 -> x10, waiting for transfers between devices: 42.1 us -> 9.85 us  [shift(): return lax.ppermute(block, axes, route)]
    ppermute x5 -> x10, starting transfers between devices: 27.4 us -> 41.7 us  [shift(): return lax.ppermute(block, axes, route)]
    all_gather x3, blocking collectives: 47.7 us -> 53.7 us  [the longest x1 29.8 us: on_device(): packed = lax.all_gather(pack(w_qkv, w_proj, w_merge, place), 'zh')]
    ppermute x0 -> x1, starting transfers between devices: none -> 4.79 us  [between_chips(): lax.ppermute(block, LON, [(i, (i + (1 if i % 2 else -1)) % len(devices))...]
    reshape x4 -> x0, local copies, waits for them, and re-layouts: 4.68 us -> none  [band_rows(): piece.reshape(2, bands, WL, 6, 512).transpose(1, 0, 2, 3, 4)]
    unnamed x21 -> x23, local copies, waits for them, and re-layouts: 6.88 us -> 4.31 us
    pallas_call x2 -> x3, Pallas kernels: 3.73 us -> 6.28 us  [the longest x1 3.59 us: merge_block(): pl.pallas_call(merge_kernel, in_specs=[pl.BlockSpec(memory_space=pltpu.SM...]
  transfers between devices with their start and end apart: 6 -> 11, of which waited for: 3 -> 3; matrix products, arithmetic and copies ran while one was open for 5% -> 1% of each run, Pallas kernels for 10% -> 12%
where the time goes in v2:
time: 139 us
  blocking collectives  53.7 us (39%)
  starting transfers between devices  46.5 us (33%)
  Pallas kernels  21.2 us (15%)
  waiting for transfers between devices  9.85 us (7%)
  local copies, waits for them, and re-layouts  5.65 us (4%)
    ppermute x10, starting transfers between devices, shift(): return lax.ppermute(block, axes, route)  41.7 us
    all_gather x1, blocking collectives, on_device(): packed = lax.all_gather(pack(w_qkv, w_proj, w_merge, place), 'zh')  29.8 us
    pallas_call x1, Pallas kernels, attention_block(): pl.pallas_call(block_kernel, grid=(bands,), in_specs=[pl.BlockSpec(memory...  14.9 us
    all_gather x1, blocking collectives, on_device(): rest = lax.all_gather(packed[:, 3:], 'y').reshape(16, 3, 16, 512)  12.9 us
    all_gather x1, blocking collectives, on_device(): qkv = lax.all_gather(packed[:, :3], 'y').reshape(16, 3, 16, 512)  11 us
    ppermute x10, waiting for transfers between devices, shift(): return lax.ppermute(block, axes, route)  9.85 us
    ppermute x1, starting transfers between devices, between_chips(): lax.ppermute(block, LON, [(i, (i + (1 if i % 2 else -1)) % len(devices))...  4.79 us
    unnamed x23, local copies, waits for them, and re-layouts  4.31 us
  transfers between devices with their start and end apart: 11, of which 3 were waited for; matrix products, arithmetic and copies ran while one was open for 1% of the time, Pallas kernels for 12%

profile of v2, /device:TPU:1, one launch (start us, length us, event | category | flops | bytes accessed | tf_op | source)
XLA Modules:
  0.0 138.7 jit_solution(9072984677964401383)
XLA Ops:
  0.6 1.1 fusion
  1.7 3.9 %collective-permute-start = (bf16[2,3,24,512]{3,2,1,0:T(8,128)(2,1)S(1)}, bf16[2,3,24,512]{3,2,1,0:T(8,128)(2,1)S(1)}, u32[]{:S(2)}, u32[]{:S(2)}) collective-permute-start(bf16[2,3,24,512]{3,2,1,0:T(8,128)(2,1)S(1)} %get-tuple-element.33), channel_id=1, source_target_pairs={{480,0},{0,32},{32,64},{64,96},{96,128},{128,160},{160,192},{192,2... | collective-permute-start | bytes 442376 | tf_op jit(solution)/shard_map/ppermute | solution.py:289
  5.7 7.2 %collective-permute-start.1 = (bf16[2,3,24,512]{3,2,1,0:T(8,128)(2,1)S(1)}, bf16[2,3,24,512]{3,2,1,0:T(8,128)(2,1)S(1)}, u32[]{:S(2)}, u32[]{:S(2)}) collective-permute-start(bf16[2,3,24,512]{3,2,1,0:T(8,128)(2,1)S(1)} %get-tuple-element.32), channel_id=1, source_target_pairs={{32,0},{64,32},{96,64},{128,96},{160,128},{192,160},{224,192},{256... | collective-permute-start | bytes 442376 | tf_op jit(solution)/shard_map/ppermute | solution.py:289
  13.6 1.6 %pack_weights.1 = bf16[6,16,512]{2,1,0:T(8,128)(2,1)} custom-call(s32[4]{0:T(128)} %pad_add_fusion.place_ref, bf16[16,1536]{1,0:T(8,128)(2,1)} %qkv_ref.1, bf16[16,512]{1,0:T(8,128)(2,1)} %proj_ref.1, bf16[64,1024]{1,0:T(8,128)(2,1)} %merge_ref.1), custom_call_target="tpu_custom_call" | custom-call | tf_op jit(solution)/shard_map/pack_weights/pallas_call | solution.py:238
  15.2 29.8 %all-gather = bf16[24,16,512]{2,1,0:T(8,128)(2,1)S(1)} all-gather(bf16[6,16,512]{2,1,0:T(8,128)(2,1)} %pack_weights.1), channel_id=2, replica_groups=mesh['zl'=4,'x'=4,'y'=4,'zh'=4,'c'=2] {'zh'}, dimensions={0}, use_global_device_ids=true | all-gather | bytes 491520 | tf_op jit(solution)/shard_map/all_gather | solution.py:301
  46.6 1.1 edge_rows.1
  47.7 4.8 %collective-permute-start.2 = (bf16[5,72,512]{2,1,0:T(8,128)(2,1)S(1)}, bf16[5,72,512]{2,1,0:T(8,128)(2,1)S(1)}, u32[]{:S(2)}, u32[]{:S(2)}) collective-permute-start(bf16[5,72,512]{2,1,0:T(8,128)(2,1)S(1)} %get-tuple-element.17), channel_id=1, source_target_pairs={{0,31},{1,2},{2,1},{3,4},{4,3},{5,6},{6,5},{7,8},{8,7},{9,10},{10,... | collective-permute-start | bytes 1105928 | tf_op jit(solution)/shard_map/ppermute | solution.py:294
  52.5 4.1 %collective-permute-start.3 = (bf16[5,72,512]{2,1,0:T(8,128)(2,1)S(1)}, bf16[5,72,512]{2,1,0:T(8,128)(2,1)S(1)}, u32[]{:S(2)}, u32[]{:S(2)}) collective-permute-start(bf16[5,72,512]{2,1,0:T(8,128)(2,1)S(1)} %get-tuple-element.18), channel_id=1, source_target_pairs={{1,0},{0,1},{3,2},{2,3},{5,4},{4,5},{7,6},{6,7},{9,8},{8,9},{11,10... | collective-permute-start | bytes 1105928 | tf_op jit(solution)/shard_map/ppermute | solution.py:289
  56.7 12.9 %all-gather.1.own_rest_ref.own_ref = bf16[16,3,16,512]{3,2,1,0:T(8,128)(2,1)S(1)} all-gather(bf16[4,3,16,512]{3,2,1,0:T(8,128)(2,1)S(1)} %get-tuple-element.35), channel_id=3, replica_groups=mesh['zl'=4,'x'=4,'y'=4,'zh'=4,'c'=2] {'y'}, dimensions={0}, use_global_device_ids=true | all-gather | bytes 983040 | tf_op jit(solution)/shard_map/all_gather | solution.py:306
  69.6 6.4 %collective-permute-start.6 = (bf16[16,3,16,512]{3,2,1,0:T(8,128)(2,1)S(1)}, bf16[16,3,16,512]{3,2,1,0:T(8,128)(2,1)S(1)}, u32[]{:S(2)}, u32[]{:S(2)}) collective-permute-start(bf16[16,3,16,512]{3,2,1,0:T(8,128)(2,1)S(1)} %all-gather.1.own_rest_ref.own_ref), channel_id=1, source_target_pairs={{1,0},{0,1},{3,2},{2,3},{5,4},{4,5},{7,6},{6,7},{9,8},{8,9},{11,10... | collective-permute-start | bytes 2359304 | tf_op jit(solution)/shard_map/ppermute | solution.py:289
  76.1 1.9 %collective-permute-start.4 = (bf16[16,2,16,512]{3,2,1,0:T(8,128)(2,1)S(1)}, bf16[16,2,16,512]{3,2,1,0:T(8,128)(2,1)S(1)}, u32[]{:S(2)}, u32[]{:S(2)}) collective-permute-start(bf16[16,2,16,512]{3,2,1,0:T(8,128)(2,1)S(1)} %slice.24), channel_id=1, source_target_pairs={{96,0},{0,32},{32,64},{64,96},{97,1},{1,33},{33,65},{65,97},{98,2}... | collective-permute-start | bytes 1572872 | tf_op jit(solution)/shard_map/ppermute | solution.py:289
  78.0 4.6 %collective-permute-start.5 = (bf16[16,2,16,512]{3,2,1,0:T(8,128)(2,1)S(1)}, bf16[16,2,16,512]{3,2,1,0:T(8,128)(2,1)S(1)}, u32[]{:S(2)}, u32[]{:S(2)}) collective-permute-start(bf16[16,2,16,512]{3,2,1,0:T(8,128)(2,1)S(1)} %slice.24), channel_id=1, source_target_pairs={{32,0},{64,32},{96,64},{0,96},{33,1},{65,33},{97,65},{1,97},{34,2}... | collective-permute-start | bytes 1572872 | tf_op jit(solution)/shard_map/ppermute | solution.py:289
  82.6 11.0 %all-gather.2.own_qkv_ref = bf16[16,3,16,512]{3,2,1,0:T(8,128)(2,1)S(1)} all-gather(bf16[4,3,16,512]{3,2,1,0:T(8,128)(2,1)S(1)} %get-tuple-element.34), channel_id=4, replica_groups=mesh['zl'=4,'x'=4,'y'=4,'zh'=4,'c'=2] {'y'}, dimensions={0}, use_global_device_ids=true | all-gather | bytes 983040 | tf_op jit(solution)/shard_map/all_gather | solution.py:312
  93.6 5.3 %collective-permute-start.9 = (bf16[8,2,16,512]{3,2,1,0:T(8,128)(2,1)S(1)}, bf16[8,2,16,512]{3,2,1,0:T(8,128)(2,1)S(1)}, u32[]{:S(2)}, u32[]{:S(2)}) collective-permute-start(bf16[8,2,16,512]{3,2,1,0:T(8,128)(2,1)S(1)} %slice.27), channel_id=1, source_target_pairs={{32,0},{64,32},{96,64},{0,96},{33,1},{65,33},{97,65},{1,97},{34,2}... | collective-permute-start | bytes 786440 | tf_op jit(solution)/shard_map/ppermute | solution.py:289
  99.0 1.9 %collective-permute-start.8 = (bf16[8,2,16,512]{3,2,1,0:T(8,128)(2,1)S(1)}, bf16[8,2,16,512]{3,2,1,0:T(8,128)(2,1)S(1)}, u32[]{:S(2)}, u32[]{:S(2)}) collective-permute-start(bf16[8,2,16,512]{3,2,1,0:T(8,128)(2,1)S(1)} %slice.26), channel_id=1, source_target_pairs={{96,0},{0,32},{32,64},{64,96},{97,1},{1,33},{33,65},{65,97},{98,2}... | collective-permute-start | bytes 786440 | tf_op jit(solution)/shard_map/ppermute | solution.py:289
  100.9 2.5 %collective-permute-done.9 = bf16[8,2,16,512]{3,2,1,0:T(8,128)(2,1)S(1)} collective-permute-done((bf16[8,2,16,512]{3,2,1,0:T(8,128)(2,1)S(1)}, bf16[8,2,16,512]{3,2,1,0:T(8,128)(2,1)S(1)}, u32[]{:S(2)}, u32[]{:S(2)}) %collective-permute-start.9) | collective-permute-done | bytes 262176 | tf_op jit(solution)/shard_map/ppermute | solution.py:289
  103.4 5.1 %collective-permute-done.8 = bf16[8,2,16,512]{3,2,1,0:T(8,128)(2,1)S(1)} collective-permute-done((bf16[8,2,16,512]{3,2,1,0:T(8,128)(2,1)S(1)}, bf16[8,2,16,512]{3,2,1,0:T(8,128)(2,1)S(1)}, u32[]{:S(2)}, u32[]{:S(2)}) %collective-permute-start.8) | collective-permute-done | bytes 262176 | tf_op jit(solution)/shard_map/ppermute | solution.py:289
  108.8 4.4 %collective-permute-start.10 = (bf16[3,16,2,16,512]{4,3,2,1,0:T(8,128)(2,1)S(1)}, bf16[3,16,2,16,512]{4,3,2,1,0:T(8,128)(2,1)S(1)}, u32[]{:S(2)}, u32[]{:S(2)}) collective-permute-start(bf16[3,16,2,16,512]{4,3,2,1,0:T(8,128)(2,1)S(1)} %pad_maximum_fusion.own_far_ref), channel_id=1, source_target_pairs={{1,0},{0,1},{3,2},{2,3},{5,4},{4,5},{7,6},{6,7},{9,8},{8,9},{11,10... | collective-permute-start | bytes 4718600 | tf_op jit(solution)/shard_map/ppermute | solution.py:289
  113.1 1.9 %collective-permute-start.7 = (bf16[16,3,16,512]{3,2,1,0:T(8,128)(2,1)S(1)}, bf16[16,3,16,512]{3,2,1,0:T(8,128)(2,1)S(1)}, u32[]{:S(2)}, u32[]{:S(2)}) collective-permute-start(bf16[16,3,16,512]{3,2,1,0:T(8,128)(2,1)S(1)} %all-gather.2.own_qkv_ref), channel_id=1, source_target_pairs={{1,0},{0,1},{3,2},{2,3},{5,4},{4,5},{7,6},{6,7},{9,8},{8,9},{11,10... | collective-permute-start | bytes 2359304 | tf_op jit(solution)/shard_map/ppermute | solution.py:289
  115.0 2.3 %collective-permute-done.7.sibling_qkv_ref = bf16[16,3,16,512]{3,2,1,0:T(8,128)(2,1)S(1)} collective-permute-done((bf16[16,3,16,512]{3,2,1,0:T(8,128)(2,1)S(1)}, bf16[16,3,16,512]{3,2,1,0:T(8,128)(2,1)S(1)}, u32[]{:S(2)}, u32[]{:S(2)}) %collective-permute-start.7) | collective-permute-done | bytes 786464 | tf_op jit(solution)/shard_map/ppermute | solution.py:289
  117.4 14.9 %attention_block.1.fine_ref = bf16[2,24,24,512]{3,2,1,0:T(8,128)(2,1)} custom-call(s32[4]{0:T(128)S(1)} %copy-done.6, bf16[2,24,24,512]{3,2,1,0:T(8,128)(2,1)S(1)} %copy-done, bf16[2,3,24,512]{3,2,1,0:T(8,128)(2,1)S(1)} %collective-permute-done.above_ref, bf16[2,3,24,512]{3,2,1,0:T(8,128)(2,1)S(1)} %collective-permute-done.1.below_ref, ...), custom_call_target="tpu_custom_call" | custom-call | flops 5200000000 | bytes 8388608 | tf_op jit(solution)/shard_map/attention_block/pallas_call | solution.py:204
  132.3 1.3 copy-done.1
  133.5 3.6 %merge_block.1 = bf16[288,1024]{1,0:T(8,128)(2,1)S(1)} custom-call(s32[4]{0:T(128)S(1)} %copy-done.6, bf16[2,24,24,512]{3,2,1,0:T(8,128)(2,1)S(1)} %copy-done.1, f32[1,2048]{1,0:T(1,128)S(1)} %bitcast.10, bf16[288,288]{1,0:T(8,128)(2,1)S(1)} %copy-done.2, bf16[16,3,16,512]{3,2,1,0:T(8,128)(2,1)S(1)} %all-gather.1.own_rest_ref.own_ref, ...), custom_call_target="tpu_custom_call" | custom-call | flops 1540000000 | bytes 8388608 | tf_op jit(solution)/shard_map/merge_block/pallas_call | solution.py:267
  137.3 1.4 %copy.15 = bf16[2,12,12,1024]{3,0,2,1:T(2,128)(2,1)} copy(bf16[2,12,12,1024]{3,2,1,0:T(8,128)(2,1)S(1)} %reshape.23) | data formatting | bytes 1179648
  (37 shorter events, 2.8 us)
Async XLA Ops:
  0.6 44.4 %copy-start = (bf16[2,24,24,512]{3,2,1,0:T(8,128)(2,1)S(1)}, bf16[2,24,24,512]{3,2,1,0:T(8,128)(2,1)}, u32[]{:S(2)}) copy-start(bf16[2,24,24,512]{3,2,1,0:T(8,128)(2,1)} %tokens_ref.3) | copy-start | bytes 3538948
  1.7 43.3 %collective-permute-start = (bf16[2,3,24,512]{3,2,1,0:T(8,128)(2,1)S(1)}, bf16[2,3,24,512]{3,2,1,0:T(8,128)(2,1)S(1)}, u32[]{:S(2)}, u32[]{:S(2)}) collective-permute-start(bf16[2,3,24,512]{3,2,1,0:T(8,128)(2,1)S(1)} %get-tuple-element.33), channel_id=1, source_target_pairs={{480,0},{0,32},{32,64},{64,96},{96,128},{128,160},{160,192},{192,2... | collective-permute-start | bytes 442376 | tf_op jit(solution)/shard_map/ppermute | solution.py:289
  5.7 39.4 %collective-permute-start.1 = (bf16[2,3,24,512]{3,2,1,0:T(8,128)(2,1)S(1)}, bf16[2,3,24,512]{3,2,1,0:T(8,128)(2,1)S(1)}, u32[]{:S(2)}, u32[]{:S(2)}) collective-permute-start(bf16[2,3,24,512]{3,2,1,0:T(8,128)(2,1)S(1)} %get-tuple-element.32), channel_id=1, source_target_pairs={{32,0},{64,32},{96,64},{128,96},{160,128},{192,160},{224,192},{256... | collective-permute-start | bytes 442376 | tf_op jit(solution)/shard_map/ppermute | solution.py:289
  45.1 0.9 copy-start.3
  46.0 0.7 copy-start.5
  47.7 21.9 %collective-permute-start.2 = (bf16[5,72,512]{2,1,0:T(8,128)(2,1)S(1)}, bf16[5,72,512]{2,1,0:T(8,128)(2,1)S(1)}, u32[]{:S(2)}, u32[]{:S(2)}) collective-permute-start(bf16[5,72,512]{2,1,0:T(8,128)(2,1)S(1)} %get-tuple-element.17), channel_id=1, source_target_pairs={{0,31},{1,2},{2,1},{3,4},{4,3},{5,6},{6,5},{7,8},{8,7},{9,10},{10,... | collective-permute-start | bytes 1105928 | tf_op jit(solution)/shard_map/ppermute | solution.py:294
  52.5 17.1 %collective-permute-start.3 = (bf16[5,72,512]{2,1,0:T(8,128)(2,1)S(1)}, bf16[5,72,512]{2,1,0:T(8,128)(2,1)S(1)}, u32[]{:S(2)}, u32[]{:S(2)}) collective-permute-start(bf16[5,72,512]{2,1,0:T(8,128)(2,1)S(1)} %get-tuple-element.18), channel_id=1, source_target_pairs={{1,0},{0,1},{3,2},{2,3},{5,4},{4,5},{7,6},{6,7},{9,8},{8,9},{11,10... | collective-permute-start | bytes 1105928 | tf_op jit(solution)/shard_map/ppermute | solution.py:289
  69.6 24.0 %collective-permute-start.6 = (bf16[16,3,16,512]{3,2,1,0:T(8,128)(2,1)S(1)}, bf16[16,3,16,512]{3,2,1,0:T(8,128)(2,1)S(1)}, u32[]{:S(2)}, u32[]{:S(2)}) collective-permute-start(bf16[16,3,16,512]{3,2,1,0:T(8,128)(2,1)S(1)} %all-gather.1.own_rest_ref.own_ref), channel_id=1, source_target_pairs={{1,0},{0,1},{3,2},{2,3},{5,4},{4,5},{7,6},{6,7},{9,8},{8,9},{11,10... | collective-permute-start | bytes 2359304 | tf_op jit(solution)/shard_map/ppermute | solution.py:289
  76.1 17.5 %collective-permute-start.4 = (bf16[16,2,16,512]{3,2,1,0:T(8,128)(2,1)S(1)}, bf16[16,2,16,512]{3,2,1,0:T(8,128)(2,1)S(1)}, u32[]{:S(2)}, u32[]{:S(2)}) collective-permute-start(bf16[16,2,16,512]{3,2,1,0:T(8,128)(2,1)S(1)} %slice.24), channel_id=1, source_target_pairs={{96,0},{0,32},{32,64},{64,96},{97,1},{1,33},{33,65},{65,97},{98,2}... | collective-permute-start | bytes 1572872 | tf_op jit(solution)/shard_map/ppermute | solution.py:289
  78.0 15.6 %collective-permute-start.5 = (bf16[16,2,16,512]{3,2,1,0:T(8,128)(2,1)S(1)}, bf16[16,2,16,512]{3,2,1,0:T(8,128)(2,1)S(1)}, u32[]{:S(2)}, u32[]{:S(2)}) collective-permute-start(bf16[16,2,16,512]{3,2,1,0:T(8,128)(2,1)S(1)} %slice.24), channel_id=1, source_target_pairs={{32,0},{64,32},{96,64},{0,96},{33,1},{65,33},{97,65},{1,97},{34,2}... | collective-permute-start | bytes 1572872 | tf_op jit(solution)/shard_map/ppermute | solution.py:289
  93.6 9.8 %collective-permute-start.9 = (bf16[8,2,16,512]{3,2,1,0:T(8,128)(2,1)S(1)}, bf16[8,2,16,512]{3,2,1,0:T(8,128)(2,1)S(1)}, u32[]{:S(2)}, u32[]{:S(2)}) collective-permute-start(bf16[8,2,16,512]{3,2,1,0:T(8,128)(2,1)S(1)} %slice.27), channel_id=1, source_target_pairs={{32,0},{64,32},{96,64},{0,96},{33,1},{65,33},{97,65},{1,97},{34,2}... | collective-permute-start | bytes 786440 | tf_op jit(solution)/shard_map/ppermute | solution.py:289
  99.0 9.5 %collective-permute-start.8 = (bf16[8,2,16,512]{3,2,1,0:T(8,128)(2,1)S(1)}, bf16[8,2,16,512]{3,2,1,0:T(8,128)(2,1)S(1)}, u32[]{:S(2)}, u32[]{:S(2)}) collective-permute-start(bf16[8,2,16,512]{3,2,1,0:T(8,128)(2,1)S(1)} %slice.26), channel_id=1, source_target_pairs={{96,0},{0,32},{32,64},{64,96},{97,1},{1,33},{33,65},{65,97},{98,2}... | collective-permute-start | bytes 786440 | tf_op jit(solution)/shard_map/ppermute | solution.py:289
  108.5 8.8 %copy-start.6 = (s32[4]{0:T(128)S(1)}, s32[4]{0:T(128)}, u32[]{:S(2)}) copy-start(s32[4]{0:T(128)} %pad_add_fusion.place_ref) | copy-start | bytes 52
  108.5 8.8 %copy-start.7 = (f32[512]{0:T(512)S(1)}, f32[512]{0:T(512)}, u32[]{:S(2)}) copy-start(f32[512]{0:T(512)} %param.12) | copy-start | bytes 6148
  108.5 8.8 %copy-start.8 = (f32[288,144]{1,0:T(8,128)S(1)}, f32[288,144]{1,0:T(8,128)}, u32[]{:S(2)}) copy-start(f32[288,144]{1,0:T(8,128)} %constant.31.clone.mask_ref) | copy-start | bytes 497668
  108.6 8.8 %copy-start.9 = (bf16[288,288]{1,0:T(8,128)(2,1)S(1)}, bf16[288,288]{1,0:T(8,128)(2,1)}, u32[]{:S(2)}) copy-start(bf16[288,288]{1,0:T(8,128)(2,1)} %constant.29.clone.perm_ref) | copy-start | bytes 497668
  108.6 8.8 %copy-start.10 = (bf16[288,288]{1,0:T(8,128)(2,1)S(1)}, bf16[288,288]{1,0:T(8,128)(2,1)}, u32[]{:S(2)}) copy-start(bf16[288,288]{1,0:T(8,128)(2,1)} %constant.30.clone.back_ref) | copy-start | bytes 497668
  108.8 23.5 %collective-permute-start.10 = (bf16[3,16,2,16,512]{4,3,2,1,0:T(8,128)(2,1)S(1)}, bf16[3,16,2,16,512]{4,3,2,1,0:T(8,128)(2,1)S(1)}, u32[]{:S(2)}, u32[]{:S(2)}) collective-permute-start(bf16[3,16,2,16,512]{4,3,2,1,0:T(8,128)(2,1)S(1)} %pad_maximum_fusion.own_far_ref), channel_id=1, source_target_pairs={{1,0},{0,1},{3,2},{2,3},{5,4},{4,5},{7,6},{6,7},{9,8},{8,9},{11,10... | collective-permute-start | bytes 4718600 | tf_op jit(solution)/shard_map/ppermute | solution.py:289
  113.1 4.2 %collective-permute-start.7 = (bf16[16,3,16,512]{3,2,1,0:T(8,128)(2,1)S(1)}, bf16[16,3,16,512]{3,2,1,0:T(8,128)(2,1)S(1)}, u32[]{:S(2)}, u32[]{:S(2)}) collective-permute-start(bf16[16,3,16,512]{3,2,1,0:T(8,128)(2,1)S(1)} %all-gather.2.own_qkv_ref), channel_id=1, source_target_pairs={{1,0},{0,1},{3,2},{2,3},{5,4},{4,5},{7,6},{6,7},{9,8},{8,9},{11,10... | collective-permute-start | bytes 2359304 | tf_op jit(solution)/shard_map/ppermute | solution.py:289
  117.3 14.9 %copy-start.2 = (bf16[288,288]{1,0:T(8,128)(2,1)S(1)}, bf16[288,288]{1,0:T(8,128)(2,1)}, u32[]{:S(2)}) copy-start(bf16[288,288]{1,0:T(8,128)(2,1)} %constant.32.clone.sel_ref) | copy-start | bytes 497668
  117.3 14.9 %copy-start.4 = (f32[2048]{0:T(1024)S(1)}, f32[2048]{0:T(1024)}, u32[]{:S(2)}) copy-start(f32[2048]{0:T(1024)} %param.15) | copy-start | bytes 24580
  132.3 1.3 copy-start.1

commit v3 on v2

v3 whole, which is shorter than its diff:
```python
import numpy as np
import jax
import jax.numpy as jnp
from jax import lax
from jax.sharding import Mesh, PartitionSpec as P
from jax.experimental import pallas as pl
from jax.experimental.pallas import tpu as pltpu

HEADS = 8
WL = 6
eps = 1e-05
f32 = jnp.float32
bf16 = jnp.bfloat16
LAT = ("zl", "x")
LON = ("y", "zh", "c")
VMEM = pl.BlockSpec(memory_space=pltpu.VMEM)
ANY = pl.BlockSpec(memory_space=pl.ANY)


def centre_order():
    order = []
    for first, last in ((0, 6), (6, 18), (18, 24)):
        for l in range(2):
            for r in range(6):
                order += [(l * 6 + r) * 24 + c for c in range(first, last)]
    return np.array(order)


def one_hot(order, n):
    return (order[:, None] == np.arange(n)[None, :]).astype(jnp.bfloat16)


def row_half():
    side = [r // 3 for l in range(2) for r in range(6) for c in range(6)]
    mid = [r // 3 for l in range(2) for r in range(6) for c in range(12)]
    return np.array(side + side + mid + side + side, np.float32)


def edge_mask():
    half = row_half()
    spans = ((0, 72), (72, 216), (216, 288))
    return np.concatenate([
        np.where(half[72 + a:72 + b, None] == half[None, n * 144:n * 144 + 144], 0.0, -1e30).astype(np.float32)
        for n, (a, b) in enumerate(spans)])


def merge_order():
    return np.array([i * 24 + 2 * j + p for p in range(2) for i in range(12) for j in range(12)])


def dot(a, b, ca=1, cb=0):
    return lax.dot_general(a, b, (((ca,), (cb,)), ((), ())), preferred_element_type=f32)


def norm(x, gain):
    centred = x - jnp.mean(x, axis=-1, keepdims=True)
    spread = jnp.mean(centred * centred, axis=-1, keepdims=True)
    return centred * lax.rsqrt(spread + eps) * gain


def x_slots(x):
    pair = x + 1 - 2 * lax.rem(x, 2)
    return ((x, pair), (3 - x, 3 - pair))


def pack_kernel(qkv_ref, proj_ref, merge_ref, out_ref):
    for n in range(3):
        out_ref[n] = qkv_ref[:, n * 512:n * 512 + 512]
    out_ref[3] = proj_ref[...]
    quarter = merge_ref[pl.ds(pl.multiple_of(lax.axis_index("x") * 16, 16), 16), :]
    out_ref[4] = quarter[:, :512]
    out_ref[5] = quarter[:, 512:]


def edge_kernel(tokens_ref, above_ref, below_ref, outer_ref, inner_ref):
    first = lax.axis_index("c") == 0
    o = lax.broadcasted_iota(jnp.int32, (144, 288), 0)
    side = (o * 911) >> 16
    lr = ((o - side * 72) * 10923) >> 16
    col = o - side * 72 - lr * 6 + side * 18
    sel = jnp.where(lax.broadcasted_iota(jnp.int32, (144, 288), 1) == lr * 24 + col, 1.0, 0.0).astype(bf16)
    for band in range(5):
        upper = tokens_ref[:, band * WL - 3:band * WL] if band > 0 else above_ref[...]
        lower = tokens_ref[:, band * WL:band * WL + 3] if band < 4 else below_ref[...]
        rows = jnp.concatenate([upper, lower], axis=1).reshape(288, 512)
        both = dot(sel, rows)
        left, right = both[:72], both[72:]
        outer_ref[band] = jnp.where(first, left, right).astype(bf16)
        inner = jnp.concatenate([jnp.where(first, right, left), jnp.zeros((8, 512), f32)], axis=0)
        inner_ref[band * 5:band * 5 + 5] = inner.astype(bf16).reshape(5, 16, 512)
    inner_ref[25:] = jnp.zeros((7, 16, 512), bf16)


def attend(q, k, v, bias, low):
    n = q.shape[0]
    out = []
    ones = jnp.ones((k.shape[0], 128), bf16)
    zero = jnp.zeros((), bf16)
    for pair in range(HEADS // 2):
        cols = slice(pair * 128, pair * 128 + 128)
        qp = q[:, cols]
        both = jnp.concatenate([jnp.where(low, qp, zero), jnp.where(low, zero, qp)], axis=0)
        s = dot(both, k[:, cols], 1, 1)
        s = s + jnp.concatenate([bias, bias], axis=0)
        e = jnp.exp(s - jnp.max(s, axis=-1, keepdims=True)).astype(bf16)
        o = dot(e, jnp.concatenate([v[:, cols], ones], axis=1))
        o = o[:, :128] / o[:, 128:]
        out.append(jnp.where(low, o[:n], o[n:]))
    return jnp.concatenate(out, axis=1)


def merge_norm(fine_ref, gain_ref, sel_ref, merged_ref):
    for l in range(2):
        parts = {}
        for p in range(2):
            rows = jnp.concatenate([fine_ref[l, 2 * i + p] for i in range(12)], axis=0)
            both = dot(sel_ref[...], rows)
            parts[p, 0] = both[:144]
            parts[p, 1] = both[144:]
        order = [parts[0, 0], parts[1, 0], parts[0, 1], parts[1, 1]]
        mean = sum(jnp.sum(a, axis=-1, keepdims=True) for a in order) * (1 / 2048)
        centred = [a - mean for a in order]
        spread = sum(jnp.sum(a * a, axis=-1, keepdims=True) for a in centred) * (1 / 2048)
        scale = lax.rsqrt(spread + eps)
        for n, a in enumerate(centred):
            cols = slice(n * 512, n * 512 + 512)
            merged_ref[l * 144:l * 144 + 144, cols] = (a * scale * gain_ref[:, cols]).astype(bf16)


def block_kernel(tokens_ref, above_ref, below_ref, outer_ref, gain_ref, own_qkv_ref, own_rest_ref, sibling_ref,
                 perm_ref, back_ref, mask_ref, merge_gain_ref, sel_ref, fine_ref, merged_ref, mid_ref, inner_ref, weights, sems):
    band = pl.program_id(0)
    bands = pl.num_programs(0)
    core = lax.axis_index("c")
    lat = lax.axis_index(LAT)

    @pl.when(band == 0)
    def _():
        copies = [
            pltpu.make_async_copy(above_ref, mid_ref.at[:, 0:3], sems.at[8]),
            pltpu.make_async_copy(tokens_ref, mid_ref.at[:, 3:27], sems.at[9]),
            pltpu.make_async_copy(below_ref, mid_ref.at[:, 27:30], sems.at[10]),
            pltpu.make_async_copy(sibling_ref.at[:, 4:6], inner_ref, sems.at[11]),
        ]
        for n in range(4):
            own = own_qkv_ref.at[:, n] if n < 3 else own_rest_ref.at[:, 0]
            copies.append(pltpu.make_async_copy(own, weights.at[n, :, core], sems.at[n]))
            copies.append(pltpu.make_async_copy(sibling_ref.at[:, n], weights.at[n, :, 1 - core], sems.at[4 + n]))
        for copy in copies:
            copy.start()
        for copy in copies:
            copy.wait()

    gain = gain_ref[...]
    raw = mid_ref[:, pl.ds(band * WL, WL)].reshape(288, 512)
    centre = norm(raw.astype(f32), gain).astype(bf16)
    centre = dot(perm_ref[...], centre)
    outer = norm(outer_ref[...].reshape(72, 512).astype(f32), gain)
    inner = inner_ref.reshape(32, 16, 512)[pl.ds(band * 5, 5)].reshape(80, 512)
    inner = norm(inner.astype(f32)[:72], gain)
    left = jnp.where(core == 0, outer, inner)
    right = jnp.where(core == 0, inner, outer)
    tokens = jnp.concatenate([left, centre, right], axis=0).astype(bf16)
    columns = [weights[n].reshape(512, 512) for n in range(4)]
    q = dot(centre.astype(bf16), columns[0]).astype(bf16) * jnp.asarray(0.125, bf16)
    k = dot(tokens, columns[1]).astype(bf16)
    v = dot(tokens, columns[2]).astype(bf16)
    low = lax.broadcasted_iota(jnp.int32, (1, 128), 1) < 64
    last = lax.axis_size(LAT) - 1
    edge = ((lat == 0) & (band == 0)) | ((lat == last) & (band == bands - 1))
    mask = mask_ref[...] * jnp.where(edge, 1.0, 0.0).astype(f32)
    spans = ((0, 72, 0), (72, 216, 144), (216, 288, 288))
    att = [attend(q[a:b], k[c:c + 144], v[c:c + 144], mask[a:b], low) for a, b, c in spans]
    att = jnp.concatenate(att, axis=0).astype(bf16)
    att = dot(back_ref[...], att).astype(bf16)
    out = dot(att, columns[3]) + raw.astype(f32)
    out = out.astype(bf16).reshape(2, WL, 24, 512)

    @pl.when(band > 0)
    def _():
        fine_ref[:, pl.ds(band * WL - 3, 3)] = out[:, :3]

    @pl.when(band < bands - 1)
    def _():
        fine_ref[:, pl.ds(band * WL, 3)] = out[:, 3:]

    @pl.when(band == bands - 1)
    def _():
        merge_norm(fine_ref, merge_gain_ref, sel_ref, merged_ref)


def merge_kernel(merged_ref, near_ref, far_ref, sibling_near_ref, sibling_far_ref, coarse_ref, weights, sems):
    core = lax.axis_index("c")
    slots = x_slots(lax.axis_index("x"))
    copies = []
    for n, (mine, other) in enumerate(((near_ref, sibling_near_ref), (far_ref, sibling_far_ref))):
        for slot in range(2):
            for col in range(2):
                for m, (ref, at) in enumerate(((mine, core), (other, 1 - core))):
                    copies.append(pltpu.make_async_copy(
                        ref.at[slot, :, col], weights.at[col, :, at, slots[n][slot]], sems.at[((n * 2 + slot) * 2 + col) * 2 + m]))
    for copy in copies:
        copy.start()
    for copy in copies:
        copy.wait()
    for col in range(2):
        part = dot(merged_ref[...], weights[col].reshape(2048, 512))
        coarse_ref[:, col * 512:col * 512 + 512] = part.astype(bf16)


def whole(shape):
    return pl.BlockSpec(shape, lambda *_: (0,) * len(shape))


def pack(w_qkv, w_proj, w_merge):
    return pl.pallas_call(
        pack_kernel,
        in_specs=[VMEM] * 3,
        out_specs=VMEM,
        out_shape=jax.ShapeDtypeStruct((6, 16, 512), bf16),
        name="pack_weights",
    )(w_qkv, w_proj, w_merge)


def edges(tokens, above, below):
    shapes = jax.ShapeDtypeStruct((5, 72, 512), bf16), jax.ShapeDtypeStruct((32, 16, 512), bf16)
    return pl.pallas_call(
        edge_kernel,
        in_specs=[VMEM] * 3,
        out_specs=(VMEM, VMEM),
        out_shape=shapes,
        compiler_params=pltpu.CompilerParams(vmem_limit_bytes=32 << 20),
        cost_estimate=pl.CostEstimate(flops=212_000_000, bytes_accessed=3 << 20, transcendentals=0),
        name="edge_rows",
    )(tokens, above, below)


def attention_block(tokens, above, below, outer, gain, own_qkv, own_rest, sibling, merge_gain):
    perm = one_hot(centre_order(), 288)
    return pl.pallas_call(
        block_kernel,
        grid=(5,),
        in_specs=[
            ANY,
            ANY,
            ANY,
            pl.BlockSpec((1, 72, 512), lambda b: (b, 0, 0)),
            whole((1, 512)),
            ANY,
            ANY,
            ANY,
            whole((288, 288)),
            whole((288, 288)),
            whole((288, 144)),
            whole((1, 2048)),
            whole((288, 288)),
        ],
        out_specs=(whole((2, 24, 24, 512)), whole((288, 2048))),
        out_shape=(jax.ShapeDtypeStruct((2, 24, 24, 512), bf16), jax.ShapeDtypeStruct((288, 2048), bf16)),
        scratch_shapes=[
            pltpu.VMEM((2, 30, 24, 512), bf16),
            pltpu.VMEM((16, 2, 16, 512), bf16),
            pltpu.VMEM((4, 16, 2, 16, 512), bf16),
            pltpu.SemaphoreType.DMA((12,)),
        ],
        compiler_params=pltpu.CompilerParams(vmem_limit_bytes=48 << 20),
        cost_estimate=pl.CostEstimate(flops=5_500_000_000, bytes_accessed=8 << 20, transcendentals=2_500_000),
        name="attention_block",
    )(tokens, above, below, outer, gain.reshape(1, 512), own_qkv, own_rest, sibling,
      jnp.asarray(perm), jnp.asarray(perm.T), jnp.asarray(edge_mask()), merge_gain.reshape(1, 2048),
      jnp.asarray(one_hot(merge_order(), 288)))


def merge_block(merged, near, far, sibling_near, sibling_far):
    return pl.pallas_call(
        merge_kernel,
        in_specs=[VMEM] + [ANY] * 4,
        out_specs=VMEM,
        out_shape=jax.ShapeDtypeStruct((288, 1024), bf16),
        scratch_shapes=[pltpu.VMEM((2, 16, 2, 4, 16, 512), bf16), pltpu.SemaphoreType.DMA((16,))],
        compiler_params=pltpu.CompilerParams(vmem_limit_bytes=40 << 20),
        cost_estimate=pl.CostEstimate(flops=1_200_000_000, bytes_accessed=8 << 20, transcendentals=0),
        name="merge_block",
    )(merged, near, far, sibling_near, sibling_far)


def shift(block, axes, distance):
    devices = range(lax.axis_size(axes))
    route = [((i - distance) % len(devices), i) for i in devices]
    return lax.ppermute(block, axes, route)


def swap(block, axis, partner):
    return lax.ppermute(block, axis, list(enumerate(partner)))


def between_chips(block):
    devices = range(lax.axis_size(LON))
    return lax.ppermute(block, LON, [(i, (i + (1 if i % 2 else -1)) % len(devices)) for i in devices])


def together(*arrays):
    return lax.optimization_barrier(arrays)


def on_device(tokens, attn_gain, w_qkv, w_proj, merge_gain, w_merge):
    above = shift(tokens[:, -3:], LAT, 1)
    below = shift(tokens[:, :3], LAT, -1)
    packed = lax.all_gather(pack(w_qkv, w_proj, w_merge), "zh")
    packed, above, below = together(packed, above, below)
    outer, inner = edges(tokens, above, below)
    outer = between_chips(outer)
    rest = lax.all_gather(packed[:, 3:], "y").reshape(16, 3, 16, 512)
    rest, outer = together(rest, outer)
    first, second = (1, 0, 3, 2), (3, 2, 1, 0)
    merge_own = rest[:, 1:]
    merge_pair = swap(merge_own, "x", first)
    qkv = lax.all_gather(packed[:, :3], "y").reshape(16, 3, 16, 512)
    merge_pair, qkv = together(merge_pair, qkv)
    near = jnp.stack([merge_own, merge_pair])
    far = swap(near, "x", second)
    sibling = shift(jnp.concatenate([qkv, rest[:, :1], inner.reshape(16, 2, 16, 512)], axis=1), "c", 1)
    sibling_near = shift(near, "c", 1)
    fine, merged = attention_block(tokens, above, below, outer, attn_gain, qkv, rest, sibling, merge_gain)
    far, sibling_near, merged = together(far, sibling_near, merged)
    sibling_far = shift(far, "c", 1)
    coarse = merge_block(merged, near, far, sibling_near, sibling_far)
    return fine, coarse.reshape(2, 12, 12, 1024)


def solution(mesh):
    lat, lon = mesh.shape["lat"], mesh.shape["lon"]
    fine_mesh = Mesh(mesh.devices.reshape(lat // 4, 4, 4, lon // 8, 2), LAT + LON)
    in_specs = (P(None, LAT, LON, None), P(), P(LON, None), P(LON, None), P(), P(LON, None))
    out_specs = (P(None, LAT, LON, None), P(None, LAT, LON, None))
    return jax.shard_map(
        on_device, mesh=fine_mesh, in_specs=in_specs, out_specs=out_specs, check_vma=False
    )
```

time: 139 us -> 126 us (0.906)
  starting transfers between devices: 46.5 us -> 34.6 us
  waiting for transfers between devices: 9.85 us -> 12 us
  local copies, waits for them, and re-layouts: 5.65 us -> 4.03 us
    ppermute x10 -> x5, starting transfers between devices: 41.7 us -> 25.1 us  [shift(): return lax.ppermute(block, axes, route)]
    ppermute x10 -> x5, waiting for transfers between devices: 9.85 us -> 2.28 us  [shift(): return lax.ppermute(block, axes, route)]
    ppermute x0 -> x2, waiting for transfers between devices: none -> 6.07 us  [swap(): return lax.ppermute(block, axis, list(enumerate(partner)))]
    ppermute x0 -> x2, starting transfers between devices: none -> 3.84 us  [swap(): return lax.ppermute(block, axis, list(enumerate(partner)))]
    ppermute x1, waiting for transfers between devices: 0.01 us -> 3.69 us  [between_chips(): lax.ppermute(block, LON, [(i, (i + (1 if i % 2 else -1)) % len(devices))...]
    unnamed x23 -> x17, local copies, waits for them, and re-layouts: 4.31 us -> 2.63 us
  transfers between devices with their start and end apart: 11 -> 8, of which waited for: 3 -> 3; matrix products, arithmetic and copies ran while one was open for 1% -> 0% of each run, Pallas kernels for 12% -> 15%
where the time goes in v3:
time: 126 us
  blocking collectives  53.1 us (42%)
  starting transfers between devices  34.6 us (27%)
  Pallas kernels  20.8 us (17%)
  waiting for transfers between devices  12 us (10%)
  local copies, waits for them, and re-layouts  4.03 us (3%)
    all_gather x1, blocking collectives, on_device(): packed = lax.all_gather(pack(w_qkv, w_proj, w_merge), 'zh')  29.1 us
    ppermute x5, starting transfers between devices, shift(): return lax.ppermute(block, axes, route)  25.1 us
    pallas_call x1, Pallas kernels, attention_block(): pl.pallas_call(block_kernel, grid=(5,), in_specs=[ANY, ANY, ANY, pl.Block...  16.7 us
    all_gather x1, blocking collectives, on_device(): rest = lax.all_gather(packed[:, 3:], 'y').reshape(16, 3, 16, 512)  12.1 us
    all_gather x1, blocking collectives, on_device(): qkv = lax.all_gather(packed[:, :3], 'y').reshape(16, 3, 16, 512)  12 us
    ppermute x2, waiting for transfers between devices, swap(): return lax.ppermute(block, axis, list(enumerate(partner)))  6.07 us
    ppermute x1, starting transfers between devices, between_chips(): lax.ppermute(block, LON, [(i, (i + (1 if i % 2 else -1)) % len(devices))...  5.64 us
    ppermute x2, starting transfers between devices, swap(): return lax.ppermute(block, axis, list(enumerate(partner)))  3.84 us
  transfers between devices with their start and end apart: 8, of which 3 were waited for; matrix products, arithmetic and copies ran while one was open for 0% of the time, Pallas kernels for 15%

profile of v3, /device:TPU:1, one launch (start us, length us, event | category | flops | bytes accessed | tf_op | source)
XLA Modules:
  0.0 125.7 jit_solution(400776588802615639)
XLA Ops:
  0.6 1.1 fusion
  1.7 3.9 %collective-permute-start = (bf16[2,3,24,512]{3,2,1,0:T(8,128)(2,1)S(1)}, bf16[2,3,24,512]{3,2,1,0:T(8,128)(2,1)S(1)}, u32[]{:S(2)}, u32[]{:S(2)}) collective-permute-start(bf16[2,3,24,512]{3,2,1,0:T(8,128)(2,1)S(1)} %get-tuple-element.37), channel_id=1, source_target_pairs={{480,0},{0,32},{32,64},{64,96},{96,128},{128,160},{160,192},{192,2... | collective-permute-start | bytes 442376 | tf_op jit(solution)/shard_map/ppermute | solution.py:290
  5.7 7.2 %collective-permute-start.1 = (bf16[2,3,24,512]{3,2,1,0:T(8,128)(2,1)S(1)}, bf16[2,3,24,512]{3,2,1,0:T(8,128)(2,1)S(1)}, u32[]{:S(2)}, u32[]{:S(2)}) collective-permute-start(bf16[2,3,24,512]{3,2,1,0:T(8,128)(2,1)S(1)} %get-tuple-element.36), channel_id=1, source_target_pairs={{32,0},{64,32},{96,64},{128,96},{160,128},{192,160},{224,192},{256... | collective-permute-start | bytes 442376 | tf_op jit(solution)/shard_map/ppermute | solution.py:290
  13.0 1.6 %pack_weights.1 = bf16[6,16,512]{2,1,0:T(8,128)(2,1)} custom-call(bf16[16,1536]{1,0:T(8,128)(2,1)} %qkv_ref.1, bf16[16,512]{1,0:T(8,128)(2,1)} %proj_ref.1, bf16[64,1024]{1,0:T(8,128)(2,1)} %merge_ref.1), custom_call_target="tpu_custom_call" | custom-call | tf_op jit(solution)/shard_map/pack_weights/pallas_call | solution.py:216
  14.6 29.1 %all-gather = bf16[24,16,512]{2,1,0:T(8,128)(2,1)S(1)} all-gather(bf16[6,16,512]{2,1,0:T(8,128)(2,1)} %pack_weights.1), channel_id=2, replica_groups=mesh['zl'=4,'x'=4,'y'=4,'zh'=4,'c'=2] {'zh'}, dimensions={0}, use_global_device_ids=true | all-gather | bytes 491520 | tf_op jit(solution)/shard_map/all_gather | solution.py:309
  43.6 0.6 edge_rows.1
  44.2 5.6 %collective-permute-start.2 = (bf16[5,72,512]{2,1,0:T(8,128)(2,1)S(1)}, bf16[5,72,512]{2,1,0:T(8,128)(2,1)S(1)}, u32[]{:S(2)}, u32[]{:S(2)}) collective-permute-start(bf16[5,72,512]{2,1,0:T(8,128)(2,1)S(1)} %get-tuple-element.19), channel_id=1, source_target_pairs={{0,31},{1,2},{2,1},{3,4},{4,3},{5,6},{6,5},{7,8},{8,7},{9,10},{10,... | collective-permute-start | bytes 1105928 | tf_op jit(solution)/shard_map/ppermute | solution.py:299
  49.9 12.1 %all-gather.1.own_rest_ref = bf16[16,3,16,512]{3,2,1,0:T(8,128)(2,1)S(1)} all-gather(bf16[4,3,16,512]{3,2,1,0:T(8,128)(2,1)S(1)} %get-tuple-element.41), channel_id=3, replica_groups=mesh['zl'=4,'x'=4,'y'=4,'zh'=4,'c'=2] {'y'}, dimensions={0}, use_global_device_ids=true | all-gather | bytes 983040 | tf_op jit(solution)/shard_map/all_gather | solution.py:313
  62.0 3.7 %collective-permute-done.2.outer_ref = bf16[5,72,512]{2,1,0:T(8,128)(2,1)S(1)} collective-permute-done((bf16[5,72,512]{2,1,0:T(8,128)(2,1)S(1)}, bf16[5,72,512]{2,1,0:T(8,128)(2,1)S(1)}, u32[]{:S(2)}, u32[]{:S(2)}) %collective-permute-start.2) | collective-permute-done | bytes 368672 | tf_op jit(solution)/shard_map/ppermute | solution.py:299
  65.6 0.1 slice_bitcast_fusion
  65.8 1.9 %collective-permute-start.3 = (bf16[16,2,16,512]{3,2,1,0:T(8,128)(2,1)S(1)}, bf16[16,2,16,512]{3,2,1,0:T(8,128)(2,1)S(1)}, u32[]{:S(2)}, u32[]{:S(2)}) collective-permute-start(bf16[16,2,16,512]{3,2,1,0:T(8,128)(2,1)S(1)} %get-tuple-element.39), channel_id=1, source_target_pairs={{0,32},{32,0},{64,96},{96,64},{1,33},{33,1},{65,97},{97,65},{2,34}... | collective-permute-start | bytes 1572872 | tf_op jit(solution)/shard_map/ppermute | solution.py:294
  67.7 12.0 %all-gather.2.own_qkv_ref = bf16[16,3,16,512]{3,2,1,0:T(8,128)(2,1)S(1)} all-gather(bf16[4,3,16,512]{3,2,1,0:T(8,128)(2,1)S(1)} %get-tuple-element.40), channel_id=4, replica_groups=mesh['zl'=4,'x'=4,'y'=4,'zh'=4,'c'=2] {'y'}, dimensions={0}, use_global_device_ids=true | all-gather | bytes 983040 | tf_op jit(solution)/shard_map/all_gather | solution.py:318
  79.7 0.2 pad_maximum_fusion
  80.0 9.3 %collective-permute-start.4 = (bf16[16,6,16,512]{3,2,1,0:T(8,128)(2,1)S(1)}, bf16[16,6,16,512]{3,2,1,0:T(8,128)(2,1)S(1)}, u32[]{:S(2)}, u32[]{:S(2)}) collective-permute-start(bf16[16,6,16,512]{3,2,1,0:T(8,128)(2,1)S(1)} %pad_maximum_fusion), channel_id=1, source_target_pairs={{1,0},{0,1},{3,2},{2,3},{5,4},{4,5},{7,6},{6,7},{9,8},{8,9},{11,10... | collective-permute-start | bytes 4718600 | tf_op jit(solution)/shard_map/ppermute | solution.py:290
  89.4 1.9 %collective-permute-start.5 = (bf16[2,16,2,16,512]{4,3,2,1,0:T(8,128)(2,1)S(1)}, bf16[2,16,2,16,512]{4,3,2,1,0:T(8,128)(2,1)S(1)}, u32[]{:S(2)}, u32[]{:S(2)}) collective-permute-start(bf16[2,16,2,16,512]{4,3,2,1,0:T(8,128)(2,1)S(1)} %pad_maximum_fusion.1.near_ref), channel_id=1, source_target_pairs={{0,96},{32,64},{64,32},{96,0},{1,97},{33,65},{65,33},{97,1},{2,98}... | collective-permute-start | bytes 3145736 | tf_op jit(solution)/shard_map/ppermute | solution.py:294
  91.3 1.9 %collective-permute-start.6 = (bf16[2,16,2,16,512]{4,3,2,1,0:T(8,128)(2,1)S(1)}, bf16[2,16,2,16,512]{4,3,2,1,0:T(8,128)(2,1)S(1)}, u32[]{:S(2)}, u32[]{:S(2)}) collective-permute-start(bf16[2,16,2,16,512]{4,3,2,1,0:T(8,128)(2,1)S(1)} %pad_maximum_fusion.1.near_ref), channel_id=1, source_target_pairs={{1,0},{0,1},{3,2},{2,3},{5,4},{4,5},{7,6},{6,7},{9,8},{8,9},{11,10... | collective-permute-start | bytes 3145736 | tf_op jit(solution)/shard_map/ppermute | solution.py:290
  93.2 1.2 copy-done.7
  94.4 16.7 %attention_block.1 = (bf16[2,24,24,512]{3,2,1,0:T(8,128)(2,1)}, bf16[288,2048]{1,0:T(8,128)(2,1)S(1)}) custom-call(bf16[2,24,24,512]{3,2,1,0:T(8,128)(2,1)S(1)} %copy-done, bf16[2,3,24,512]{3,2,1,0:T(8,128)(2,1)S(1)} %collective-permute-done.above_ref, bf16[2,3,24,512]{3,2,1,0:T(8,128)(2,1)S(1)} %collective-permute-done.1.below_ref, ...), custom_call_target="tpu_custom_call" | custom-call | flops 5500000256 | bytes 8388608 | tf_op jit(solution)/shard_map/attention_block/pallas_call | solution.py:240
  111.2 6.1 %collective-permute-done.5.far_ref = bf16[2,16,2,16,512]{4,3,2,1,0:T(8,128)(2,1)S(1)} collective-permute-done((bf16[2,16,2,16,512]{4,3,2,1,0:T(8,128)(2,1)S(1)}, bf16[2,16,2,16,512]{4,3,2,1,0:T(8,128)(2,1)S(1)}, u32[]{:S(2)}, u32[]{:S(2)}) %collective-permute-start.5) | collective-permute-done | bytes 1048608 | tf_op jit(solution)/shard_map/ppermute | solution.py:294
  117.3 2.7 %collective-permute-start.7 = (bf16[2,16,2,16,512]{4,3,2,1,0:T(8,128)(2,1)S(1)}, bf16[2,16,2,16,512]{4,3,2,1,0:T(8,128)(2,1)S(1)}, u32[]{:S(2)}, u32[]{:S(2)}) collective-permute-start(bf16[2,16,2,16,512]{4,3,2,1,0:T(8,128)(2,1)S(1)} %collective-permute-done.5.far_ref), channel_id=1, source_target_pairs={{1,0},{0,1},{3,2},{2,3},{5,4},{4,5},{7,6},{6,7},{9,8},{8,9},{11,10... | collective-permute-start | bytes 3145736 | tf_op jit(solution)/shard_map/ppermute | solution.py:290
  120.0 2.3 %collective-permute-done.7.sibling_far_ref = bf16[2,16,2,16,512]{4,3,2,1,0:T(8,128)(2,1)S(1)} collective-permute-done((bf16[2,16,2,16,512]{4,3,2,1,0:T(8,128)(2,1)S(1)}, bf16[2,16,2,16,512]{4,3,2,1,0:T(8,128)(2,1)S(1)}, u32[]{:S(2)}, u32[]{:S(2)}) %collective-permute-start.7) | collective-permute-done | bytes 1048608 | tf_op jit(solution)/shard_map/ppermute | solution.py:290
  122.2 1.9 %merge_block.1 = bf16[288,1024]{1,0:T(8,128)(2,1)S(1)} custom-call(bf16[288,2048]{1,0:T(8,128)(2,1)S(1)} %get-tuple-element.27.merged_ref, bf16[2,16,2,16,512]{4,3,2,1,0:T(8,128)(2,1)S(1)} %pad_maximum_fusion.1.near_ref, bf16[2,16,2,16,512]{4,3,2,1,0:T(8,128)(2,1)S(1)} %collective-permute-done.5.far_ref, ...), custom_call_target="tpu_custom_call" | custom-call | flops 1200000000 | bytes 8388608 | tf_op jit(solution)/shard_map/merge_block/pallas_call | solution.py:275
  124.1 0.1 reshape.27
  124.3 1.4 %copy.14 = bf16[2,12,12,1024]{3,0,2,1:T(2,128)(2,1)} copy(bf16[2,12,12,1024]{3,2,1,0:T(8,128)(2,1)S(1)} %reshape.27) | data formatting | bytes 1179648
  (23 shorter events, 0.2 us)
Async XLA Ops:
  0.6 43.0 %copy-start = (bf16[2,24,24,512]{3,2,1,0:T(8,128)(2,1)S(1)}, bf16[2,24,24,512]{3,2,1,0:T(8,128)(2,1)}, u32[]{:S(2)}) copy-start(bf16[2,24,24,512]{3,2,1,0:T(8,128)(2,1)} %tokens_ref.3) | copy-start | bytes 3538948
  1.7 41.9 %collective-permute-start = (bf16[2,3,24,512]{3,2,1,0:T(8,128)(2,1)S(1)}, bf16[2,3,24,512]{3,2,1,0:T(8,128)(2,1)S(1)}, u32[]{:S(2)}, u32[]{:S(2)}) collective-permute-start(bf16[2,3,24,512]{3,2,1,0:T(8,128)(2,1)S(1)} %get-tuple-element.37), channel_id=1, source_target_pairs={{480,0},{0,32},{32,64},{64,96},{96,128},{128,160},{160,192},{192,2... | collective-permute-start | bytes 442376 | tf_op jit(solution)/shard_map/ppermute | solution.py:290
  5.7 37.9 %collective-permute-start.1 = (bf16[2,3,24,512]{3,2,1,0:T(8,128)(2,1)S(1)}, bf16[2,3,24,512]{3,2,1,0:T(8,128)(2,1)S(1)}, u32[]{:S(2)}, u32[]{:S(2)}) collective-permute-start(bf16[2,3,24,512]{3,2,1,0:T(8,128)(2,1)S(1)} %get-tuple-element.36), channel_id=1, source_target_pairs={{32,0},{64,32},{96,64},{128,96},{160,128},{192,160},{224,192},{256... | collective-permute-start | bytes 442376 | tf_op jit(solution)/shard_map/ppermute | solution.py:290
  44.2 21.4 %collective-permute-start.2 = (bf16[5,72,512]{2,1,0:T(8,128)(2,1)S(1)}, bf16[5,72,512]{2,1,0:T(8,128)(2,1)S(1)}, u32[]{:S(2)}, u32[]{:S(2)}) collective-permute-start(bf16[5,72,512]{2,1,0:T(8,128)(2,1)S(1)} %get-tuple-element.19), channel_id=1, source_target_pairs={{0,31},{1,2},{2,1},{3,4},{4,3},{5,6},{6,5},{7,8},{8,7},{9,10},{10,... | collective-permute-start | bytes 1105928 | tf_op jit(solution)/shard_map/ppermute | solution.py:299
  65.8 13.9 %collective-permute-start.3 = (bf16[16,2,16,512]{3,2,1,0:T(8,128)(2,1)S(1)}, bf16[16,2,16,512]{3,2,1,0:T(8,128)(2,1)S(1)}, u32[]{:S(2)}, u32[]{:S(2)}) collective-permute-start(bf16[16,2,16,512]{3,2,1,0:T(8,128)(2,1)S(1)} %get-tuple-element.39), channel_id=1, source_target_pairs={{0,32},{32,0},{64,96},{96,64},{1,33},{33,1},{65,97},{97,65},{2,34}... | collective-permute-start | bytes 1572872 | tf_op jit(solution)/shard_map/ppermute | solution.py:294
  79.9 14.5 %copy-start.1 = (f32[2048]{0:T(1024)S(1)}, f32[2048]{0:T(1024)}, u32[]{:S(2)}) copy-start(f32[2048]{0:T(1024)} %param.14) | copy-start | bytes 24580
  79.9 14.5 %copy-start.2 = (f32[512]{0:T(512)S(1)}, f32[512]{0:T(512)}, u32[]{:S(2)}) copy-start(f32[512]{0:T(512)} %param.11) | copy-start | bytes 6148
  79.9 14.5 %copy-start.3 = (f32[288,144]{1,0:T(8,128)S(1)}, f32[288,144]{1,0:T(8,128)}, u32[]{:S(2)}) copy-start(f32[288,144]{1,0:T(8,128)} %constant.10.clone.mask_ref) | copy-start | bytes 497668
  79.9 14.5 %copy-start.4 = (bf16[288,288]{1,0:T(8,128)(2,1)S(1)}, bf16[288,288]{1,0:T(8,128)(2,1)}, u32[]{:S(2)}) copy-start(bf16[288,288]{1,0:T(8,128)(2,1)} %constant.11.clone.sel_ref) | copy-start | bytes 497668
  80.0 14.5 %copy-start.5 = (bf16[288,288]{1,0:T(8,128)(2,1)S(1)}, bf16[288,288]{1,0:T(8,128)(2,1)}, u32[]{:S(2)}) copy-start(bf16[288,288]{1,0:T(8,128)(2,1)} %constant.8.clone.perm_ref) | copy-start | bytes 497668
  80.0 14.5 %copy-start.6 = (bf16[288,288]{1,0:T(8,128)(2,1)S(1)}, bf16[288,288]{1,0:T(8,128)(2,1)}, u32[]{:S(2)}) copy-start(bf16[288,288]{1,0:T(8,128)(2,1)} %constant.9.clone.back_ref) | copy-start | bytes 497668
  80.0 13.2 %collective-permute-start.4 = (bf16[16,6,16,512]{3,2,1,0:T(8,128)(2,1)S(1)}, bf16[16,6,16,512]{3,2,1,0:T(8,128)(2,1)S(1)}, u32[]{:S(2)}, u32[]{:S(2)}) collective-permute-start(bf16[16,6,16,512]{3,2,1,0:T(8,128)(2,1)S(1)} %pad_maximum_fusion), channel_id=1, source_target_pairs={{1,0},{0,1},{3,2},{2,3},{5,4},{4,5},{7,6},{6,7},{9,8},{8,9},{11,10... | collective-permute-start | bytes 4718600 | tf_op jit(solution)/shard_map/ppermute | solution.py:290
  89.4 27.9 %collective-permute-start.5 = (bf16[2,16,2,16,512]{4,3,2,1,0:T(8,128)(2,1)S(1)}, bf16[2,16,2,16,512]{4,3,2,1,0:T(8,128)(2,1)S(1)}, u32[]{:S(2)}, u32[]{:S(2)}) collective-permute-start(bf16[2,16,2,16,512]{4,3,2,1,0:T(8,128)(2,1)S(1)} %pad_maximum_fusion.1.near_ref), channel_id=1, source_target_pairs={{0,96},{32,64},{64,32},{96,0},{1,97},{33,65},{65,33},{97,1},{2,98}... | collective-permute-start | bytes 3145736 | tf_op jit(solution)/shard_map/ppermute | solution.py:294
  91.3 26.0 %collective-permute-start.6 = (bf16[2,16,2,16,512]{4,3,2,1,0:T(8,128)(2,1)S(1)}, bf16[2,16,2,16,512]{4,3,2,1,0:T(8,128)(2,1)S(1)}, u32[]{:S(2)}, u32[]{:S(2)}) collective-permute-start(bf16[2,16,2,16,512]{4,3,2,1,0:T(8,128)(2,1)S(1)} %pad_maximum_fusion.1.near_ref), channel_id=1, source_target_pairs={{1,0},{0,1},{3,2},{2,3},{5,4},{4,5},{7,6},{6,7},{9,8},{8,9},{11,10... | collective-permute-start | bytes 3145736 | tf_op jit(solution)/shard_map/ppermute | solution.py:290
  93.2 1.2 copy-start.7
  117.3 5.0 %collective-permute-start.7 = (bf16[2,16,2,16,512]{4,3,2,1,0:T(8,128)(2,1)S(1)}, bf16[2,16,2,16,512]{4,3,2,1,0:T(8,128)(2,1)S(1)}, u32[]{:S(2)}, u32[]{:S(2)}) collective-permute-start(bf16[2,16,2,16,512]{4,3,2,1,0:T(8,128)(2,1)S(1)} %collective-permute-done.5.far_ref), channel_id=1, source_target_pairs={{1,0},{0,1},{3,2},{2,3},{5,4},{4,5},{7,6},{6,7},{9,8},{8,9},{11,10... | collective-permute-start | bytes 3145736 | tf_op jit(solution)/shard_map/ppermute | solution.py:290

commit v4 on v3

v4 whole, which is shorter than its diff:
```python
import numpy as np
import jax
import jax.numpy as jnp
from jax import lax
from jax.sharding import Mesh, PartitionSpec as P
from jax.experimental import pallas as pl
from jax.experimental.pallas import tpu as pltpu

HEADS = 8
WL = 6
eps = 1e-05
f32 = jnp.float32
bf16 = jnp.bfloat16
LAT = ("zl", "x")
LON = ("y", "zh", "c")
VMEM = pl.BlockSpec(memory_space=pltpu.VMEM)
ANY = pl.BlockSpec(memory_space=pl.ANY)


def centre_order():
    return np.array([r * 24 + c for first, last in ((0, 6), (6, 18), (18, 24)) for r in range(4) for c in range(first, last)])


def one_hot(order, n):
    return (order[:, None] == np.arange(n)[None, :]).astype(jnp.bfloat16)


def row_half():
    side = [r // 3 for l in range(2) for r in range(6) for c in range(6)]
    mid = [r // 3 for l in range(2) for r in range(6) for c in range(12)]
    return np.array(side + side + mid + side + side, np.float32)


def edge_mask():
    half = row_half()
    spans = ((0, 72), (72, 216), (216, 288))
    return np.concatenate([
        np.where(half[72 + a:72 + b, None] == half[None, n * 144:n * 144 + 144], 0.0, -1e30).astype(np.float32)
        for n, (a, b) in enumerate(spans)])


def merge_order():
    return np.array([(l * 4 + i) * 24 + 2 * j + p for p in range(2) for i in range(4) for j in range(12) for l in range(2)])


def dot(a, b, ca=1, cb=0):
    return lax.dot_general(a, b, (((ca,), (cb,)), ((), ())), preferred_element_type=f32)


def norm(x, gain):
    centred = x - jnp.mean(x, axis=-1, keepdims=True)
    spread = jnp.mean(centred * centred, axis=-1, keepdims=True)
    return centred * lax.rsqrt(spread + eps) * gain


def pack_kernel(tokens_ref, qkv_ref, proj_ref, merge_ref, out_ref, top_ref, bottom_ref):
    top_ref[...] = tokens_ref[:, 0:3]
    bottom_ref[...] = tokens_ref[:, 21:24]
    for n in range(3):
        out_ref[n] = qkv_ref[:, n * 512:n * 512 + 512]
    out_ref[3] = proj_ref[...]
    quarter = merge_ref[pl.ds(pl.multiple_of(lax.axis_index("x") * 16, 16), 16), :]
    out_ref[4] = quarter[:, :512]
    out_ref[5] = quarter[:, 512:]


def edge_kernel(tokens_ref, above_ref, below_ref, outer_ref, inner_ref):
    first = lax.axis_index("c") == 0
    o = lax.broadcasted_iota(jnp.int32, (144, 288), 0)
    side = (o * 911) >> 16
    lr = ((o - side * 72) * 10923) >> 16
    col = o - side * 72 - lr * 6 + side * 18
    sel = jnp.where(lax.broadcasted_iota(jnp.int32, (144, 288), 1) == lr * 24 + col, 1.0, 0.0).astype(bf16)
    for band in range(5):
        upper = tokens_ref[:, band * WL - 3:band * WL] if band > 0 else above_ref[...]
        lower = tokens_ref[:, band * WL:band * WL + 3] if band < 4 else below_ref[...]
        rows = jnp.concatenate([upper, lower], axis=1).reshape(288, 512)
        both = dot(sel, rows)
        left, right = both[:72], both[72:]
        outer_ref[band] = jnp.where(first, left, right).astype(bf16)
        inner = jnp.concatenate([jnp.where(first, right, left), jnp.zeros((8, 512), f32)], axis=0)
        inner_ref[band * 5:band * 5 + 5] = inner.astype(bf16).reshape(5, 16, 512)
    inner_ref[25:] = jnp.zeros((7, 16, 512), bf16)


def attend(q, k, v, bias, low):
    n = q.shape[0]
    out = []
    ones = jnp.ones((k.shape[0], 128), bf16)
    zero = jnp.zeros((), bf16)
    for pair in range(HEADS // 2):
        cols = slice(pair * 128, pair * 128 + 128)
        qp = q[:, cols]
        both = jnp.concatenate([jnp.where(low, qp, zero), jnp.where(low, zero, qp)], axis=0)
        s = dot(both, k[:, cols], 1, 1)
        s = s + jnp.concatenate([bias, bias], axis=0)
        e = jnp.exp(s - jnp.max(s, axis=-1, keepdims=True)).astype(bf16)
        o = dot(e, jnp.concatenate([v[:, cols], ones], axis=1))
        o = o[:, :128] / o[:, 128:]
        out.append(jnp.where(low, o[:n], o[n:]))
    return jnp.concatenate(out, axis=1)


def merge_norm(fine_ref, gain_ref, sel_ref, merged_ref):
    for chunk in range(3):
        parts = {}
        for p in range(2):
            rows = [fine_ref[l, 2 * (chunk * 4 + i) + p] for l in range(2) for i in range(4)]
            both = dot(sel_ref[...], jnp.concatenate(rows, axis=0))
            parts[p, 0] = both[:96]
            parts[p, 1] = both[96:]
        order = [parts[0, 0], parts[1, 0], parts[0, 1], parts[1, 1]]
        mean = sum(jnp.sum(a, axis=-1, keepdims=True) for a in order) * (1 / 2048)
        centred = [a - mean for a in order]
        spread = sum(jnp.sum(a * a, axis=-1, keepdims=True) for a in centred) * (1 / 2048)
        scale = lax.rsqrt(spread + eps)
        for n, a in enumerate(centred):
            cols = slice(n * 512, n * 512 + 512)
            merged_ref[chunk * 96:chunk * 96 + 96, cols] = (a * scale * gain_ref[:, cols]).astype(bf16)


def block_kernel(tokens_ref, above_ref, below_ref, outer_ref, gain_ref, own_qkv_ref, own_rest_ref, sibling_ref,
                 perm_ref, back_ref, mask_ref, merge_gain_ref, sel_ref, fine_ref, merged_ref,
                 mid_ref, inner_ref, weights, all_ref, q_ref, k_ref, v_ref, att_ref, sems):
    core = lax.axis_index("c")
    lat = lax.axis_index(LAT)
    last = lax.axis_size(LAT) - 1
    bands = 5
    copies = [
        pltpu.make_async_copy(above_ref, mid_ref.at[:, 0:3], sems.at[8]),
        pltpu.make_async_copy(tokens_ref, mid_ref.at[:, 3:27], sems.at[9]),
        pltpu.make_async_copy(below_ref, mid_ref.at[:, 27:30], sems.at[10]),
        pltpu.make_async_copy(sibling_ref.at[:, 4:6], inner_ref, sems.at[11]),
    ]
    for n in range(4):
        own = own_qkv_ref.at[:, n] if n < 3 else own_rest_ref.at[:, 0]
        copies.append(pltpu.make_async_copy(own, weights.at[n, :, core], sems.at[n]))
        copies.append(pltpu.make_async_copy(sibling_ref.at[:, n], weights.at[n, :, 1 - core], sems.at[4 + n]))
    for copy in copies:
        copy.start()
    for copy in copies[:4]:
        copy.wait()
    gain = gain_ref[...]

    def prepare(band, _):
        raw = mid_ref[:, pl.ds(band * WL, WL)].reshape(288, 512)
        centre = norm(raw.astype(f32), gain).astype(bf16)
        sets = [dot(perm_ref[...], centre[n * 96:n * 96 + 96]) for n in range(3)]
        outer = norm(outer_ref[band].astype(f32), gain)
        inner = inner_ref.reshape(32, 16, 512)[pl.ds(band * 5, 5)].reshape(80, 512)
        inner = norm(inner.astype(f32)[:72], gain)
        left = jnp.where(core == 0, outer, inner)
        right = jnp.where(core == 0, inner, outer)
        centre = [part[a:b] for a, b in ((0, 24), (24, 72), (72, 96)) for part in sets]
        rows = jnp.concatenate([left] + centre + [right], axis=0).astype(bf16)
        all_ref[pl.ds(pl.multiple_of(band * 432, 16), 432)] = rows
        return 0

    lax.fori_loop(0, bands, prepare, 0)
    for copy in copies[4:]:
        copy.wait()

    def product(n):
        return dot(all_ref[...], weights[n].reshape(512, 512)).astype(bf16)

    q_ref[...] = product(0) * jnp.asarray(0.125, bf16)
    k_ref[...] = product(1)
    v_ref[...] = product(2)
    low = lax.broadcasted_iota(jnp.int32, (1, 128), 1) < 64

    def attention(band, _):
        rows = pl.ds(pl.multiple_of(band * 432, 16), 432)
        q = q_ref[rows].astype(f32)[72:360].astype(bf16)
        k, v = k_ref[rows], v_ref[rows]
        edge = ((lat == 0) & (band == 0)) | ((lat == last) & (band == bands - 1))
        mask = mask_ref[...] * jnp.where(edge, 1.0, 0.0).astype(f32)
        spans = ((0, 72, 0), (72, 216, 144), (216, 288, 288))
        att = [attend(q[a:b], k[c:c + 144], v[c:c + 144], mask[a:b], low) for a, b, c in spans]
        for n in range(3):
            part = [att[0][24 * n:24 * n + 24], att[1][48 * n:48 * n + 48], att[2][24 * n:24 * n + 24]]
            part = dot(back_ref[...], jnp.concatenate(part, axis=0).astype(bf16)).astype(bf16)
            att_ref[pl.ds(pl.multiple_of(band * 288 + n * 96, 16), 96)] = part
        return 0

    lax.fori_loop(0, bands, attention, 0)
    for band in range(bands):
        raw = mid_ref[:, band * WL:band * WL + WL].reshape(288, 512)
        out = dot(att_ref[band * 288:band * 288 + 288], weights[3].reshape(512, 512)) + raw.astype(f32)
        out = out.astype(bf16).reshape(2, WL, 24, 512)
        if band > 0:
            fine_ref[:, band * WL - 3:band * WL] = out[:, :3]
        if band < bands - 1:
            fine_ref[:, band * WL:band * WL + 3] = out[:, 3:]
    merge_norm(fine_ref, merge_gain_ref, sel_ref, merged_ref)


def merge_kernel(merged_ref, own_ref, pair_ref, across_ref, opposite_ref, sibling_ref, sibling_opposite_ref, coarse_ref,
                 weights, sems):
    core = lax.axis_index("c")
    x = lax.axis_index("x")
    pair = x + 1 - 2 * lax.rem(x, 2)
    pieces = [
        (own_ref.at[:, 1:3], core, x),
        (pair_ref, core, pair),
        (across_ref, core, 3 - x),
        (opposite_ref, core, 3 - pair),
        (sibling_ref.at[0], 1 - core, x),
        (sibling_ref.at[1], 1 - core, pair),
        (sibling_ref.at[2], 1 - core, 3 - x),
        (sibling_opposite_ref, 1 - core, 3 - pair),
    ]
    copies = [pltpu.make_async_copy(ref.at[:, col], weights.at[col, :, at, there], sems.at[2 * n + col])
              for n, (ref, at, there) in enumerate(pieces) for col in range(2)]
    for copy in copies:
        copy.start()
    for copy in copies:
        copy.wait()
    for col in range(2):
        part = dot(merged_ref[...], weights[col].reshape(2048, 512)).astype(bf16)
        coarse_ref[:, :, col * 512:col * 512 + 512] = part.reshape(144, 2, 512)


def pack(tokens, w_qkv, w_proj, w_merge):
    rows = jax.ShapeDtypeStruct((2, 3, 24, 512), bf16)
    return pl.pallas_call(
        pack_kernel,
        in_specs=[VMEM] * 4,
        out_specs=(VMEM,) * 3,
        out_shape=(jax.ShapeDtypeStruct((6, 16, 512), bf16), rows, rows),
        name="pack_parts",
    )(tokens, w_qkv, w_proj, w_merge)


def edges(tokens, above, below):
    shapes = jax.ShapeDtypeStruct((5, 72, 512), bf16), jax.ShapeDtypeStruct((32, 16, 512), bf16)
    return pl.pallas_call(
        edge_kernel,
        in_specs=[VMEM] * 3,
        out_specs=(VMEM, VMEM),
        out_shape=shapes,
        compiler_params=pltpu.CompilerParams(vmem_limit_bytes=32 << 20),
        cost_estimate=pl.CostEstimate(flops=212_000_000, bytes_accessed=3 << 20, transcendentals=0),
        name="edge_rows",
    )(tokens, above, below)


def attention_block(tokens, above, below, outer, gain, own_qkv, own_rest, sibling, merge_gain):
    perm = one_hot(centre_order(), 96)
    return pl.pallas_call(
        block_kernel,
        in_specs=[ANY, ANY, ANY, VMEM, VMEM, ANY, ANY, ANY] + [VMEM] * 5,
        out_specs=(VMEM, VMEM),
        out_shape=(jax.ShapeDtypeStruct((2, 24, 24, 512), bf16), jax.ShapeDtypeStruct((288, 2048), bf16)),
        scratch_shapes=[
            pltpu.VMEM((2, 30, 24, 512), bf16),
            pltpu.VMEM((16, 2, 16, 512), bf16),
            pltpu.VMEM((4, 16, 2, 16, 512), bf16),
            pltpu.VMEM((2160, 512), bf16),
            pltpu.VMEM((2160, 512), bf16),
            pltpu.VMEM((2160, 512), bf16),
            pltpu.VMEM((2160, 512), bf16),
            pltpu.VMEM((1440, 512), bf16),
            pltpu.SemaphoreType.DMA((12,)),
        ],
        compiler_params=pltpu.CompilerParams(vmem_limit_bytes=40 << 20),
        cost_estimate=pl.CostEstimate(flops=5_500_000_000, bytes_accessed=8 << 20, transcendentals=2_500_000),
        name="attention_block",
    )(tokens, above, below, outer, gain.reshape(1, 512), own_qkv, own_rest, sibling,
      jnp.asarray(perm), jnp.asarray(perm.T), jnp.asarray(edge_mask()), merge_gain.reshape(1, 2048),
      jnp.asarray(one_hot(merge_order(), 192)))


def merge_block(merged, own, pair, across, opposite, sibling, sibling_opposite):
    return pl.pallas_call(
        merge_kernel,
        in_specs=[VMEM] + [ANY] * 6,
        out_specs=VMEM,
        out_shape=jax.ShapeDtypeStruct((144, 2, 1024), bf16),
        scratch_shapes=[pltpu.VMEM((2, 16, 2, 4, 16, 512), bf16), pltpu.SemaphoreType.DMA((16,))],
        compiler_params=pltpu.CompilerParams(vmem_limit_bytes=24 << 20),
        cost_estimate=pl.CostEstimate(flops=1_200_000_000, bytes_accessed=8 << 20, transcendentals=0),
        name="merge_block",
    )(merged, own, pair, across, opposite, sibling, sibling_opposite)


def shift(block, axes, distance):
    devices = range(lax.axis_size(axes))
    route = [((i - distance) % len(devices), i) for i in devices]
    return lax.ppermute(block, axes, route)


def swap(block, axis, partner):
    return lax.ppermute(block, axis, list(enumerate(partner)))


def between_chips(block):
    devices = range(lax.axis_size(LON))
    return lax.ppermute(block, LON, [(i, (i + (1 if i % 2 else -1)) % len(devices)) for i in devices])


def together(*arrays):
    return lax.optimization_barrier(arrays)


def on_device(tokens, attn_gain, w_qkv, w_proj, merge_gain, w_merge):
    packed, top, bottom = pack(tokens, w_qkv, w_proj, w_merge)
    above = shift(bottom, LAT, 1)
    below = shift(top, LAT, -1)
    packed = lax.all_gather(packed, "zh")
    packed, above, below = together(packed, above, below)
    outer, inner = edges(tokens, above, below)
    outer = between_chips(outer)
    rest = lax.all_gather(packed[:, 3:], "y").reshape(16, 3, 16, 512)
    first, second = (1, 0, 3, 2), (3, 2, 1, 0)
    merge_own = rest[:, 1:]
    pair = swap(merge_own, "x", first)
    across = swap(merge_own, "x", second)
    qkv = lax.all_gather(packed[:, :3], "y").reshape(16, 3, 16, 512)
    pair, across, qkv, outer = together(pair, across, qkv, outer)
    opposite = swap(across, "x", first)
    sibling = shift(jnp.concatenate([qkv, rest[:, :1], inner.reshape(16, 2, 16, 512)], axis=1), "c", 1)
    sibling_merge = shift(jnp.stack([merge_own, pair, across]), "c", 1)
    fine, merged = attention_block(tokens, above, below, outer, attn_gain, qkv, rest, sibling, merge_gain)
    opposite, sibling_merge, merged = together(opposite, sibling_merge, merged)
    sibling_opposite = shift(opposite, "c", 1)
    coarse = merge_block(merged, rest, pair, across, opposite, sibling_merge, sibling_opposite)
    return fine, coarse.reshape(12, 12, 2, 1024).transpose(2, 0, 1, 3)


def solution(mesh):
    lat, lon = mesh.shape["lat"], mesh.shape["lon"]
    fine_mesh = Mesh(mesh.devices.reshape(lat // 4, 4, 4, lon // 8, 2), LAT + LON)
    in_specs = (P(None, LAT, LON, None), P(), P(LON, None), P(LON, None), P(), P(LON, None))
    out_specs = (P(None, LAT, LON, None), P(None, LAT, LON, None))
    return jax.shard_map(
        on_device, mesh=fine_mesh, in_specs=in_specs, out_specs=out_specs, check_vma=False
    )
```

time: 126 us -> 118 us (0.937)
  waiting for transfers between devices: 12 us -> 4.98 us
  local copies, waits for them, and re-layouts: 4.03 us -> 0.17 us
  starting transfers between devices: 34.6 us -> 37.1 us
    ppermute x2 -> x3, waiting for transfers between devices: 6.07 us -> 0.01 us  [swap(): return lax.ppermute(block, axis, list(enumerate(partner)))]
    ppermute x1, starting transfers between devices: 5.64 us -> 8.49 us  [between_chips(): lax.ppermute(block, LON, [(i, (i + (1 if i % 2 else -1)) % len(devices))...]
    unnamed x17 -> x14, local copies, waits for them, and re-layouts: 2.63 us -> 0.05 us
    ppermute x5, starting transfers between devices: 25.1 us -> 22.5 us  [shift(): return lax.ppermute(block, axes, route)]
    ppermute x2 -> x3, starting transfers between devices: 3.84 us -> 6.05 us  [swap(): return lax.ppermute(block, axis, list(enumerate(partner)))]
  transfers between devices with their start and end apart: 8 -> 9, of which waited for: 3 -> 2; matrix products, arithmetic and copies ran while one was open for 0% -> 0% of each run, Pallas kernels for 15% -> 13%
where the time goes in v4:
time: 118 us
  blocking collectives  53.9 us (46%)
  starting transfers between devices  37.1 us (31%)
  Pallas kernels  20.7 us (18%)
  waiting for transfers between devices  4.98 us (4%)
    all_gather x1, blocking collectives, on_device(): packed = lax.all_gather(packed, 'zh')  28.4 us
    ppermute x5, starting transfers between devices, shift(): return lax.ppermute(block, axes, route)  22.5 us
    pallas_call x1, Pallas kernels, attention_block(): pl.pallas_call(block_kernel, in_specs=[ANY, ANY, ANY, VMEM, VMEM, ANY, AN...  15.3 us
    all_gather x1, blocking collectives, on_device(): qkv = lax.all_gather(packed[:, :3], 'y').reshape(16, 3, 16, 512)  12.8 us
    all_gather x1, blocking collectives, on_device(): rest = lax.all_gather(packed[:, 3:], 'y').reshape(16, 3, 16, 512)  12.7 us
    ppermute x1, starting transfers between devices, between_chips(): lax.ppermute(block, LON, [(i, (i + (1 if i % 2 else -1)) % len(devices))...  8.49 us
    ppermute x3, starting transfers between devices, swap(): return lax.ppermute(block, axis, list(enumerate(partner)))  6.05 us
    ppermute x1, waiting for transfers between devices, between_chips(): lax.ppermute(block, LON, [(i, (i + (1 if i % 2 else -1)) % len(devices))...  3.45 us
  transfers between devices with their start and end apart: 9, of which 2 were waited for; matrix products, arithmetic and copies ran while one was open for 0% of the time, Pallas kernels for 13%

profile of v4, /device:TPU:1, one launch (start us, length us, event | category | flops | bytes accessed | tf_op | source)
XLA Modules:
  0.0 118.0 jit_solution(8061101186069618031)
XLA Ops:
  0.6 2.1 %pack_parts.1 = (bf16[6,16,512]{2,1,0:T(8,128)(2,1)}, bf16[2,3,24,512]{3,2,1,0:T(8,128)(2,1)}, bf16[2,3,24,512]{3,2,1,0:T(8,128)(2,1)}) custom-call(bf16[2,24,24,512]{3,2,1,0:T(8,128)(2,1)} %tokens_ref.5, bf16[16,1536]{1,0:T(8,128)(2,1)} %qkv_ref.1, bf16[16,512]{1,0:T(8,128)(2,1)} %proj_ref.1, bf16[64,1024]{1,0:T(8,128)(2,1)} %merge_ref.1), custom_call_target="tpu_custom_call" | custom-call | tf_op jit(solution)/shard_map/pack_parts/pallas_call | solution.py:225
  2.7 3.9 %collective-permute-start = (bf16[2,3,24,512]{3,2,1,0:T(8,128)(2,1)}, bf16[2,3,24,512]{3,2,1,0:T(8,128)(2,1)S(1)}, u32[]{:S(2)}, u32[]{:S(2)}) collective-permute-start(bf16[2,3,24,512]{3,2,1,0:T(8,128)(2,1)} %get-tuple-element.20), channel_id=1, source_target_pairs={{480,0},{0,32},{32,64},{64,96},{96,128},{128,160},{160,192},{192,2... | collective-permute-start | bytes 442376 | tf_op jit(solution)/shard_map/ppermute | solution.py:289
  6.6 7.2 %collective-permute-start.1 = (bf16[2,3,24,512]{3,2,1,0:T(8,128)(2,1)}, bf16[2,3,24,512]{3,2,1,0:T(8,128)(2,1)S(1)}, u32[]{:S(2)}, u32[]{:S(2)}) collective-permute-start(bf16[2,3,24,512]{3,2,1,0:T(8,128)(2,1)} %get-tuple-element.21), channel_id=1, source_target_pairs={{32,0},{64,32},{96,64},{128,96},{160,128},{192,160},{224,192},{256... | collective-permute-start | bytes 442376 | tf_op jit(solution)/shard_map/ppermute | solution.py:289
  13.9 28.4 %all-gather = bf16[24,16,512]{2,1,0:T(8,128)(2,1)S(1)} all-gather(bf16[6,16,512]{2,1,0:T(8,128)(2,1)} %get-tuple-element.19), channel_id=2, replica_groups=mesh['zl'=4,'x'=4,'y'=4,'zh'=4,'c'=2] {'zh'}, dimensions={0}, use_global_device_ids=true | all-gather | bytes 491520 | tf_op jit(solution)/shard_map/all_gather | solution.py:309
  42.4 12.7 %all-gather.1.own_rest_ref.own_ref = bf16[16,3,16,512]{3,2,1,0:T(8,128)(2,1)S(1)} all-gather(bf16[4,3,16,512]{3,2,1,0:T(8,128)(2,1)S(1)} %get-tuple-element.39), channel_id=3, replica_groups=mesh['zl'=4,'x'=4,'y'=4,'zh'=4,'c'=2] {'y'}, dimensions={0}, use_global_device_ids=true | all-gather | bytes 983040 | tf_op jit(solution)/shard_map/all_gather | solution.py:313
  55.0 0.1 slice_bitcast_fusion
  55.1 1.9 %collective-permute-start.2 = (bf16[16,2,16,512]{3,2,1,0:T(8,128)(2,1)S(1)}, bf16[16,2,16,512]{3,2,1,0:T(8,128)(2,1)S(1)}, u32[]{:S(2)}, u32[]{:S(2)}) collective-permute-start(bf16[16,2,16,512]{3,2,1,0:T(8,128)(2,1)S(1)} %get-tuple-element.37), channel_id=1, source_target_pairs={{0,32},{32,0},{64,96},{96,64},{1,33},{33,1},{65,97},{97,65},{2,34}... | collective-permute-start | bytes 1572872 | tf_op jit(solution)/shard_map/ppermute | solution.py:293
  57.0 1.9 %collective-permute-start.3 = (bf16[16,2,16,512]{3,2,1,0:T(8,128)(2,1)S(1)}, bf16[16,2,16,512]{3,2,1,0:T(8,128)(2,1)S(1)}, u32[]{:S(2)}, u32[]{:S(2)}) collective-permute-start(bf16[16,2,16,512]{3,2,1,0:T(8,128)(2,1)S(1)} %get-tuple-element.37), channel_id=1, source_target_pairs={{0,96},{32,64},{64,32},{96,0},{1,97},{33,65},{65,33},{97,1},{2,98}... | collective-permute-start | bytes 1572872 | tf_op jit(solution)/shard_map/ppermute | solution.py:293
  59.0 0.6 edge_rows.1
  59.5 8.5 %collective-permute-start.4 = (bf16[5,72,512]{2,1,0:T(8,128)(2,1)S(1)}, bf16[5,72,512]{2,1,0:T(8,128)(2,1)S(1)}, u32[]{:S(2)}, u32[]{:S(2)}) collective-permute-start(bf16[5,72,512]{2,1,0:T(8,128)(2,1)S(1)} %get-tuple-element.25), channel_id=1, source_target_pairs={{0,31},{1,2},{2,1},{3,4},{4,3},{5,6},{6,5},{7,8},{8,7},{9,10},{10,... | collective-permute-start | bytes 1105928 | tf_op jit(solution)/shard_map/ppermute | solution.py:298
  68.1 12.8 %all-gather.2.own_qkv_ref = bf16[16,3,16,512]{3,2,1,0:T(8,128)(2,1)S(1)} all-gather(bf16[4,3,16,512]{3,2,1,0:T(8,128)(2,1)S(1)} %get-tuple-element.38), channel_id=4, replica_groups=mesh['zl'=4,'x'=4,'y'=4,'zh'=4,'c'=2] {'y'}, dimensions={0}, use_global_device_ids=true | all-gather | bytes 983040 | tf_op jit(solution)/shard_map/all_gather | solution.py:318
  80.9 3.4 %collective-permute-done.4.outer_ref = bf16[5,72,512]{2,1,0:T(8,128)(2,1)S(1)} collective-permute-done((bf16[5,72,512]{2,1,0:T(8,128)(2,1)S(1)}, bf16[5,72,512]{2,1,0:T(8,128)(2,1)S(1)}, u32[]{:S(2)}, u32[]{:S(2)}) %collective-permute-start.4) | collective-permute-done | bytes 368672 | tf_op jit(solution)/shard_map/ppermute | solution.py:298
  84.3 0.2 pad_maximum_fusion
  84.5 6.7 %collective-permute-start.5 = (bf16[16,6,16,512]{3,2,1,0:T(8,128)(2,1)S(1)}, bf16[16,6,16,512]{3,2,1,0:T(8,128)(2,1)S(1)}, u32[]{:S(2)}, u32[]{:S(2)}) collective-permute-start(bf16[16,6,16,512]{3,2,1,0:T(8,128)(2,1)S(1)} %pad_maximum_fusion), channel_id=1, source_target_pairs={{1,0},{0,1},{3,2},{2,3},{5,4},{4,5},{7,6},{6,7},{9,8},{8,9},{11,10... | collective-permute-start | bytes 4718600 | tf_op jit(solution)/shard_map/ppermute | solution.py:289
  91.3 0.0 copy-start.3
  91.3 0.0 copy-start.5
  91.3 0.0 copy-start.6
  91.3 0.2 pad_maximum_fusion.1
  91.5 1.9 %collective-permute-start.7 = (bf16[3,16,2,16,512]{4,3,2,1,0:T(8,128)(2,1)S(1)}, bf16[3,16,2,16,512]{4,3,2,1,0:T(8,128)(2,1)S(1)}, u32[]{:S(2)}, u32[]{:S(2)}) collective-permute-start(bf16[3,16,2,16,512]{4,3,2,1,0:T(8,128)(2,1)S(1)} %pad_maximum_fusion.1), channel_id=1, source_target_pairs={{1,0},{0,1},{3,2},{2,3},{5,4},{4,5},{7,6},{6,7},{9,8},{8,9},{11,10... | collective-permute-start | bytes 4718600 | tf_op jit(solution)/shard_map/ppermute | solution.py:289
  93.4 2.2 %collective-permute-start.6 = (bf16[16,2,16,512]{3,2,1,0:T(8,128)(2,1)S(1)}, bf16[16,2,16,512]{3,2,1,0:T(8,128)(2,1)S(1)}, u32[]{:S(2)}, u32[]{:S(2)}) collective-permute-start(bf16[16,2,16,512]{3,2,1,0:T(8,128)(2,1)S(1)} %collective-permute-done.3.across_ref), channel_id=1, source_target_pairs={{0,32},{32,0},{64,96},{96,64},{1,33},{33,1},{65,97},{97,65},{2,34}... | collective-permute-start | bytes 1572872 | tf_op jit(solution)/shard_map/ppermute | solution.py:293
  95.7 15.3 %attention_block.1 = (bf16[2,24,24,512]{3,2,1,0:T(8,128)(2,1)}, bf16[288,2048]{1,0:T(8,128)(2,1)S(1)}) custom-call(bf16[2,24,24,512]{3,2,1,0:T(8,128)(2,1)S(1)} %copy-done, bf16[2,3,24,512]{3,2,1,0:T(8,128)(2,1)S(1)} %collective-permute-done.above_ref, bf16[2,3,24,512]{3,2,1,0:T(8,128)(2,1)S(1)} %collective-permute-done.1.below_ref, ...), custom_call_target="tpu_custom_call" | custom-call | flops 5500000256 | bytes 8388608 | tf_op jit(solution)/shard_map/attention_block/pallas_call | solution.py:249
  111.1 2.7 %collective-permute-start.8 = (bf16[16,2,16,512]{3,2,1,0:T(8,128)(2,1)S(1)}, bf16[16,2,16,512]{3,2,1,0:T(8,128)(2,1)S(1)}, u32[]{:S(2)}, u32[]{:S(2)}) collective-permute-start(bf16[16,2,16,512]{3,2,1,0:T(8,128)(2,1)S(1)} %collective-permute-done.6.opposite_ref), channel_id=1, source_target_pairs={{1,0},{0,1},{3,2},{2,3},{5,4},{4,5},{7,6},{6,7},{9,8},{8,9},{11,10... | collective-permute-start | bytes 1572872 | tf_op jit(solution)/shard_map/ppermute | solution.py:289
  113.8 1.5 %collective-permute-done.8.sibling_opposite_ref = bf16[16,2,16,512]{3,2,1,0:T(8,128)(2,1)S(1)} collective-permute-done((bf16[16,2,16,512]{3,2,1,0:T(8,128)(2,1)S(1)}, bf16[16,2,16,512]{3,2,1,0:T(8,128)(2,1)S(1)}, u32[]{:S(2)}, u32[]{:S(2)}) %collective-permute-start.8) | collective-permute-done | bytes 524320 | tf_op jit(solution)/shard_map/ppermute | solution.py:289
  115.3 2.7 %merge_block.1 = bf16[144,2,1024]{2,1,0:T(2,128)(2,1)} custom-call(bf16[288,2048]{1,0:T(8,128)(2,1)S(1)} %get-tuple-element.33.merged_ref, bf16[16,3,16,512]{3,2,1,0:T(8,128)(2,1)S(1)} %all-gather.1.own_rest_ref.own_ref, bf16[16,2,16,512]{3,2,1,0:T(8,128)(2,1)S(1)} %collective-permute-done.2.pair_ref, ...), custom_call_target="tpu_custom_call" | custom-call | flops 1200000000 | bytes 8388608 | tf_op jit(solution)/shard_map/merge_block/pallas_call | solution.py:274
  (20 shorter events, 0.1 us)
Async XLA Ops:
  2.7 39.6 %collective-permute-start = (bf16[2,3,24,512]{3,2,1,0:T(8,128)(2,1)}, bf16[2,3,24,512]{3,2,1,0:T(8,128)(2,1)S(1)}, u32[]{:S(2)}, u32[]{:S(2)}) collective-permute-start(bf16[2,3,24,512]{3,2,1,0:T(8,128)(2,1)} %get-tuple-element.20), channel_id=1, source_target_pairs={{480,0},{0,32},{32,64},{64,96},{96,128},{128,160},{160,192},{192,2... | collective-permute-start | bytes 442376 | tf_op jit(solution)/shard_map/ppermute | solution.py:289
  6.6 35.7 %collective-permute-start.1 = (bf16[2,3,24,512]{3,2,1,0:T(8,128)(2,1)}, bf16[2,3,24,512]{3,2,1,0:T(8,128)(2,1)S(1)}, u32[]{:S(2)}, u32[]{:S(2)}) collective-permute-start(bf16[2,3,24,512]{3,2,1,0:T(8,128)(2,1)} %get-tuple-element.21), channel_id=1, source_target_pairs={{32,0},{64,32},{96,64},{128,96},{160,128},{192,160},{224,192},{256... | collective-permute-start | bytes 442376 | tf_op jit(solution)/shard_map/ppermute | solution.py:289
  42.3 16.6 %copy-start = (bf16[2,24,24,512]{3,2,1,0:T(8,128)(2,1)S(1)}, bf16[2,24,24,512]{3,2,1,0:T(8,128)(2,1)}, u32[]{:S(2)}) copy-start(bf16[2,24,24,512]{3,2,1,0:T(8,128)(2,1)} %tokens_ref.5) | copy-start | bytes 3538948
  55.1 29.2 %collective-permute-start.2 = (bf16[16,2,16,512]{3,2,1,0:T(8,128)(2,1)S(1)}, bf16[16,2,16,512]{3,2,1,0:T(8,128)(2,1)S(1)}, u32[]{:S(2)}, u32[]{:S(2)}) collective-permute-start(bf16[16,2,16,512]{3,2,1,0:T(8,128)(2,1)S(1)} %get-tuple-element.37), channel_id=1, source_target_pairs={{0,32},{32,0},{64,96},{96,64},{1,33},{33,1},{65,97},{97,65},{2,34}... | collective-permute-start | bytes 1572872 | tf_op jit(solution)/shard_map/ppermute | solution.py:293
  57.0 27.3 %collective-permute-start.3 = (bf16[16,2,16,512]{3,2,1,0:T(8,128)(2,1)S(1)}, bf16[16,2,16,512]{3,2,1,0:T(8,128)(2,1)S(1)}, u32[]{:S(2)}, u32[]{:S(2)}) collective-permute-start(bf16[16,2,16,512]{3,2,1,0:T(8,128)(2,1)S(1)} %get-tuple-element.37), channel_id=1, source_target_pairs={{0,96},{32,64},{64,32},{96,0},{1,97},{33,65},{65,33},{97,1},{2,98}... | collective-permute-start | bytes 1572872 | tf_op jit(solution)/shard_map/ppermute | solution.py:293
  59.5 24.8 %collective-permute-start.4 = (bf16[5,72,512]{2,1,0:T(8,128)(2,1)S(1)}, bf16[5,72,512]{2,1,0:T(8,128)(2,1)S(1)}, u32[]{:S(2)}, u32[]{:S(2)}) collective-permute-start(bf16[5,72,512]{2,1,0:T(8,128)(2,1)S(1)} %get-tuple-element.25), channel_id=1, source_target_pairs={{0,31},{1,2},{2,1},{3,4},{4,3},{5,6},{6,5},{7,8},{8,7},{9,10},{10,... | collective-permute-start | bytes 1105928 | tf_op jit(solution)/shard_map/ppermute | solution.py:298
  84.5 11.1 %collective-permute-start.5 = (bf16[16,6,16,512]{3,2,1,0:T(8,128)(2,1)S(1)}, bf16[16,6,16,512]{3,2,1,0:T(8,128)(2,1)S(1)}, u32[]{:S(2)}, u32[]{:S(2)}) collective-permute-start(bf16[16,6,16,512]{3,2,1,0:T(8,128)(2,1)S(1)} %pad_maximum_fusion), channel_id=1, source_target_pairs={{1,0},{0,1},{3,2},{2,3},{5,4},{4,5},{7,6},{6,7},{9,8},{8,9},{11,10... | collective-permute-start | bytes 4718600 | tf_op jit(solution)/shard_map/ppermute | solution.py:289
  91.2 4.4 %copy-start.1 = (f32[2048]{0:T(1024)S(1)}, f32[2048]{0:T(1024)}, u32[]{:S(2)}) copy-start(f32[2048]{0:T(1024)} %param.14) | copy-start | bytes 24580
  91.2 4.4 %copy-start.2 = (f32[512]{0:T(512)S(1)}, f32[512]{0:T(512)}, u32[]{:S(2)}) copy-start(f32[512]{0:T(512)} %param.11) | copy-start | bytes 6148
  91.3 4.4 %copy-start.3 = (f32[288,144]{1,0:T(8,128)S(1)}, f32[288,144]{1,0:T(8,128)}, u32[]{:S(2)}) copy-start(f32[288,144]{1,0:T(8,128)} %constant.10.clone.mask_ref) | copy-start | bytes 497668
  91.3 4.4 %copy-start.4 = (bf16[192,192]{1,0:T(8,128)(2,1)S(1)}, bf16[192,192]{1,0:T(8,128)(2,1)}, u32[]{:S(2)}) copy-start(bf16[192,192]{1,0:T(8,128)(2,1)} %constant.11.clone.sel_ref) | copy-start | bytes 221188
  91.3 4.4 %copy-start.5 = (bf16[96,96]{1,0:T(8,128)(2,1)S(1)}, bf16[96,96]{1,0:T(8,128)(2,1)}, u32[]{:S(2)}) copy-start(bf16[96,96]{1,0:T(8,128)(2,1)} %constant.8.clone.perm_ref) | copy-start | bytes 55300
  91.3 4.4 %copy-start.6 = (bf16[96,96]{1,0:T(8,128)(2,1)S(1)}, bf16[96,96]{1,0:T(8,128)(2,1)}, u32[]{:S(2)}) copy-start(bf16[96,96]{1,0:T(8,128)(2,1)} %constant.9.clone.back_ref) | copy-start | bytes 55300
  91.5 19.6 %collective-permute-start.7 = (bf16[3,16,2,16,512]{4,3,2,1,0:T(8,128)(2,1)S(1)}, bf16[3,16,2,16,512]{4,3,2,1,0:T(8,128)(2,1)S(1)}, u32[]{:S(2)}, u32[]{:S(2)}) collective-permute-start(bf16[3,16,2,16,512]{4,3,2,1,0:T(8,128)(2,1)S(1)} %pad_maximum_fusion.1), channel_id=1, source_target_pairs={{1,0},{0,1},{3,2},{2,3},{5,4},{4,5},{7,6},{6,7},{9,8},{8,9},{11,10... | collective-permute-start | bytes 4718600 | tf_op jit(solution)/shard_map/ppermute | solution.py:289
  93.4 17.6 %collective-permute-start.6 = (bf16[16,2,16,512]{3,2,1,0:T(8,128)(2,1)S(1)}, bf16[16,2,16,512]{3,2,1,0:T(8,128)(2,1)S(1)}, u32[]{:S(2)}, u32[]{:S(2)}) collective-permute-start(bf16[16,2,16,512]{3,2,1,0:T(8,128)(2,1)S(1)} %collective-permute-done.3.across_ref), channel_id=1, source_target_pairs={{0,32},{32,0},{64,96},{96,64},{1,33},{33,1},{65,97},{97,65},{2,34}... | collective-permute-start | bytes 1572872 | tf_op jit(solution)/shard_map/ppermute | solution.py:293
  111.1 4.2 %collective-permute-start.8 = (bf16[16,2,16,512]{3,2,1,0:T(8,128)(2,1)S(1)}, bf16[16,2,16,512]{3,2,1,0:T(8,128)(2,1)S(1)}, u32[]{:S(2)}, u32[]{:S(2)}) collective-permute-start(bf16[16,2,16,512]{3,2,1,0:T(8,128)(2,1)S(1)} %collective-permute-done.6.opposite_ref), channel_id=1, source_target_pairs={{1,0},{0,1},{3,2},{2,3},{5,4},{4,5},{7,6},{6,7},{9,8},{8,9},{11,10... | collective-permute-start | bytes 1572872 | tf_op jit(solution)/shard_map/ppermute | solution.py:289

commit v5 on v4

--- a/solution.py
+++ b/solution.py
@@ -93,7 +93,8 @@
         qp = q[:, cols]
         both = jnp.concatenate([jnp.where(low, qp, zero), jnp.where(low, zero, qp)], axis=0)
         s = dot(both, k[:, cols], 1, 1)
-        s = s + jnp.concatenate([bias, bias], axis=0)
+        if bias is not None:
+            s = s + jnp.concatenate([bias, bias], axis=0)
         e = jnp.exp(s - jnp.max(s, axis=-1, keepdims=True)).astype(bf16)
         o = dot(e, jnp.concatenate([v[:, cols], ones], axis=1))
         o = o[:, :128] / o[:, 128:]
@@ -120,8 +121,8 @@
 
 
 def block_kernel(tokens_ref, above_ref, below_ref, outer_ref, gain_ref, own_qkv_ref, own_rest_ref, sibling_ref,
-                 perm_ref, back_ref, mask_ref, merge_gain_ref, sel_ref, fine_ref, merged_ref,
-                 mid_ref, inner_ref, weights, all_ref, q_ref, k_ref, v_ref, att_ref, sems):
+                 perm_ref, back_ref, mask_ref, merge_gain_ref, sel_ref, result_ref, merged_ref,
+                 fine_ref, mid_ref, inner_ref, weights, sems):
     core = lax.axis_index("c")
     lat = lax.axis_index(LAT)
     last = lax.axis_size(LAT) - 1
@@ -142,56 +143,67 @@
         copy.wait()
     gain = gain_ref[...]
 
-    def prepare(band, _):
-        raw = mid_ref[:, pl.ds(band * WL, WL)].reshape(288, 512)
+    low = lax.broadcasted_iota(jnp.int32, (1, 128), 1) < 64
+    def prepare(band):
+        raw = mid_ref[:, band * WL:band * WL + WL].reshape(288, 512)
         centre = norm(raw.astype(f32), gain).astype(bf16)
         sets = [dot(perm_ref[...], centre[n * 96:n * 96 + 96]) for n in range(3)]
         outer = norm(outer_ref[band].astype(f32), gain)
-        inner = inner_ref.reshape(32, 16, 512)[pl.ds(band * 5, 5)].reshape(80, 512)
+        inner = inner_ref.reshape(32, 16, 512)[band * 5:band * 5 + 5].reshape(80, 512)
         inner = norm(inner.astype(f32)[:72], gain)
         left = jnp.where(core == 0, outer, inner)
         right = jnp.where(core == 0, inner, outer)
         centre = [part[a:b] for a, b in ((0, 24), (24, 72), (72, 96)) for part in sets]
         rows = jnp.concatenate([left] + centre + [right], axis=0).astype(bf16)
-        all_ref[pl.ds(pl.multiple_of(band * 432, 16), 432)] = rows
-        return 0
-
-    lax.fori_loop(0, bands, prepare, 0)
-    for copy in copies[4:]:
-        copy.wait()
-
-    def product(n):
-        return dot(all_ref[...], weights[n].reshape(512, 512)).astype(bf16)
-
-    q_ref[...] = product(0) * jnp.asarray(0.125, bf16)
-    k_ref[...] = product(1)
-    v_ref[...] = product(2)
-    low = lax.broadcasted_iota(jnp.int32, (1, 128), 1) < 64
-
-    def attention(band, _):
-        rows = pl.ds(pl.multiple_of(band * 432, 16), 432)
-        q = q_ref[rows].astype(f32)[72:360].astype(bf16)
-        k, v = k_ref[rows], v_ref[rows]
-        edge = ((lat == 0) & (band == 0)) | ((lat == last) & (band == bands - 1))
-        mask = mask_ref[...] * jnp.where(edge, 1.0, 0.0).astype(f32)
+        return rows, jnp.concatenate(centre, axis=0).astype(bf16)
+
+    def attention(band, q, k, v):
+        mask = [None] * 3
         spans = ((0, 72, 0), (72, 216, 144), (216, 288, 288))
-        att = [attend(q[a:b], k[c:c + 144], v[c:c + 144], mask[a:b], low) for a, b, c in spans]
+        if band in (0, bands - 1):
+            edge = (lat == 0) if band == 0 else (lat == last)
+            bias = mask_ref[...] * jnp.where(edge, 1.0, 0.0).astype(f32)
+            mask = [bias[a:b] for a, b, c in spans]
+        att = [attend(q[a:b], k[c:c + 144], v[c:c + 144], m, low) for (a, b, c), m in zip(spans, mask)]
+        parts = []
         for n in range(3):
             part = [att[0][24 * n:24 * n + 24], att[1][48 * n:48 * n + 48], att[2][24 * n:24 * n + 24]]
-            part = dot(back_ref[...], jnp.concatenate(part, axis=0).astype(bf16)).astype(bf16)
-            att_ref[pl.ds(pl.multiple_of(band * 288 + n * 96, 16), 96)] = part
-        return 0
-
-    lax.fori_loop(0, bands, attention, 0)
-    for band in range(bands):
-        raw = mid_ref[:, band * WL:band * WL + WL].reshape(288, 512)
-        out = dot(att_ref[band * 288:band * 288 + 288], weights[3].reshape(512, 512)) + raw.astype(f32)
+            parts.append(dot(back_ref[...], jnp.concatenate(part, axis=0).astype(bf16)))
+        return jnp.concatenate(parts, axis=0).astype(bf16)
+
+    def finish(band, part, raw):
+        out = dot(part, weights[3].reshape(512, 512)) + raw.astype(f32)
         out = out.astype(bf16).reshape(2, WL, 24, 512)
         if band > 0:
             fine_ref[:, band * WL - 3:band * WL] = out[:, :3]
         if band < bands - 1:
             fine_ref[:, band * WL:band * WL + 3] = out[:, 3:]
+        rows = pl.ds(max(band * WL - 3, 0), 3 if band in (0, bands - 1) else WL)
+        copy = pltpu.make_async_copy(fine_ref.at[:, rows], result_ref.at[:, rows], sems.at[12 + band])
+        copy.start()
+        return copy
+
+    scale = jnp.asarray(0.125, bf16)
+
+    def project(band):
+        rows, centre = prepare(band)
+        q = dot(centre, weights[0].reshape(512, 512)).astype(bf16) * scale
+        k = dot(rows, weights[1].reshape(512, 512)).astype(bf16)
+        v = dot(rows, weights[2].reshape(512, 512)).astype(bf16)
+        return q, k, v
+
+    for copy in copies[4:]:
+        copy.wait()
+    copies = []
+    held = project(0)
+    for band in range(bands):
+        following = project(band + 1) if band < bands - 1 else None
+        raw = mid_ref[:, band * WL:band * WL + WL].reshape(288, 512)
+        copies.append(finish(band, attention(band, *held), raw))
+        held = following
     merge_norm(fine_ref, merge_gain_ref, sel_ref, merged_ref)
+    for copy in copies:
+        copy.wait()
 
 
 def merge_kernel(merged_ref, own_ref, pair_ref, across_ref, opposite_ref, sibling_ref, sibling_opposite_ref, coarse_ref,
@@ -210,12 +222,12 @@
         (sibling_opposite_ref, 1 - core, 3 - pair),
     ]
     copies = [pltpu.make_async_copy(ref.at[:, col], weights.at[col, :, at, there], sems.at[2 * n + col])
-              for n, (ref, at, there) in enumerate(pieces) for col in range(2)]
+              for col in range(2) for n, (ref, at, there) in enumerate(pieces)]
     for copy in copies:
         copy.start()
-    for copy in copies:
-        copy.wait()
     for col in range(2):
+        for copy in copies[8 * col:8 * col + 8]:
+            copy.wait()
         part = dot(merged_ref[...], weights[col].reshape(2048, 512)).astype(bf16)
         coarse_ref[:, :, col * 512:col * 512 + 512] = part.reshape(144, 2, 512)
 
@@ -249,18 +261,14 @@
     return pl.pallas_call(
         block_kernel,
         in_specs=[ANY, ANY, ANY, VMEM, VMEM, ANY, ANY, ANY] + [VMEM] * 5,
-        out_specs=(VMEM, VMEM),
+        out_specs=(ANY, VMEM),
         out_shape=(jax.ShapeDtypeStruct((2, 24, 24, 512), bf16), jax.ShapeDtypeStruct((288, 2048), bf16)),
         scratch_shapes=[
+            pltpu.VMEM((2, 24, 24, 512), bf16),
             pltpu.VMEM((2, 30, 24, 512), bf16),
             pltpu.VMEM((16, 2, 16, 512), bf16),
             pltpu.VMEM((4, 16, 2, 16, 512), bf16),
-            pltpu.VMEM((2160, 512), bf16),
-            pltpu.VMEM((2160, 512), bf16),
-            pltpu.VMEM((2160, 512), bf16),
-            pltpu.VMEM((2160, 512), bf16),
-            pltpu.VMEM((1440, 512), bf16),
-            pltpu.SemaphoreType.DMA((12,)),
+            pltpu.SemaphoreType.DMA((17,)),
         ],
         compiler_params=pltpu.CompilerParams(vmem_limit_bytes=40 << 20),
         cost_estimate=pl.CostEstimate(flops=5_500_000_000, bytes_accessed=8 << 20, transcendentals=2_500_000),
@@ -316,7 +324,8 @@
     pair = swap(merge_own, "x", first)
     across = swap(merge_own, "x", second)
     qkv = lax.all_gather(packed[:, :3], "y").reshape(16, 3, 16, 512)
-    pair, across, qkv, outer = together(pair, across, qkv, outer)
+    pair, across, qkv = together(pair, across, qkv)
+    across, outer = together(across, outer)
     opposite = swap(across, "x", first)
     sibling = shift(jnp.concatenate([qkv, rest[:, :1], inner.reshape(16, 2, 16, 512)], axis=1), "c", 1)
     sibling_merge = shift(jnp.stack([merge_own, pair, across]), "c", 1)

time: 118 us -> 114 us (0.966)
  Pallas kernels: 20.7 us -> 17.2 us
    pallas_call x1, Pallas kernels: 15.3 us -> 11.7 us  [attention_block(): pl.pallas_call(block_kernel, in_specs=[ANY, ANY, ANY, VMEM, VMEM, ANY, AN...]
    ppermute x1, waiting for transfers between devices: 3.45 us -> 1.12 us  [between_chips(): lax.ppermute(block, LON, [(i, (i + (1 if i % 2 else -1)) % len(devices))...]
    ppermute x3, waiting for transfers between devices: 0.01 us -> 1.25 us  [swap(): return lax.ppermute(block, axis, list(enumerate(partner)))]
  transfers between devices with their start and end apart: 9 -> 9, of which waited for: 2 -> 3; matrix products, arithmetic and copies ran while one was open for 0% -> 0% of each run, Pallas kernels for 13% -> 11%
where the time goes in v5:
time: 114 us
  blocking collectives  53.9 us (47%)
  starting transfers between devices  37.5 us (33%)
  Pallas kernels  17.2 us (15%)
  waiting for transfers between devices  3.89 us (3%)
    all_gather x1, blocking collectives, on_device(): packed = lax.all_gather(packed, 'zh')  28.4 us
    ppermute x5, starting transfers between devices, shift(): return lax.ppermute(block, axes, route)  22.8 us
    all_gather x1, blocking collectives, on_device(): qkv = lax.all_gather(packed[:, :3], 'y').reshape(16, 3, 16, 512)  12.8 us
    all_gather x1, blocking collectives, on_device(): rest = lax.all_gather(packed[:, 3:], 'y').reshape(16, 3, 16, 512)  12.7 us
    pallas_call x1, Pallas kernels, attention_block(): pl.pallas_call(block_kernel, in_specs=[ANY, ANY, ANY, VMEM, VMEM, ANY, AN...  11.7 us
    ppermute x1, starting transfers between devices, between_chips(): lax.ppermute(block, LON, [(i, (i + (1 if i % 2 else -1)) % len(devices))...  8.5 us
    ppermute x3, starting transfers between devices, swap(): return lax.ppermute(block, axis, list(enumerate(partner)))  6.26 us
    pallas_call x1, Pallas kernels, merge_block(): pl.pallas_call(merge_kernel, in_specs=[VMEM] + [ANY] * 6, out_specs=VMEM,...  2.88 us
  transfers between devices with their start and end apart: 9, of which 3 were waited for; matrix products, arithmetic and copies ran while one was open for 0% of the time, Pallas kernels for 11%

profile of v5, /device:TPU:1, one launch (start us, length us, event | category | flops | bytes accessed | tf_op | source)
XLA Modules:
  0.0 114.0 jit_solution(18443500203007614958)
XLA Ops:
  0.6 2.1 %pack_parts.1 = (bf16[6,16,512]{2,1,0:T(8,128)(2,1)}, bf16[2,3,24,512]{3,2,1,0:T(8,128)(2,1)}, bf16[2,3,24,512]{3,2,1,0:T(8,128)(2,1)}) custom-call(bf16[2,24,24,512]{3,2,1,0:T(8,128)(2,1)} %tokens_ref.5, bf16[16,1536]{1,0:T(8,128)(2,1)} %qkv_ref.1, bf16[16,512]{1,0:T(8,128)(2,1)} %proj_ref.1, bf16[64,1024]{1,0:T(8,128)(2,1)} %merge_ref.1), custom_call_target="tpu_custom_call" | custom-call | tf_op jit(solution)/shard_map/pack_parts/pallas_call | solution.py:237
  2.7 3.9 %collective-permute-start = (bf16[2,3,24,512]{3,2,1,0:T(8,128)(2,1)}, bf16[2,3,24,512]{3,2,1,0:T(8,128)(2,1)S(1)}, u32[]{:S(2)}, u32[]{:S(2)}) collective-permute-start(bf16[2,3,24,512]{3,2,1,0:T(8,128)(2,1)} %get-tuple-element.21), channel_id=1, source_target_pairs={{480,0},{0,32},{32,64},{64,96},{96,128},{128,160},{160,192},{192,2... | collective-permute-start | bytes 442376 | tf_op jit(solution)/shard_map/ppermute | solution.py:297
  6.6 7.2 %collective-permute-start.1 = (bf16[2,3,24,512]{3,2,1,0:T(8,128)(2,1)}, bf16[2,3,24,512]{3,2,1,0:T(8,128)(2,1)S(1)}, u32[]{:S(2)}, u32[]{:S(2)}) collective-permute-start(bf16[2,3,24,512]{3,2,1,0:T(8,128)(2,1)} %get-tuple-element.22), channel_id=1, source_target_pairs={{32,0},{64,32},{96,64},{128,96},{160,128},{192,160},{224,192},{256... | collective-permute-start | bytes 442376 | tf_op jit(solution)/shard_map/ppermute | solution.py:297
  13.9 28.4 %all-gather = bf16[24,16,512]{2,1,0:T(8,128)(2,1)S(1)} all-gather(bf16[6,16,512]{2,1,0:T(8,128)(2,1)} %get-tuple-element.20), channel_id=2, replica_groups=mesh['zl'=4,'x'=4,'y'=4,'zh'=4,'c'=2] {'zh'}, dimensions={0}, use_global_device_ids=true | all-gather | bytes 491520 | tf_op jit(solution)/shard_map/all_gather | solution.py:317
  42.4 12.7 %all-gather.1.own_rest_ref.own_ref = bf16[16,3,16,512]{3,2,1,0:T(8,128)(2,1)S(1)} all-gather(bf16[4,3,16,512]{3,2,1,0:T(8,128)(2,1)S(1)} %get-tuple-element.41), channel_id=3, replica_groups=mesh['zl'=4,'x'=4,'y'=4,'zh'=4,'c'=2] {'y'}, dimensions={0}, use_global_device_ids=true | all-gather | bytes 983040 | tf_op jit(solution)/shard_map/all_gather | solution.py:321
  55.0 0.1 slice_bitcast_fusion
  55.1 1.9 %collective-permute-start.2 = (bf16[16,2,16,512]{3,2,1,0:T(8,128)(2,1)S(1)}, bf16[16,2,16,512]{3,2,1,0:T(8,128)(2,1)S(1)}, u32[]{:S(2)}, u32[]{:S(2)}) collective-permute-start(bf16[16,2,16,512]{3,2,1,0:T(8,128)(2,1)S(1)} %get-tuple-element.39), channel_id=1, source_target_pairs={{0,32},{32,0},{64,96},{96,64},{1,33},{33,1},{65,97},{97,65},{2,34}... | collective-permute-start | bytes 1572872 | tf_op jit(solution)/shard_map/ppermute | solution.py:301
  57.0 1.9 %collective-permute-start.3 = (bf16[16,2,16,512]{3,2,1,0:T(8,128)(2,1)S(1)}, bf16[16,2,16,512]{3,2,1,0:T(8,128)(2,1)S(1)}, u32[]{:S(2)}, u32[]{:S(2)}) collective-permute-start(bf16[16,2,16,512]{3,2,1,0:T(8,128)(2,1)S(1)} %get-tuple-element.39), channel_id=1, source_target_pairs={{0,96},{32,64},{64,32},{96,0},{1,97},{33,65},{65,33},{97,1},{2,98}... | collective-permute-start | bytes 1572872 | tf_op jit(solution)/shard_map/ppermute | solution.py:301
  59.0 0.5 edge_rows.1
  59.6 8.5 %collective-permute-start.4 = (bf16[5,72,512]{2,1,0:T(8,128)(2,1)S(1)}, bf16[5,72,512]{2,1,0:T(8,128)(2,1)S(1)}, u32[]{:S(2)}, u32[]{:S(2)}) collective-permute-start(bf16[5,72,512]{2,1,0:T(8,128)(2,1)S(1)} %get-tuple-element.27), channel_id=1, source_target_pairs={{0,31},{1,2},{2,1},{3,4},{4,3},{5,6},{6,5},{7,8},{8,7},{9,10},{10,... | collective-permute-start | bytes 1105928 | tf_op jit(solution)/shard_map/ppermute | solution.py:306
  68.1 12.8 %all-gather.2.own_qkv_ref = bf16[16,3,16,512]{3,2,1,0:T(8,128)(2,1)S(1)} all-gather(bf16[4,3,16,512]{3,2,1,0:T(8,128)(2,1)S(1)} %get-tuple-element.40), channel_id=4, replica_groups=mesh['zl'=4,'x'=4,'y'=4,'zh'=4,'c'=2] {'y'}, dimensions={0}, use_global_device_ids=true | all-gather | bytes 983040 | tf_op jit(solution)/shard_map/all_gather | solution.py:326
  80.9 0.2 pad_maximum_fusion
  81.1 2.2 %collective-permute-start.5 = (bf16[16,6,16,512]{3,2,1,0:T(8,128)(2,1)S(1)}, bf16[16,6,16,512]{3,2,1,0:T(8,128)(2,1)S(1)}, u32[]{:S(2)}, u32[]{:S(2)}) collective-permute-start(bf16[16,6,16,512]{3,2,1,0:T(8,128)(2,1)S(1)} %pad_maximum_fusion), channel_id=1, source_target_pairs={{1,0},{0,1},{3,2},{2,3},{5,4},{4,5},{7,6},{6,7},{9,8},{8,9},{11,10... | collective-permute-start | bytes 4718600 | tf_op jit(solution)/shard_map/ppermute | solution.py:297
  83.2 1.1 collective-permute-done.4.outer_ref
  84.4 0.0 copy-start.5
  84.4 0.0 copy-start.6
  84.4 0.2 pad_maximum_fusion.1
  84.6 6.7 %collective-permute-start.7 = (bf16[3,16,2,16,512]{4,3,2,1,0:T(8,128)(2,1)S(1)}, bf16[3,16,2,16,512]{4,3,2,1,0:T(8,128)(2,1)S(1)}, u32[]{:S(2)}, u32[]{:S(2)}) collective-permute-start(bf16[3,16,2,16,512]{4,3,2,1,0:T(8,128)(2,1)S(1)} %pad_maximum_fusion.1), channel_id=1, source_target_pairs={{1,0},{0,1},{3,2},{2,3},{5,4},{4,5},{7,6},{6,7},{9,8},{8,9},{11,10... | collective-permute-start | bytes 4718600 | tf_op jit(solution)/shard_map/ppermute | solution.py:297
  91.3 2.4 %collective-permute-start.6 = (bf16[16,2,16,512]{3,2,1,0:T(8,128)(2,1)S(1)}, bf16[16,2,16,512]{3,2,1,0:T(8,128)(2,1)S(1)}, u32[]{:S(2)}, u32[]{:S(2)}) collective-permute-start(bf16[16,2,16,512]{3,2,1,0:T(8,128)(2,1)S(1)} %collective-permute-done.3.across_ref), channel_id=1, source_target_pairs={{0,32},{32,0},{64,96},{96,64},{1,33},{33,1},{65,97},{97,65},{2,34}... | collective-permute-start | bytes 1572872 | tf_op jit(solution)/shard_map/ppermute | solution.py:301
  93.8 11.7 %attention_block.1 = (bf16[2,24,24,512]{3,2,1,0:T(8,128)(2,1)}, bf16[288,2048]{1,0:T(8,128)(2,1)S(1)}) custom-call(bf16[2,24,24,512]{3,2,1,0:T(8,128)(2,1)S(1)} %copy-done, bf16[2,3,24,512]{3,2,1,0:T(8,128)(2,1)S(1)} %collective-permute-done.above_ref, bf16[2,3,24,512]{3,2,1,0:T(8,128)(2,1)S(1)} %collective-permute-done.1.below_ref, ...), custom_call_target="tpu_custom_call" | custom-call | flops 5500000256 | bytes 8388608 | tf_op jit(solution)/shard_map/attention_block/pallas_call | solution.py:261
  105.5 1.2 %collective-permute-done.6.opposite_ref = bf16[16,2,16,512]{3,2,1,0:T(8,128)(2,1)S(1)} collective-permute-done((bf16[16,2,16,512]{3,2,1,0:T(8,128)(2,1)S(1)}, bf16[16,2,16,512]{3,2,1,0:T(8,128)(2,1)S(1)}, u32[]{:S(2)}, u32[]{:S(2)}) %collective-permute-start.6) | collective-permute-done | bytes 524320 | tf_op jit(solution)/shard_map/ppermute | solution.py:301
  106.7 2.7 %collective-permute-start.8 = (bf16[16,2,16,512]{3,2,1,0:T(8,128)(2,1)S(1)}, bf16[16,2,16,512]{3,2,1,0:T(8,128)(2,1)S(1)}, u32[]{:S(2)}, u32[]{:S(2)}) collective-permute-start(bf16[16,2,16,512]{3,2,1,0:T(8,128)(2,1)S(1)} %collective-permute-done.6.opposite_ref), channel_id=1, source_target_pairs={{1,0},{0,1},{3,2},{2,3},{5,4},{4,5},{7,6},{6,7},{9,8},{8,9},{11,10... | collective-permute-start | bytes 1572872 | tf_op jit(solution)/shard_map/ppermute | solution.py:297
  109.4 1.5 %collective-permute-done.8.sibling_opposite_ref = bf16[16,2,16,512]{3,2,1,0:T(8,128)(2,1)S(1)} collective-permute-done((bf16[16,2,16,512]{3,2,1,0:T(8,128)(2,1)S(1)}, bf16[16,2,16,512]{3,2,1,0:T(8,128)(2,1)S(1)}, u32[]{:S(2)}, u32[]{:S(2)}) %collective-permute-start.8) | collective-permute-done | bytes 524320 | tf_op jit(solution)/shard_map/ppermute | solution.py:297
  111.0 2.9 %merge_block.1 = bf16[144,2,1024]{2,1,0:T(2,128)(2,1)} custom-call(bf16[288,2048]{1,0:T(8,128)(2,1)S(1)} %get-tuple-element.35.merged_ref, bf16[16,3,16,512]{3,2,1,0:T(8,128)(2,1)S(1)} %all-gather.1.own_rest_ref.own_ref, bf16[16,2,16,512]{3,2,1,0:T(8,128)(2,1)S(1)} %collective-permute-done.2.pair_ref, ...), custom_call_target="tpu_custom_call" | custom-call | flops 1200000000 | bytes 8388608 | tf_op jit(solution)/shard_map/merge_block/pallas_call | solution.py:282
  (20 shorter events, 0.1 us)
Async XLA Ops:
  2.7 39.6 %collective-permute-start = (bf16[2,3,24,512]{3,2,1,0:T(8,128)(2,1)}, bf16[2,3,24,512]{3,2,1,0:T(8,128)(2,1)S(1)}, u32[]{:S(2)}, u32[]{:S(2)}) collective-permute-start(bf16[2,3,24,512]{3,2,1,0:T(8,128)(2,1)} %get-tuple-element.21), channel_id=1, source_target_pairs={{480,0},{0,32},{32,64},{64,96},{96,128},{128,160},{160,192},{192,2... | collective-permute-start | bytes 442376 | tf_op jit(solution)/shard_map/ppermute | solution.py:297
  6.6 35.7 %collective-permute-start.1 = (bf16[2,3,24,512]{3,2,1,0:T(8,128)(2,1)}, bf16[2,3,24,512]{3,2,1,0:T(8,128)(2,1)S(1)}, u32[]{:S(2)}, u32[]{:S(2)}) collective-permute-start(bf16[2,3,24,512]{3,2,1,0:T(8,128)(2,1)} %get-tuple-element.22), channel_id=1, source_target_pairs={{32,0},{64,32},{96,64},{128,96},{160,128},{192,160},{224,192},{256... | collective-permute-start | bytes 442376 | tf_op jit(solution)/shard_map/ppermute | solution.py:297
  42.4 16.6 %copy-start = (bf16[2,24,24,512]{3,2,1,0:T(8,128)(2,1)S(1)}, bf16[2,24,24,512]{3,2,1,0:T(8,128)(2,1)}, u32[]{:S(2)}) copy-start(bf16[2,24,24,512]{3,2,1,0:T(8,128)(2,1)} %tokens_ref.5) | copy-start | bytes 3538948
  55.1 25.8 %collective-permute-start.2 = (bf16[16,2,16,512]{3,2,1,0:T(8,128)(2,1)S(1)}, bf16[16,2,16,512]{3,2,1,0:T(8,128)(2,1)S(1)}, u32[]{:S(2)}, u32[]{:S(2)}) collective-permute-start(bf16[16,2,16,512]{3,2,1,0:T(8,128)(2,1)S(1)} %get-tuple-element.39), channel_id=1, source_target_pairs={{0,32},{32,0},{64,96},{96,64},{1,33},{33,1},{65,97},{97,65},{2,34}... | collective-permute-start | bytes 1572872 | tf_op jit(solution)/shard_map/ppermute | solution.py:301
  57.0 23.8 %collective-permute-start.3 = (bf16[16,2,16,512]{3,2,1,0:T(8,128)(2,1)S(1)}, bf16[16,2,16,512]{3,2,1,0:T(8,128)(2,1)S(1)}, u32[]{:S(2)}, u32[]{:S(2)}) collective-permute-start(bf16[16,2,16,512]{3,2,1,0:T(8,128)(2,1)S(1)} %get-tuple-element.39), channel_id=1, source_target_pairs={{0,96},{32,64},{64,32},{96,0},{1,97},{33,65},{65,33},{97,1},{2,98}... | collective-permute-start | bytes 1572872 | tf_op jit(solution)/shard_map/ppermute | solution.py:301
  59.6 24.8 %collective-permute-start.4 = (bf16[5,72,512]{2,1,0:T(8,128)(2,1)S(1)}, bf16[5,72,512]{2,1,0:T(8,128)(2,1)S(1)}, u32[]{:S(2)}, u32[]{:S(2)}) collective-permute-start(bf16[5,72,512]{2,1,0:T(8,128)(2,1)S(1)} %get-tuple-element.27), channel_id=1, source_target_pairs={{0,31},{1,2},{2,1},{3,4},{4,3},{5,6},{6,5},{7,8},{8,7},{9,10},{10,... | collective-permute-start | bytes 1105928 | tf_op jit(solution)/shard_map/ppermute | solution.py:306
  81.1 12.7 %collective-permute-start.5 = (bf16[16,6,16,512]{3,2,1,0:T(8,128)(2,1)S(1)}, bf16[16,6,16,512]{3,2,1,0:T(8,128)(2,1)S(1)}, u32[]{:S(2)}, u32[]{:S(2)}) collective-permute-start(bf16[16,6,16,512]{3,2,1,0:T(8,128)(2,1)S(1)} %pad_maximum_fusion), channel_id=1, source_target_pairs={{1,0},{0,1},{3,2},{2,3},{5,4},{4,5},{7,6},{6,7},{9,8},{8,9},{11,10... | collective-permute-start | bytes 4718600 | tf_op jit(solution)/shard_map/ppermute | solution.py:297
  84.3 9.4 %copy-start.1 = (f32[2048]{0:T(1024)S(1)}, f32[2048]{0:T(1024)}, u32[]{:S(2)}) copy-start(f32[2048]{0:T(1024)} %param.14) | copy-start | bytes 24580
  84.3 9.4 %copy-start.2 = (f32[512]{0:T(512)S(1)}, f32[512]{0:T(512)}, u32[]{:S(2)}) copy-start(f32[512]{0:T(512)} %param.11) | copy-start | bytes 6148
  84.4 9.4 %copy-start.3 = (f32[288,144]{1,0:T(8,128)S(1)}, f32[288,144]{1,0:T(8,128)}, u32[]{:S(2)}) copy-start(f32[288,144]{1,0:T(8,128)} %constant.10.clone.mask_ref) | copy-start | bytes 497668
  84.4 9.4 %copy-start.4 = (bf16[192,192]{1,0:T(8,128)(2,1)S(1)}, bf16[192,192]{1,0:T(8,128)(2,1)}, u32[]{:S(2)}) copy-start(bf16[192,192]{1,0:T(8,128)(2,1)} %constant.11.clone.sel_ref) | copy-start | bytes 221188
  84.4 9.4 %copy-start.5 = (bf16[96,96]{1,0:T(8,128)(2,1)S(1)}, bf16[96,96]{1,0:T(8,128)(2,1)}, u32[]{:S(2)}) copy-start(bf16[96,96]{1,0:T(8,128)(2,1)} %constant.8.clone.perm_ref) | copy-start | bytes 55300
  84.4 9.4 %copy-start.6 = (bf16[96,96]{1,0:T(8,128)(2,1)S(1)}, bf16[96,96]{1,0:T(8,128)(2,1)}, u32[]{:S(2)}) copy-start(bf16[96,96]{1,0:T(8,128)(2,1)} %constant.9.clone.back_ref) | copy-start | bytes 55300
  84.6 22.2 %collective-permute-start.7 = (bf16[3,16,2,16,512]{4,3,2,1,0:T(8,128)(2,1)S(1)}, bf16[3,16,2,16,512]{4,3,2,1,0:T(8,128)(2,1)S(1)}, u32[]{:S(2)}, u32[]{:S(2)}) collective-permute-start(bf16[3,16,2,16,512]{4,3,2,1,0:T(8,128)(2,1)S(1)} %pad_maximum_fusion.1), channel_id=1, source_target_pairs={{1,0},{0,1},{3,2},{2,3},{5,4},{4,5},{7,6},{6,7},{9,8},{8,9},{11,10... | collective-permute-start | bytes 4718600 | tf_op jit(solution)/shard_map/ppermute | solution.py:297
  91.3 15.4 %collective-permute-start.6 = (bf16[16,2,16,512]{3,2,1,0:T(8,128)(2,1)S(1)}, bf16[16,2,16,512]{3,2,1,0:T(8,128)(2,1)S(1)}, u32[]{:S(2)}, u32[]{:S(2)}) collective-permute-start(bf16[16,2,16,512]{3,2,1,0:T(8,128)(2,1)S(1)} %collective-permute-done.3.across_ref), channel_id=1, source_target_pairs={{0,32},{32,0},{64,96},{96,64},{1,33},{33,1},{65,97},{97,65},{2,34}... | collective-permute-start | bytes 1572872 | tf_op jit(solution)/shard_map/ppermute | solution.py:301
  106.7 4.2 %collective-permute-start.8 = (bf16[16,2,16,512]{3,2,1,0:T(8,128)(2,1)S(1)}, bf16[16,2,16,512]{3,2,1,0:T(8,128)(2,1)S(1)}, u32[]{:S(2)}, u32[]{:S(2)}) collective-permute-start(bf16[16,2,16,512]{3,2,1,0:T(8,128)(2,1)S(1)} %collective-permute-done.6.opposite_ref), channel_id=1, source_target_pairs={{1,0},{0,1},{3,2},{2,3},{5,4},{4,5},{7,6},{6,7},{9,8},{8,9},{11,10... | collective-permute-start | bytes 1572872 | tf_op jit(solution)/shard_map/ppermute | solution.py:297

commit v6 on v5

--- a/solution.py
+++ b/solution.py
@@ -53,15 +53,16 @@
     return centred * lax.rsqrt(spread + eps) * gain
 
 
-def pack_kernel(tokens_ref, qkv_ref, proj_ref, merge_ref, out_ref, top_ref, bottom_ref):
-    top_ref[...] = tokens_ref[:, 0:3]
-    bottom_ref[...] = tokens_ref[:, 21:24]
-    for n in range(3):
-        out_ref[n] = qkv_ref[:, n * 512:n * 512 + 512]
-    out_ref[3] = proj_ref[...]
-    quarter = merge_ref[pl.ds(pl.multiple_of(lax.axis_index("x") * 16, 16), 16), :]
-    out_ref[4] = quarter[:, :512]
-    out_ref[5] = quarter[:, 512:]
+def pack_kernel(tokens_ref, qkv_ref, proj_ref, merge_ref, out_ref, top_ref, bottom_ref, sems):
+    rows = pl.ds(pl.multiple_of(lax.axis_index("x") * 16, 16), 16)
+    pairs = [(tokens_ref.at[:, 0:3], top_ref), (tokens_ref.at[:, 21:24], bottom_ref), (proj_ref, out_ref.at[3])]
+    pairs += [(qkv_ref.at[:, n * 512:n * 512 + 512], out_ref.at[n]) for n in range(3)]
+    pairs += [(merge_ref.at[rows, n * 512:n * 512 + 512], out_ref.at[4 + n]) for n in range(2)]
+    copies = [pltpu.make_async_copy(source, target, sems.at[n]) for n, (source, target) in enumerate(pairs)]
+    for copy in copies:
+        copy.start()
+    for copy in copies:
+        copy.wait()
 
 
 def edge_kernel(tokens_ref, above_ref, below_ref, outer_ref, inner_ref):
@@ -236,9 +237,10 @@
     rows = jax.ShapeDtypeStruct((2, 3, 24, 512), bf16)
     return pl.pallas_call(
         pack_kernel,
-        in_specs=[VMEM] * 4,
+        in_specs=[ANY] * 4,
         out_specs=(VMEM,) * 3,
         out_shape=(jax.ShapeDtypeStruct((6, 16, 512), bf16), rows, rows),
+        scratch_shapes=[pltpu.SemaphoreType.DMA((8,))],
         name="pack_parts",
     )(tokens, w_qkv, w_proj, w_merge)
 

time: 114 us -> 114 us (level)
  no operation moved by 1% of the time
where the time goes in v6:
time: 114 us
  blocking collectives  53.9 us (47%)
  starting transfers between devices  37.5 us (33%)
  Pallas kernels  16.9 us (15%)
  waiting for transfers between devices  3.9 us (3%)
    all_gather x1, blocking collectives, on_device(): packed = lax.all_gather(packed, 'zh')  28.4 us
    ppermute x5, starting transfers between devices, shift(): return lax.ppermute(block, axes, route)  22.8 us
    all_gather x1, blocking collectives, on_device(): qkv = lax.all_gather(packed[:, :3], 'y').reshape(16, 3, 16, 512)  12.8 us
    all_gather x1, blocking collectives, on_device(): rest = lax.all_gather(packed[:, 3:], 'y').reshape(16, 3, 16, 512)  12.7 us
    pallas_call x1, Pallas kernels, attention_block(): pl.pallas_call(block_kernel, in_specs=[ANY, ANY, ANY, VMEM, VMEM, ANY, AN...  11.7 us
    ppermute x1, starting transfers between devices, between_chips(): lax.ppermute(block, LON, [(i, (i + (1 if i % 2 else -1)) % len(devices))...  8.5 us
    ppermute x3, starting transfers between devices, swap(): return lax.ppermute(block, axis, list(enumerate(partner)))  6.25 us
    pallas_call x1, Pallas kernels, merge_block(): pl.pallas_call(merge_kernel, in_specs=[VMEM] + [ANY] * 6, out_specs=VMEM,...  2.88 us
  transfers between devices with their start and end apart: 9, of which 3 were waited for; matrix products, arithmetic and copies ran while one was open for 0% of the time, Pallas kernels for 11%

profile of v6, /device:TPU:1, one launch (start us, length us, event | category | flops | bytes accessed | tf_op | source)
XLA Modules:
  0.0 113.8 jit_solution(15707910624931452085)
XLA Ops:
  0.6 1.8 %pack_parts.1 = (bf16[6,16,512]{2,1,0:T(8,128)(2,1)}, bf16[2,3,24,512]{3,2,1,0:T(8,128)(2,1)}, bf16[2,3,24,512]{3,2,1,0:T(8,128)(2,1)}) custom-call(bf16[2,24,24,512]{3,2,1,0:T(8,128)(2,1)} %tokens_ref.5, bf16[16,1536]{1,0:T(8,128)(2,1)} %qkv_ref.1, bf16[16,512]{1,0:T(8,128)(2,1)} %proj_ref.1, bf16[64,1024]{1,0:T(8,128)(2,1)} %merge_ref.1), custom_call_target="tpu_custom_call" | custom-call | tf_op jit(solution)/shard_map/pack_parts/pallas_call | solution.py:238
  2.4 3.9 %collective-permute-start = (bf16[2,3,24,512]{3,2,1,0:T(8,128)(2,1)}, bf16[2,3,24,512]{3,2,1,0:T(8,128)(2,1)S(1)}, u32[]{:S(2)}, u32[]{:S(2)}) collective-permute-start(bf16[2,3,24,512]{3,2,1,0:T(8,128)(2,1)} %get-tuple-element.21), channel_id=1, source_target_pairs={{480,0},{0,32},{32,64},{64,96},{96,128},{128,160},{160,192},{192,2... | collective-permute-start | bytes 442376 | tf_op jit(solution)/shard_map/ppermute | solution.py:299
  6.4 7.2 %collective-permute-start.1 = (bf16[2,3,24,512]{3,2,1,0:T(8,128)(2,1)}, bf16[2,3,24,512]{3,2,1,0:T(8,128)(2,1)S(1)}, u32[]{:S(2)}, u32[]{:S(2)}) collective-permute-start(bf16[2,3,24,512]{3,2,1,0:T(8,128)(2,1)} %get-tuple-element.22), channel_id=1, source_target_pairs={{32,0},{64,32},{96,64},{128,96},{160,128},{192,160},{224,192},{256... | collective-permute-start | bytes 442376 | tf_op jit(solution)/shard_map/ppermute | solution.py:299
  13.7 28.4 %all-gather = bf16[24,16,512]{2,1,0:T(8,128)(2,1)S(1)} all-gather(bf16[6,16,512]{2,1,0:T(8,128)(2,1)} %get-tuple-element.20), channel_id=2, replica_groups=mesh['zl'=4,'x'=4,'y'=4,'zh'=4,'c'=2] {'zh'}, dimensions={0}, use_global_device_ids=true | all-gather | bytes 491520 | tf_op jit(solution)/shard_map/all_gather | solution.py:319
  42.1 12.7 %all-gather.1.own_rest_ref.own_ref = bf16[16,3,16,512]{3,2,1,0:T(8,128)(2,1)S(1)} all-gather(bf16[4,3,16,512]{3,2,1,0:T(8,128)(2,1)S(1)} %get-tuple-element.41), channel_id=3, replica_groups=mesh['zl'=4,'x'=4,'y'=4,'zh'=4,'c'=2] {'y'}, dimensions={0}, use_global_device_ids=true | all-gather | bytes 983040 | tf_op jit(solution)/shard_map/all_gather | solution.py:323
  54.8 0.1 slice_bitcast_fusion
  54.9 1.9 %collective-permute-start.2 = (bf16[16,2,16,512]{3,2,1,0:T(8,128)(2,1)S(1)}, bf16[16,2,16,512]{3,2,1,0:T(8,128)(2,1)S(1)}, u32[]{:S(2)}, u32[]{:S(2)}) collective-permute-start(bf16[16,2,16,512]{3,2,1,0:T(8,128)(2,1)S(1)} %get-tuple-element.39), channel_id=1, source_target_pairs={{0,32},{32,0},{64,96},{96,64},{1,33},{33,1},{65,97},{97,65},{2,34}... | collective-permute-start | bytes 1572872 | tf_op jit(solution)/shard_map/ppermute | solution.py:303
  56.8 1.9 %collective-permute-start.3 = (bf16[16,2,16,512]{3,2,1,0:T(8,128)(2,1)S(1)}, bf16[16,2,16,512]{3,2,1,0:T(8,128)(2,1)S(1)}, u32[]{:S(2)}, u32[]{:S(2)}) collective-permute-start(bf16[16,2,16,512]{3,2,1,0:T(8,128)(2,1)S(1)} %get-tuple-element.39), channel_id=1, source_target_pairs={{0,96},{32,64},{64,32},{96,0},{1,97},{33,65},{65,33},{97,1},{2,98}... | collective-permute-start | bytes 1572872 | tf_op jit(solution)/shard_map/ppermute | solution.py:303
  58.8 0.5 edge_rows.1
  59.3 8.5 %collective-permute-start.4 = (bf16[5,72,512]{2,1,0:T(8,128)(2,1)S(1)}, bf16[5,72,512]{2,1,0:T(8,128)(2,1)S(1)}, u32[]{:S(2)}, u32[]{:S(2)}) collective-permute-start(bf16[5,72,512]{2,1,0:T(8,128)(2,1)S(1)} %get-tuple-element.27), channel_id=1, source_target_pairs={{0,31},{1,2},{2,1},{3,4},{4,3},{5,6},{6,5},{7,8},{8,7},{9,10},{10,... | collective-permute-start | bytes 1105928 | tf_op jit(solution)/shard_map/ppermute | solution.py:308
  67.8 12.8 %all-gather.2.own_qkv_ref = bf16[16,3,16,512]{3,2,1,0:T(8,128)(2,1)S(1)} all-gather(bf16[4,3,16,512]{3,2,1,0:T(8,128)(2,1)S(1)} %get-tuple-element.40), channel_id=4, replica_groups=mesh['zl'=4,'x'=4,'y'=4,'zh'=4,'c'=2] {'y'}, dimensions={0}, use_global_device_ids=true | all-gather | bytes 983040 | tf_op jit(solution)/shard_map/all_gather | solution.py:328
  80.6 0.2 pad_maximum_fusion
  80.8 2.2 %collective-permute-start.5 = (bf16[16,6,16,512]{3,2,1,0:T(8,128)(2,1)S(1)}, bf16[16,6,16,512]{3,2,1,0:T(8,128)(2,1)S(1)}, u32[]{:S(2)}, u32[]{:S(2)}) collective-permute-start(bf16[16,6,16,512]{3,2,1,0:T(8,128)(2,1)S(1)} %pad_maximum_fusion), channel_id=1, source_target_pairs={{1,0},{0,1},{3,2},{2,3},{5,4},{4,5},{7,6},{6,7},{9,8},{8,9},{11,10... | collective-permute-start | bytes 4718600 | tf_op jit(solution)/shard_map/ppermute | solution.py:299
  83.0 1.1 collective-permute-done.4.outer_ref
  84.1 0.0 copy-start.5
  84.1 0.0 copy-start.6
  84.1 0.2 pad_maximum_fusion.1
  84.3 6.7 %collective-permute-start.7 = (bf16[3,16,2,16,512]{4,3,2,1,0:T(8,128)(2,1)S(1)}, bf16[3,16,2,16,512]{4,3,2,1,0:T(8,128)(2,1)S(1)}, u32[]{:S(2)}, u32[]{:S(2)}) collective-permute-start(bf16[3,16,2,16,512]{4,3,2,1,0:T(8,128)(2,1)S(1)} %pad_maximum_fusion.1), channel_id=1, source_target_pairs={{1,0},{0,1},{3,2},{2,3},{5,4},{4,5},{7,6},{6,7},{9,8},{8,9},{11,10... | collective-permute-start | bytes 4718600 | tf_op jit(solution)/shard_map/ppermute | solution.py:299
  91.1 2.4 %collective-permute-start.6 = (bf16[16,2,16,512]{3,2,1,0:T(8,128)(2,1)S(1)}, bf16[16,2,16,512]{3,2,1,0:T(8,128)(2,1)S(1)}, u32[]{:S(2)}, u32[]{:S(2)}) collective-permute-start(bf16[16,2,16,512]{3,2,1,0:T(8,128)(2,1)S(1)} %collective-permute-done.3.across_ref), channel_id=1, source_target_pairs={{0,32},{32,0},{64,96},{96,64},{1,33},{33,1},{65,97},{97,65},{2,34}... | collective-permute-start | bytes 1572872 | tf_op jit(solution)/shard_map/ppermute | solution.py:303
  93.5 11.7 %attention_block.1 = (bf16[2,24,24,512]{3,2,1,0:T(8,128)(2,1)}, bf16[288,2048]{1,0:T(8,128)(2,1)S(1)}) custom-call(bf16[2,24,24,512]{3,2,1,0:T(8,128)(2,1)S(1)} %copy-done, bf16[2,3,24,512]{3,2,1,0:T(8,128)(2,1)S(1)} %collective-permute-done.above_ref, bf16[2,3,24,512]{3,2,1,0:T(8,128)(2,1)S(1)} %collective-permute-done.1.below_ref, ...), custom_call_target="tpu_custom_call" | custom-call | flops 5500000256 | bytes 8388608 | tf_op jit(solution)/shard_map/attention_block/pallas_call | solution.py:263
  105.2 1.3 %collective-permute-done.6.opposite_ref = bf16[16,2,16,512]{3,2,1,0:T(8,128)(2,1)S(1)} collective-permute-done((bf16[16,2,16,512]{3,2,1,0:T(8,128)(2,1)S(1)}, bf16[16,2,16,512]{3,2,1,0:T(8,128)(2,1)S(1)}, u32[]{:S(2)}, u32[]{:S(2)}) %collective-permute-start.6) | collective-permute-done | bytes 524320 | tf_op jit(solution)/shard_map/ppermute | solution.py:303
  106.5 2.7 %collective-permute-start.8 = (bf16[16,2,16,512]{3,2,1,0:T(8,128)(2,1)S(1)}, bf16[16,2,16,512]{3,2,1,0:T(8,128)(2,1)S(1)}, u32[]{:S(2)}, u32[]{:S(2)}) collective-permute-start(bf16[16,2,16,512]{3,2,1,0:T(8,128)(2,1)S(1)} %collective-permute-done.6.opposite_ref), channel_id=1, source_target_pairs={{1,0},{0,1},{3,2},{2,3},{5,4},{4,5},{7,6},{6,7},{9,8},{8,9},{11,10... | collective-permute-start | bytes 1572872 | tf_op jit(solution)/shard_map/ppermute | solution.py:299
  109.2 1.5 %collective-permute-done.8.sibling_opposite_ref = bf16[16,2,16,512]{3,2,1,0:T(8,128)(2,1)S(1)} collective-permute-done((bf16[16,2,16,512]{3,2,1,0:T(8,128)(2,1)S(1)}, bf16[16,2,16,512]{3,2,1,0:T(8,128)(2,1)S(1)}, u32[]{:S(2)}, u32[]{:S(2)}) %collective-permute-start.8) | collective-permute-done | bytes 524320 | tf_op jit(solution)/shard_map/ppermute | solution.py:299
  110.7 2.9 %merge_block.1 = bf16[144,2,1024]{2,1,0:T(2,128)(2,1)} custom-call(bf16[288,2048]{1,0:T(8,128)(2,1)S(1)} %get-tuple-element.35.merged_ref, bf16[16,3,16,512]{3,2,1,0:T(8,128)(2,1)S(1)} %all-gather.1.own_rest_ref.own_ref, bf16[16,2,16,512]{3,2,1,0:T(8,128)(2,1)S(1)} %collective-permute-done.2.pair_ref, ...), custom_call_target="tpu_custom_call" | custom-call | flops 1200000000 | bytes 8388608 | tf_op jit(solution)/shard_map/merge_block/pallas_call | solution.py:284
  (20 shorter events, 0.1 us)
Async XLA Ops:
  2.4 39.6 %collective-permute-start = (bf16[2,3,24,512]{3,2,1,0:T(8,128)(2,1)}, bf16[2,3,24,512]{3,2,1,0:T(8,128)(2,1)S(1)}, u32[]{:S(2)}, u32[]{:S(2)}) collective-permute-start(bf16[2,3,24,512]{3,2,1,0:T(8,128)(2,1)} %get-tuple-element.21), channel_id=1, source_target_pairs={{480,0},{0,32},{32,64},{64,96},{96,128},{128,160},{160,192},{192,2... | collective-permute-start | bytes 442376 | tf_op jit(solution)/shard_map/ppermute | solution.py:299
  6.4 35.7 %collective-permute-start.1 = (bf16[2,3,24,512]{3,2,1,0:T(8,128)(2,1)}, bf16[2,3,24,512]{3,2,1,0:T(8,128)(2,1)S(1)}, u32[]{:S(2)}, u32[]{:S(2)}) collective-permute-start(bf16[2,3,24,512]{3,2,1,0:T(8,128)(2,1)} %get-tuple-element.22), channel_id=1, source_target_pairs={{32,0},{64,32},{96,64},{128,96},{160,128},{192,160},{224,192},{256... | collective-permute-start | bytes 442376 | tf_op jit(solution)/shard_map/ppermute | solution.py:299
  42.1 16.6 %copy-start = (bf16[2,24,24,512]{3,2,1,0:T(8,128)(2,1)S(1)}, bf16[2,24,24,512]{3,2,1,0:T(8,128)(2,1)}, u32[]{:S(2)}) copy-start(bf16[2,24,24,512]{3,2,1,0:T(8,128)(2,1)} %tokens_ref.5) | copy-start | bytes 3538948
  54.9 25.8 %collective-permute-start.2 = (bf16[16,2,16,512]{3,2,1,0:T(8,128)(2,1)S(1)}, bf16[16,2,16,512]{3,2,1,0:T(8,128)(2,1)S(1)}, u32[]{:S(2)}, u32[]{:S(2)}) collective-permute-start(bf16[16,2,16,512]{3,2,1,0:T(8,128)(2,1)S(1)} %get-tuple-element.39), channel_id=1, source_target_pairs={{0,32},{32,0},{64,96},{96,64},{1,33},{33,1},{65,97},{97,65},{2,34}... | collective-permute-start | bytes 1572872 | tf_op jit(solution)/shard_map/ppermute | solution.py:303
  56.8 23.8 %collective-permute-start.3 = (bf16[16,2,16,512]{3,2,1,0:T(8,128)(2,1)S(1)}, bf16[16,2,16,512]{3,2,1,0:T(8,128)(2,1)S(1)}, u32[]{:S(2)}, u32[]{:S(2)}) collective-permute-start(bf16[16,2,16,512]{3,2,1,0:T(8,128)(2,1)S(1)} %get-tuple-element.39), channel_id=1, source_target_pairs={{0,96},{32,64},{64,32},{96,0},{1,97},{33,65},{65,33},{97,1},{2,98}... | collective-permute-start | bytes 1572872 | tf_op jit(solution)/shard_map/ppermute | solution.py:303
  59.3 24.8 %collective-permute-start.4 = (bf16[5,72,512]{2,1,0:T(8,128)(2,1)S(1)}, bf16[5,72,512]{2,1,0:T(8,128)(2,1)S(1)}, u32[]{:S(2)}, u32[]{:S(2)}) collective-permute-start(bf16[5,72,512]{2,1,0:T(8,128)(2,1)S(1)} %get-tuple-element.27), channel_id=1, source_target_pairs={{0,31},{1,2},{2,1},{3,4},{4,3},{5,6},{6,5},{7,8},{8,7},{9,10},{10,... | collective-permute-start | bytes 1105928 | tf_op jit(solution)/shard_map/ppermute | solution.py:308
  80.8 12.7 %collective-permute-start.5 = (bf16[16,6,16,512]{3,2,1,0:T(8,128)(2,1)S(1)}, bf16[16,6,16,512]{3,2,1,0:T(8,128)(2,1)S(1)}, u32[]{:S(2)}, u32[]{:S(2)}) collective-permute-start(bf16[16,6,16,512]{3,2,1,0:T(8,128)(2,1)S(1)} %pad_maximum_fusion), channel_id=1, source_target_pairs={{1,0},{0,1},{3,2},{2,3},{5,4},{4,5},{7,6},{6,7},{9,8},{8,9},{11,10... | collective-permute-start | bytes 4718600 | tf_op jit(solution)/shard_map/ppermute | solution.py:299
  84.1 9.4 %copy-start.1 = (f32[2048]{0:T(1024)S(1)}, f32[2048]{0:T(1024)}, u32[]{:S(2)}) copy-start(f32[2048]{0:T(1024)} %param.14) | copy-start | bytes 24580
  84.1 9.4 %copy-start.2 = (f32[512]{0:T(512)S(1)}, f32[512]{0:T(512)}, u32[]{:S(2)}) copy-start(f32[512]{0:T(512)} %param.11) | copy-start | bytes 6148
  84.1 9.4 %copy-start.3 = (f32[288,144]{1,0:T(8,128)S(1)}, f32[288,144]{1,0:T(8,128)}, u32[]{:S(2)}) copy-start(f32[288,144]{1,0:T(8,128)} %constant.10.clone.mask_ref) | copy-start | bytes 497668
  84.1 9.4 %copy-start.4 = (bf16[192,192]{1,0:T(8,128)(2,1)S(1)}, bf16[192,192]{1,0:T(8,128)(2,1)}, u32[]{:S(2)}) copy-start(bf16[192,192]{1,0:T(8,128)(2,1)} %constant.11.clone.sel_ref) | copy-start | bytes 221188
  84.1 9.4 %copy-start.5 = (bf16[96,96]{1,0:T(8,128)(2,1)S(1)}, bf16[96,96]{1,0:T(8,128)(2,1)}, u32[]{:S(2)}) copy-start(bf16[96,96]{1,0:T(8,128)(2,1)} %constant.8.clone.perm_ref) | copy-start | bytes 55300
  84.1 9.4 %copy-start.6 = (bf16[96,96]{1,0:T(8,128)(2,1)S(1)}, bf16[96,96]{1,0:T(8,128)(2,1)}, u32[]{:S(2)}) copy-start(bf16[96,96]{1,0:T(8,128)(2,1)} %constant.9.clone.back_ref) | copy-start | bytes 55300
  84.3 22.2 %collective-permute-start.7 = (bf16[3,16,2,16,512]{4,3,2,1,0:T(8,128)(2,1)S(1)}, bf16[3,16,2,16,512]{4,3,2,1,0:T(8,128)(2,1)S(1)}, u32[]{:S(2)}, u32[]{:S(2)}) collective-permute-start(bf16[3,16,2,16,512]{4,3,2,1,0:T(8,128)(2,1)S(1)} %pad_maximum_fusion.1), channel_id=1, source_target_pairs={{1,0},{0,1},{3,2},{2,3},{5,4},{4,5},{7,6},{6,7},{9,8},{8,9},{11,10... | collective-permute-start | bytes 4718600 | tf_op jit(solution)/shard_map/ppermute | solution.py:299
  91.1 15.4 %collective-permute-start.6 = (bf16[16,2,16,512]{3,2,1,0:T(8,128)(2,1)S(1)}, bf16[16,2,16,512]{3,2,1,0:T(8,128)(2,1)S(1)}, u32[]{:S(2)}, u32[]{:S(2)}) collective-permute-start(bf16[16,2,16,512]{3,2,1,0:T(8,128)(2,1)S(1)} %collective-permute-done.3.across_ref), channel_id=1, source_target_pairs={{0,32},{32,0},{64,96},{96,64},{1,33},{33,1},{65,97},{97,65},{2,34}... | collective-permute-start | bytes 1572872 | tf_op jit(solution)/shard_map/ppermute | solution.py:303
  106.5 4.2 %collective-permute-start.8 = (bf16[16,2,16,512]{3,2,1,0:T(8,128)(2,1)S(1)}, bf16[16,2,16,512]{3,2,1,0:T(8,128)(2,1)S(1)}, u32[]{:S(2)}, u32[]{:S(2)}) collective-permute-start(bf16[16,2,16,512]{3,2,1,0:T(8,128)(2,1)S(1)} %collective-permute-done.6.opposite_ref), channel_id=1, source_target_pairs={{1,0},{0,1},{3,2},{2,3},{5,4},{4,5},{7,6},{6,7},{9,8},{8,9},{11,10... | collective-permute-start | bytes 1572872 | tf_op jit(solution)/shard_map/ppermute | solution.py:299
